TPU v7x, 32 devices: a whole 2x2x4 slice. The times are simulated.
32 devices in a mesh: section: 2 (over y), wide: 4 (over z), narrow: 4 (over x, core).
Axes of the slice: x: 2, y: 2, z: 4, core: 2. Of those that a mesh axis runs over, the one named last changes fastest.
Arguments:
- token_shard: int32 [1024, 1], P(('section', 'wide')), may hold values from 0 to 7; in each aligned block of 128 rows (0 to 127, 128 to 255, ...) at most 32 rows name the same one
- token_row: int32 [1024], P(('section', 'wide')), may hold values from 0 to 511
- table: bfloat16 [4096, 8192], P(('section', 'wide'), 'narrow'), may hold values from -51 to 51
- gain: float32 [8192], P('narrow'), may hold values from 0.1 to 1.9
- key_value_weight: bfloat16 [2048, 8192], P(('section', 'wide'), 'narrow'), may hold values from -0.0625 to 0.0625
- kv_target: bfloat16 [1024, 2048], P(('section', 'wide'), 'narrow'), may hold values from -6 to 6
Outputs:
- table_grad: bfloat16 [4096, 8192], P(('section', 'wide'), 'narrow')
Inputs may be any that keep to these rules, and one draw needn't show every extreme that they name: `token_shard`: among the rows of one device, no value is named by more than 32 rows.
All inputs are finite; a program needn't handle non-finite values.
Results may differ from a plain program's by a relative error of at most 0.0056.
Values may be sent and summed in bfloat16 or wider, within the bound.
No kernel may reach another device: no remote copies, remote signals or barrier semaphores. Data moves between devices by JAX's collectives and lax.ppermute only.
A program may use at most 64 MiB of HBM per device.

v0:
```python
import jax
import jax.numpy as jnp
from jax import lax
from jax.sharding import PartitionSpec as P

D = 8192


EPSILON = 1e-05


def contract_last(left, right):
    return lax.dot_general(
        left, right, (((1,), (1,)), ((), ())), preferred_element_type=jnp.float32
    )


def on_device(token_shard, token_row, table, gain, key_value_weight, kv_target):
    tokens_here = token_row.shape[0]
    owners = lax.axis_size(("section", "wide"))
    slot_count = 2 * tokens_here // owners
    width_here = table.shape[1]
    shard_of = token_shard[:, 0]
    membership = (shard_of[:, None] == jnp.arange(owners, dtype=jnp.int32)[None, :]).astype(
        jnp.int32
    )
    ranking = jnp.sum((jnp.cumsum(membership, axis=0) - 1) * membership, axis=1)
    position = shard_of * slot_count + ranking
    requests = (
        jnp.full((owners * slot_count,), -1, jnp.int32)
        .at[position]
        .set(token_row)
        .reshape(owners, slot_count)
    )
    holder = (
        jnp.full((owners * slot_count,), -1, jnp.int32)
        .at[position]
        .set(jnp.arange(tokens_here, dtype=jnp.int32))
    )
    wanted = lax.all_to_all(requests, ("section", "wide"), split_axis=0, concat_axis=0, tiled=True)
    present = wanted >= 0
    picked = jnp.take(table, jnp.where(present, wanted, 0), axis=0)
    returned = lax.all_to_all(
        jnp.where(present[..., None], picked, jnp.zeros((), table.dtype)),
        ("section", "wide"),
        split_axis=0,
        concat_axis=0,
        tiled=True,
    )
    hidden = jnp.take(returned.reshape(owners * slot_count, width_here), position, axis=0)
    rows_float = hidden.astype(jnp.float32)
    mean_square = lax.psum(jnp.sum(rows_float * rows_float, axis=1), "narrow") / D
    row_scale = lax.rsqrt(mean_square + EPSILON)
    normed = (rows_float * row_scale[:, None] * gain[None, :]).astype(jnp.bfloat16)
    weight_full = lax.all_gather(key_value_weight, ("section", "wide"), axis=0, tiled=True)
    partial_value = contract_last(normed, weight_full)
    projected = lax.psum_scatter(partial_value, "narrow", scatter_dimension=1, tiled=True)
    residual = (projected - kv_target.astype(jnp.float32)).astype(jnp.bfloat16)
    residual_full = lax.all_gather(residual, "narrow", axis=1, tiled=True)
    back_rows = jnp.dot(residual_full, weight_full, preferred_element_type=jnp.float32)
    weighted = back_rows * gain[None, :]
    inner_sum = lax.psum(jnp.sum(weighted * rows_float, axis=1), "narrow")
    grad_rows = (
        row_scale[:, None] * weighted - rows_float * (row_scale**3 * inner_sum / D)[:, None]
    ).astype(jnp.bfloat16)
    occupied = holder >= 0
    outgoing = jnp.where(
        occupied[:, None],
        jnp.take(grad_rows, jnp.where(occupied, holder, 0), axis=0),
        jnp.zeros((), jnp.bfloat16),
    )
    incoming = lax.all_to_all(
        outgoing.reshape(owners, slot_count, width_here),
        ("section", "wide"),
        split_axis=0,
        concat_axis=0,
        tiled=True,
    )
    vocab_rows = table.shape[0]
    matches = (
        wanted.reshape(1, owners * slot_count) == jnp.arange(vocab_rows, dtype=jnp.int32)[:, None]
    ).astype(jnp.bfloat16)
    table_grad = jnp.dot(
        matches,
        incoming.reshape(owners * slot_count, width_here),
        preferred_element_type=jnp.float32,
    )
    return table_grad.astype(jnp.bfloat16)


def solution(mesh):
    return jax.shard_map(
        on_device,
        mesh=mesh,
        in_specs=(
            P(("section", "wide"), None),
            P(("section", "wide")),
            P(("section", "wide"), "narrow"),
            P("narrow"),
            P(("section", "wide"), "narrow"),
            P(("section", "wide"), "narrow"),
        ),
        out_specs=P(("section", "wide"), "narrow"),
        check_vma=False,
    )
```

profile of v0, /device:TPU:0, one launch (start us, length us, event | category | flops | bytes accessed | tf_op | source)
XLA Modules:
  0.0 256.6 jit_solution(17003256931177738602)
XLA Ops:
  6.5 0.0 copy-start
  6.5 0.0 all-gather.2.cloned.1.call-start
  6.5 0.7 all-gather.2.cloned.1.call-update
  7.3 0.7 fusion.11
  8.0 0.2 reduce_window_sum.11
  8.2 0.8 select_reduce_fusion
  9.0 0.7 and_bitcast_fusion
  9.7 1.1 scatter_custom_fusion
  10.8 0.1 all_to_all.16
  10.9 13.6 %all_to_all.25 = s32[8,1,32]{2,1,0:T(1,128)S(1)} all-to-all(s32[8,1,32]{2,1,0:T(1,128)S(1)} %all_to_all.16), channel_id=1, replica_groups=mesh['section'=2,'wide'=4,'narrow'=4] {'section','wide'}, dimensions={0} | all-to-all | bytes 2048 | tf_op jit(solution)/shard_map/all_to_all | solution.py:40
  24.5 0.1 reshape.81
  24.5 0.0 copy-done
  24.5 0.0 copy-start.3
  24.6 1.4 gather_fusion
  25.9 1.2 select_select_fusion.1
  27.1 3.6 %all-to-all-start.1 = ((bf16[8,32,2048]{2,1,0:T(8,128)(2,1)}), bf16[8,32,2048]{2,1,0:T(8,128)(2,1)S(1)}, u32[]{:S(2)}, u32[]{:S(2)}) async-start(bf16[8,32,2048]{2,1,0:T(8,128)(2,1)} %select_select_fusion.1), calls=%async_computation.1 | async-start | bytes 2097152 | tf_op jit(solution)/shard_map/all_to_all | solution.py:43
  30.7 0.0 copy-start.2
  30.7 0.0 reduce-scatter.2.cloned.1.call-start
  30.8 50.5 %all-to-all-done.1 = bf16[8,32,2048]{2,1,0:T(8,128)(2,1)S(1)} async-done(((bf16[8,32,2048]{2,1,0:T(8,128)(2,1)}), bf16[8,32,2048]{2,1,0:T(8,128)(2,1)S(1)}, u32[]{:S(2)}, u32[]{:S(2)}) %all-to-all-start.1) | async-done | bytes 1048608 | tf_op jit(solution)/shard_map/all_to_all | solution.py:43
  81.3 1.8 gather_fusion.1
  83.1 0.0 copy-start.1
  83.1 1.4 fusion
  84.5 5.7 %psum.14 = f32[128]{0:T(128)S(1)} all-reduce(f32[128]{0:T(128)S(1)} %fusion), channel_id=1, replica_groups=mesh['section'=2,'wide'=4,'narrow'=4] {'narrow'}, use_global_device_ids=true, to_apply=%region_5.6 | all-reduce | flops 128 | bytes 1024 | tf_op jit(solution)/shard_map/psum | solution.py:52
  90.2 69.3 %all-gather.2.cloned.1.call-done = bf16[2048,2048]{1,0:T(8,128)(2,1)} async-done(((bf16[256,2048]{1,0:T(8,128)(2,1)}), bf16[2048,2048]{1,0:T(8,128)(2,1)}) %all-gather.2.cloned.1.call-update) | async-done | bytes 8388624 | tf_op jit(solution)/shard_map/all_gather | solution.py:55
  159.5 0.0 copy-done.3
  159.5 7.4 %fusion.6 = f32[128,2048]{1,0:T(8,128)} fusion(bf16[2048,2048]{1,0:T(8,128)(2,1)} %all-gather.2.cloned.1.call-done, f32[2048]{0:T(1024)S(1)} %copy-done.3, f32[128]{0:T(128)S(1)} %add_rsqrt_fusion, bf16[128,2048]{1,0:T(8,128)(2,1)} %gather_fusion.1, pred[128]{0:T(512)(128)(4,1)S(1)} %get-tuple-element.7), kind=kOutput, calls=%fused_computation.19 | convolution fusion | flops 1075052544 | bytes 9970304 | tf_op jit(solution)/shard_map/dot_general | solution.py:13
  166.9 0.0 reduce-scatter.2.cloned.1.call-update
  167.0 1.0 scatter_custom_fusion.1
  168.0 0.1 broadcast_in_dim.71
  168.1 0.1 broadcast_in_dim.73
  168.1 22.0 %reduce-scatter.2.cloned.1.call-done = f32[128,512]{1,0:T(8,128)} async-done(((f32[128,2048]{1,0:T(8,128)}), f32[128,512]{1,0:T(8,128)}) %reduce-scatter.2.cloned.1.call-update) | async-done | bytes 262160 | tf_op jit(solution)/shard_map/reduce_scatter | solution.py:57
  190.2 0.0 copy-done.2
  190.2 1.0 subtract_convert_fusion
  191.1 6.8 %all_gather.7 = bf16[128,2048]{1,0:T(8,128)(2,1)S(1)} all-gather(bf16[128,512]{1,0:T(8,128)(2,1)S(1)} %subtract_convert_fusion), channel_id=1, replica_groups=mesh['section'=2,'wide'=4,'narrow'=4] {'narrow'}, dimensions={1}, use_global_device_ids=true | all-gather | bytes 655360 | tf_op jit(solution)/shard_map/all_gather | solution.py:59
  197.9 0.0 copy-done.1
  197.9 5.7 %fusion.3 = (f32[128]{0:T(128)S(1)}, f32[128,2048]{1,0:T(8,128)}) fusion(bf16[128,2048]{1,0:T(8,128)(2,1)S(1)} %copy-done.1, pred[128]{0:T(512)(128)(4,1)S(1)} %get-tuple-element.7, f32[2048]{0:T(1024)S(1)} %copy-done.3, bf16[128,2048]{1,0:T(8,128)(2,1)S(1)} %all_gather.7, bf16[2048,2048]{1,0:T(8,128)(2,1)} %all-gather.2.cloned.1.call-done), kind=kOutput, calls=%fused_computation.14 | convolution fusion | flops 1075052416 | bytes 10494592 | tf_op jit(solution)/shard_map/dot_general | solution.py:60
  203.7 6.5 %psum.15 = f32[128]{0:T(128)S(1)} all-reduce(f32[128]{0:T(128)S(1)} %get-tuple-element.12), channel_id=1, replica_groups=mesh['section'=2,'wide'=4,'narrow'=4] {'narrow'}, use_global_device_ids=true, to_apply=%region_8.9 | all-reduce | flops 128 | bytes 1024 | tf_op jit(solution)/shard_map/psum | solution.py:62
  210.2 1.5 fusion.5
  211.7 2.3 gather_fusion.2
  214.0 2.4 select_select_fusion
  216.4 5.5 %all-to-all-start.2 = ((bf16[8,32,2048]{2,1,0:T(8,128)(2,1)}), bf16[8,32,2048]{2,1,0:T(8,128)(2,1)S(1)}, u32[]{:S(2)}, u32[]{:S(2)}) async-start(bf16[8,32,2048]{2,1,0:T(8,128)(2,1)} %select_select_fusion), calls=%async_computation.3 | async-start | bytes 2097152 | tf_op jit(solution)/shard_map/all_to_all | solution.py:72
  221.9 0.6 broadcast.120
  222.5 0.7 reduce.3
  223.2 0.1 eq.34
  223.3 24.4 %all-to-all-done.2 = bf16[8,32,2048]{2,1,0:T(8,128)(2,1)S(1)} async-done(((bf16[8,32,2048]{2,1,0:T(8,128)(2,1)}), bf16[8,32,2048]{2,1,0:T(8,128)(2,1)S(1)}, u32[]{:S(2)}, u32[]{:S(2)}) %all-to-all-start.2) | async-done | bytes 1048608 | tf_op jit(solution)/shard_map/all_to_all | solution.py:72
  247.7 2.0 convolution_convert_fusion
  (9 shorter events, 0.1 us)
Async XLA Ops:
  6.5 18.0 %copy-start = (bf16[512,2048]{1,0:T(8,128)(2,1)S(1)}, bf16[512,2048]{1,0:T(8,128)(2,1)}, u32[]{:S(2)}) copy-start(bf16[512,2048]{1,0:T(8,128)(2,1)} %param.8) | copy-start | bytes 6291460
  6.5 153.0 %all-gather.2.cloned.1.call-start = ((), (), s32[]{:S(2)}) async-start(), calls=%async_computation.4 | async-start | bytes 9437184 | tf_op jit(solution)/shard_map/all_gather | solution.py:55
  24.5 134.9 %copy-start.3 = (f32[2048]{0:T(1024)S(1)}, f32[2048]{0:T(1024)}, u32[]{:S(2)}) copy-start(f32[2048]{0:T(1024)} %param.9) | copy-start | bytes 24580
  27.1 54.2 %all-to-all-start.1 = ((bf16[8,32,2048]{2,1,0:T(8,128)(2,1)}), bf16[8,32,2048]{2,1,0:T(8,128)(2,1)S(1)}, u32[]{:S(2)}, u32[]{:S(2)}) async-start(bf16[8,32,2048]{2,1,0:T(8,128)(2,1)} %select_select_fusion.1), calls=%async_computation.1 | async-start | bytes 2097152 | tf_op jit(solution)/shard_map/all_to_all | solution.py:43
  30.7 159.5 %copy-start.2 = (bf16[128,512]{1,0:T(8,128)(2,1)S(1)}, bf16[128,512]{1,0:T(8,128)(2,1)}, u32[]{:S(2)}) copy-start(bf16[128,512]{1,0:T(8,128)(2,1)} %param.11) | copy-start | bytes 393220
  30.7 159.5 %reduce-scatter.2.cloned.1.call-start = ((), (), s32[]{:S(2)}) async-start(), calls=%async_computation.5 | async-start | bytes 1310720 | tf_op jit(solution)/shard_map/reduce_scatter | solution.py:57
  83.1 114.8 %copy-start.1 = (bf16[128,2048]{1,0:T(8,128)(2,1)S(1)}, bf16[128,2048]{1,0:T(8,128)(2,1)}, u32[]{:S(2)}) copy-start(bf16[128,2048]{1,0:T(8,128)(2,1)} %gather_fusion.1) | copy-start | bytes 1572868
  216.4 31.3 %all-to-all-start.2 = ((bf16[8,32,2048]{2,1,0:T(8,128)(2,1)}), bf16[8,32,2048]{2,1,0:T(8,128)(2,1)S(1)}, u32[]{:S(2)}, u32[]{:S(2)}) async-start(bf16[8,32,2048]{2,1,0:T(8,128)(2,1)} %select_select_fusion), calls=%async_computation.3 | async-start | bytes 2097152 | tf_op jit(solution)/shard_map/all_to_all | solution.py:72
Sparse Core Ops, SparseCore 0:
  9.5 149.9 all-gather.1
  167.1 23.0 reduce-scatter.1
where the time goes:
time: 257 us
  waiting for transfers between devices  167 us (65%)
  blocking collectives  32.5 us (13%)
  matrix products  15.2 us (6%)
  between operations  13.5 us (5%)
  other arithmetic  10.6 us (4%)
  starting transfers between devices  9.12 us (4%)
  local copies, waits for them, and re-layouts  8.57 us (3%)
    all_gather x1, waiting for transfers between devices, on_device(): lax.all_gather(key_value_weight, ('section', 'wide'), axis=0, tiled=True)  69.3 us
    all_to_all x1, waiting for transfers between devices, on_device(): lax.all_to_all(jnp.where(present[..., None], picked, jnp.zeros((), table....  50.5 us
    all_to_all x1, waiting for transfers between devices, on_device(): lax.all_to_all(outgoing.reshape(owners, slot_count, width_here), ('sectio...  24.4 us
    reduce_scatter x1, waiting for transfers between devices, on_device(): lax.psum_scatter(partial_value, 'narrow', scatter_dimension=1, tiled=True)  22 us
    all_to_all x1, blocking collectives, on_device(): lax.all_to_all(requests, ('section', 'wide'), split_axis=0, concat_axis=0...  13.6 us
    dot_general x1, matrix products, contract_last(): lax.dot_general(left, right, (((1,), (1,)), ((), ())), preferred_element_...  7.44 us
    all_gather x1, blocking collectives, on_device(): residual_full = lax.all_gather(residual, 'narrow', axis=1, tiled=True)  6.78 us
    psum x1, blocking collectives, on_device(): inner_sum = lax.psum(jnp.sum(weighted * rows_float, axis=1), 'narrow')  6.5 us
  transfers between devices with their start and end apart: 4, of which 4 were waited for; matrix products, arithmetic and copies ran while one was open for 5% of the time, Pallas kernels for 0%

commit v1 on v0

v1 whole, which is shorter than its diff:
```python
import jax
import jax.numpy as jnp
from jax import lax
from jax.sharding import PartitionSpec as P

EPSILON = 1e-05

HOLDERS = ("section", "wide")
LANES = 128


def contract_last(left, right):
    return lax.dot_general(
        left, right, (((1,), (1,)), ((), ())), preferred_element_type=jnp.float32
    )


def contract_first(left, right):
    return lax.dot_general(
        left, right, (((0,), (0,)), ((), ())), preferred_element_type=jnp.float32
    )


def exchange_narrow(value, distance):
    narrow = lax.axis_size("narrow")
    return lax.ppermute(value, "narrow", [(i, i ^ distance) for i in range(narrow)])


def sum_narrow(value):
    distance = 1
    while distance < lax.axis_size("narrow"):
        value = value + exchange_narrow(value, distance)
        distance *= 2
    return value


def send_wide(value, pairs):
    return lax.ppermute(value, "wide", pairs)


def send_section(value):
    return lax.ppermute(value, "section", [(0, 1), (1, 0)])


def slots_of(shard_column, slot_count):
    tokens = shard_column.shape[0]
    shard_row = shard_column.reshape(1, tokens)
    earlier = lax.broadcasted_iota(jnp.int32, (tokens, tokens), 0) < lax.broadcasted_iota(
        jnp.int32, (tokens, tokens), 1
    )
    rank = jnp.sum(((shard_column == shard_row) & earlier).astype(jnp.int32), axis=0)
    position = shard_row * slot_count + rank[None, :]
    slots = lax.axis_size(HOLDERS) * slot_count
    return lax.broadcasted_iota(jnp.int32, (slots, tokens), 0) == position


def weight_pieces(weight):
    section, wide = lax.axis_index("section"), lax.axis_index("wide")
    rows = weight.shape[0]
    if lax.axis_size("section") != 2 or lax.axis_size("wide") != 4:
        whole = lax.all_gather(weight, HOLDERS, axis=0, tiled=True)
        size = 256
        return [
            (jnp.int32(at // size), whole[at : at + size])
            for at in range(0, whole.shape[0], size)
        ]
    half = rows // 2
    halves = (weight[:half], weight[half:])
    inner = (wide == 1) | (wide == 2)
    pair = [(0, 1), (1, 0), (2, 3), (3, 2)]
    middle = [(1, 2), (2, 1)]
    outward = [(1, 0), (2, 3)]
    here = section * 4
    there = (1 - section) * 4
    near, far = wide ^ 1, jnp.where(inner, 3 - wide, wide ^ 2)
    last = jnp.where(inner, wide ^ 2, 3 - wide)
    out = [(here + wide, 0, halves[0]), (here + wide, 1, halves[1])]
    p1 = [send_wide(w, pair) for w in halves]
    q2 = [send_wide(w, middle) for w in halves]
    y0 = [send_section(w) for w in halves]
    e1 = [send_wide(w, outward) for w in q2]
    q3 = [send_wide(w, middle) for w in p1]
    y1 = send_section(p1[0])
    e2 = [send_wide(w, outward) for w in q3]
    m2 = [jnp.where(inner, a, b) for a, b in zip(q2, e1)]
    y2 = [send_section(w) for w in m2]
    x1 = send_wide(y0[1], pair)
    m3 = [jnp.where(inner, a, b) for a, b in zip(q3, e2)]
    y3 = [send_section(w) for w in m3]
    out += [(there + wide, i, y0[i]) for i in range(2)]
    out += [(here + near, i, p1[i]) for i in range(2)]
    out += [(here + far, i, m2[i]) for i in range(2)]
    out += [(there + near, 0, y1)]
    out += [(there + far, i, y2[i]) for i in range(2)]
    out += [(here + last, i, m3[i]) for i in range(2)]
    out += [(there + near, 1, x1)]
    out += [(there + last, i, y3[i]) for i in range(2)]
    return [(holder * 2 + part, piece) for holder, part, piece in out]


def on_device(token_shard, token_row, table, gain, key_value_weight, kv_target):
    tokens_here = token_row.shape[0]
    owners = lax.axis_size(HOLDERS)
    narrow = lax.axis_size("narrow")
    slot_count = 2 * tokens_here // owners
    slots = owners * slot_count
    vocab_rows, width_here = table.shape
    width = width_here * narrow
    target_width = kv_target.shape[1]
    pieces = weight_pieces(key_value_weight)

    to_slot = slots_of(token_shard, slot_count).astype(jnp.bfloat16)
    row_parts = jnp.stack(
        [token_row // 256, token_row % 256, jnp.ones_like(token_row)], axis=1
    ).astype(jnp.bfloat16)
    row_parts = jnp.pad(row_parts, ((0, 0), (0, LANES - 3)))
    sent = jnp.dot(
        to_slot,
        jnp.concatenate([kv_target, row_parts], axis=1),
        preferred_element_type=jnp.float32,
    ).astype(jnp.bfloat16)
    arrived = lax.all_to_all(
        sent.reshape(owners, slot_count, target_width + LANES),
        HOLDERS,
        split_axis=0,
        concat_axis=0,
        tiled=True,
    ).reshape(slots, target_width + LANES)
    row_parts = arrived[:, target_width : target_width + 3].astype(jnp.float32)
    row = (row_parts[:, :1] * 256 + row_parts[:, 1:2]).astype(jnp.int32)
    row = jnp.where(row_parts[:, 2:3] > 0.5, row, -1)
    picks = (row == lax.broadcasted_iota(jnp.int32, (slots, vocab_rows), 1)).astype(jnp.bfloat16)
    hidden = jnp.dot(picks, table, preferred_element_type=jnp.float32).astype(jnp.bfloat16)
    rows_float = hidden.astype(jnp.float32)
    mean_square = sum_narrow(jnp.sum(rows_float * rows_float, axis=1, keepdims=True)) / width
    row_scale = lax.rsqrt(mean_square + EPSILON)
    normed = (rows_float * row_scale * gain[None, :]).astype(jnp.bfloat16)

    target_here = arrived[:, :target_width]
    targets = jnp.stack(
        [target_here] + [exchange_narrow(target_here, d) for d in range(1, narrow)]
    )
    my_narrow = lax.axis_index("narrow")

    back_rows = jnp.zeros((slots, width_here), jnp.float32)
    inner_sum = jnp.zeros((slots, 1), jnp.float32)
    for place, piece in pieces:
        features = piece.shape[0]
        at = place * features
        projected = sum_narrow(contract_last(normed, piece))
        source = at // target_width
        target = lax.dynamic_slice(
            targets, (source ^ my_narrow, 0, at % target_width), (1, slots, features)
        )[0]
        residual = (projected - target.astype(jnp.float32)).astype(jnp.bfloat16)
        inner_sum += jnp.sum(residual.astype(jnp.float32) * projected, axis=1, keepdims=True)
        back_rows += jnp.dot(residual, piece, preferred_element_type=jnp.float32)

    grad_rows = (
        row_scale * (back_rows * gain[None, :])
        - rows_float * (row_scale * row_scale * inner_sum / width)
    ).astype(jnp.bfloat16)
    return contract_first(picks, grad_rows).astype(jnp.bfloat16)


def solution(mesh):
    return jax.shard_map(
        on_device,
        mesh=mesh,
        in_specs=(
            P(("section", "wide"), None),
            P(("section", "wide")),
            P(("section", "wide"), "narrow"),
            P("narrow"),
            P(("section", "wide"), "narrow"),
            P(("section", "wide"), "narrow"),
        ),
        out_specs=P(("section", "wide"), "narrow"),
        check_vma=False,
    )
```

time: 257 us -> 205 us (0.80)
  waiting for transfers between devices: 167 us -> 85.8 us
  starting transfers between devices: 9.12 us -> 46 us
  matrix products: 15.2 us -> 39.3 us
  blocking collectives: 32.5 us -> 18.3 us
  between operations: 13.5 us -> 1.15 us
  local copies, waits for them, and re-layouts: 8.57 us -> 1.75 us
    ppermute x0 -> x55, waiting for transfers between devices: none -> 85.8 us  [the longest x37 39.9 us: exchange_narrow(): lax.ppermute(value, 'narrow', [(i, i ^ distance) for i in range(narrow)])]
    all_to_all x2 -> x0, waiting for transfers between devices: 74.9 us -> none  [the longest x1 50.5 us: on_device(): lax.all_to_all(jnp.where(present[..., None], picked, jnp.zeros((), table....]
    all_gather x1 -> x0, waiting for transfers between devices: 69.3 us -> none  [on_device(): lax.all_gather(key_value_weight, ('section', 'wide'), axis=0, tiled=True)]
    ppermute x0 -> x55, starting transfers between devices: none -> 46 us  [the longest x37 21.6 us: exchange_narrow(): lax.ppermute(value, 'narrow', [(i, i ^ distance) for i in range(narrow)])]
    reduce_scatter x1 -> x0, waiting for transfers between devices: 22 us -> none  [on_device(): lax.psum_scatter(partial_value, 'narrow', scatter_dimension=1, tiled=True)]
    dot_general x2 -> x18, matrix products: 7.79 us -> 27.6 us  [the longest x15 17.5 us: on_device(): back_rows += jnp.dot(residual, piece, preferred_element_type=jnp.float32)]
    psum x2 -> x0, blocking collectives: 12.2 us -> none  [the longest x1 6.5 us: on_device(): inner_sum = lax.psum(jnp.sum(weighted * rows_float, axis=1), 'narrow')]
    all_to_all x2 -> x0, starting transfers between devices: 9.07 us -> none  [the longest x1 5.51 us: on_device(): lax.all_to_all(outgoing.reshape(owners, slot_count, width_here), ('sectio...]
  transfers between devices with their start and end apart: 4 -> 55, of which waited for: 4 -> 22; matrix products, arithmetic and copies ran while one was open for 5% -> 18% of each run, Pallas kernels for 0% -> 0%
where the time goes in v1:
time: 205 us; the launch traced here: 204 us
  waiting for transfers between devices  85.8 us (42%)
  starting transfers between devices  46 us (22%)
  matrix products  39.3 us (19%)
  blocking collectives  18.3 us (9%)
  other arithmetic  12.2 us (6%)
    ppermute x37, waiting for transfers between devices, exchange_narrow(): lax.ppermute(value, 'narrow', [(i, i ^ distance) for i in range(narrow)])  39.9 us
    ppermute x11, waiting for transfers between devices, send_wide(): return lax.ppermute(value, 'wide', pairs)  38.6 us
    ppermute x37, starting transfers between devices, exchange_narrow(): lax.ppermute(value, 'narrow', [(i, i ^ distance) for i in range(narrow)])  21.6 us
    all_to_all x1, blocking collectives, on_device(): lax.all_to_all(sent.reshape(owners, slot_count, target_width + LANES), HO...  18.3 us
    dot_general x15, matrix products, on_device(): back_rows += jnp.dot(residual, piece, preferred_element_type=jnp.float32)  17.5 us
    ppermute x11, starting transfers between devices, send_wide(): return lax.ppermute(value, 'wide', pairs)  17.3 us
    dot_general x16, matrix products, contract_last(): lax.dot_general(left, right, (((1,), (1,)), ((), ())), preferred_element_...  11.8 us
    ppermute x7, waiting for transfers between devices, send_section(): return lax.ppermute(value, 'section', [(0, 1), (1, 0)])  7.27 us
  transfers between devices with their start and end apart: 55, of which 22 were waited for; matrix products, arithmetic and copies ran while one was open for 18% of the time, Pallas kernels for 0%

profile of v1, /device:TPU:0, one launch (start us, length us, event | category | flops | bytes accessed | tf_op | source)
XLA Modules:
  0.0 204.5 jit_solution(12274930600627980456)
XLA Ops:
  3.7 18.3 %all_to_all.5 = bf16[8,32,640]{2,1,0:T(8,128)(2,1)S(1)} all-to-all(bf16[8,32,640]{2,1,0:T(8,128)(2,1)S(1)} %bitcast.162), channel_id=1, replica_groups=mesh['section'=2,'wide'=4,'narrow'=4] {'section','wide'}, dimensions={0} | all-to-all | bytes 655360 | tf_op jit(solution)/shard_map/all_to_all | solution.py:122
  22.2 1.7 fusion.16
  25.1 1.5 collective-permute-start.1
  27.7 1.5 collective-permute-start.21
  29.2 1.6 collective-permute-start.15
  31.9 1.5 collective-permute-start.9
  33.5 1.5 fusion.18
  35.0 9.3 %collective-permute-done.15 = bf16[128,2048]{1,0:T(8,128)(2,1)} collective-permute-done((bf16[128,2048]{1,0:T(8,128)(2,1)}, bf16[128,2048]{1,0:T(8,128)(2,1)}, u32[]{:S(2)}, u32[]{:S(2)}) %collective-permute-start.15) | collective-permute-done | bytes 524320 | tf_op jit(solution)/shard_map/ppermute | solution.py:38
  44.3 1.5 fusion.113
  46.0 1.5 fusion.112
  48.0 6.4 %collective-permute-done.18 = bf16[128,2048]{1,0:T(8,128)(2,1)} collective-permute-done((bf16[128,2048]{1,0:T(8,128)(2,1)}, bf16[128,2048]{1,0:T(8,128)(2,1)}, u32[]{:S(2)}, u32[]{:S(2)}) %collective-permute-start.18) | collective-permute-done | bytes 524320 | tf_op jit(solution)/shard_map/ppermute | solution.py:38
  54.5 1.5 fusion.114
  58.5 1.5 collective-permute-start.5
  70.4 1.3 collective-permute-start.22
  72.7 1.2 pad_maximum_fusion
  73.9 3.5 %collective-permute-done.11 = f32[256,128]{0,1:T(8,128)S(1)} collective-permute-done((f32[256,128]{0,1:T(8,128)S(1)}, f32[256,128]{0,1:T(8,128)S(1)}, u32[]{:S(2)}, u32[]{:S(2)}) %collective-permute-start.11) | collective-permute-done | bytes 131104 | tf_op jit(solution)/shard_map/ppermute | solution.py:26
  78.4 4.0 %collective-permute-done.14 = f32[256,128]{0,1:T(8,128)S(1)} collective-permute-done((f32[256,128]{0,1:T(8,128)S(1)}, f32[256,128]{0,1:T(8,128)S(1)}, u32[]{:S(2)}, u32[]{:S(2)}) %collective-permute-start.14) | collective-permute-done | bytes 131104 | tf_op jit(solution)/shard_map/ppermute | solution.py:26
  82.9 1.5 fusion.57
  84.4 2.9 %collective-permute-done.8 = f32[256,128]{0,1:T(8,128)S(1)} collective-permute-done((f32[256,128]{0,1:T(8,128)S(1)}, f32[256,128]{0,1:T(8,128)S(1)}, u32[]{:S(2)}, u32[]{:S(2)}) %collective-permute-start.8) | collective-permute-done | bytes 131104 | tf_op jit(solution)/shard_map/ppermute | solution.py:26
  88.4 4.9 %collective-permute-done.17 = f32[256,128]{0,1:T(8,128)S(1)} collective-permute-done((f32[256,128]{0,1:T(8,128)S(1)}, f32[256,128]{0,1:T(8,128)S(1)}, u32[]{:S(2)}, u32[]{:S(2)}) %collective-permute-start.17) | collective-permute-done | bytes 131104 | tf_op jit(solution)/shard_map/ppermute | solution.py:26
  93.8 1.5 fusion.59
  96.0 2.2 %collective-permute-done.20 = f32[256,128]{0,1:T(8,128)S(1)} collective-permute-done((f32[256,128]{0,1:T(8,128)S(1)}, f32[256,128]{0,1:T(8,128)S(1)}, u32[]{:S(2)}, u32[]{:S(2)}) %collective-permute-start.20) | collective-permute-done | bytes 131104 | tf_op jit(solution)/shard_map/ppermute | solution.py:26
  98.3 1.3 collective-permute-start.26
  99.5 1.5 fusion.61
  101.1 6.5 %collective-permute-start.46 = (bf16[128,2048]{1,0:T(8,128)(2,1)}, bf16[128,2048]{1,0:T(8,128)(2,1)S(1)}, u32[]{:S(2)}, u32[]{:S(2)}) collective-permute-start(bf16[128,2048]{1,0:T(8,128)(2,1)} %collective-permute-done.12), channel_id=1, source_target_pairs={{0,4},{4,0},{8,12},{12,8},{1,5},{5,1},{9,13},{13,9},{2,6},{6,2},{1... | collective-permute-start | bytes 1572872 | tf_op jit(solution)/shard_map/ppermute | solution.py:38
  107.7 10.7 %collective-permute-done.26 = bf16[128,2048]{1,0:T(8,128)(2,1)S(1)} collective-permute-done((bf16[128,2048]{1,0:T(8,128)(2,1)S(1)}, bf16[128,2048]{1,0:T(8,128)(2,1)S(1)}, u32[]{:S(2)}, u32[]{:S(2)}) %collective-permute-start.26) | collective-permute-done | bytes 524320 | tf_op jit(solution)/shard_map/ppermute | solution.py:38
  120.9 3.1 %collective-permute-done.46 = bf16[128,2048]{1,0:T(8,128)(2,1)S(1)} collective-permute-done((bf16[128,2048]{1,0:T(8,128)(2,1)}, bf16[128,2048]{1,0:T(8,128)(2,1)S(1)}, u32[]{:S(2)}, u32[]{:S(2)}) %collective-permute-start.46) | collective-permute-done | bytes 524320 | tf_op jit(solution)/shard_map/ppermute | solution.py:38
  127.6 1.5 collective-permute-start.32
  129.8 1.3 collective-permute-start.39
  131.1 1.5 collective-permute-start.43
  132.6 1.2 collective-permute-start.31
  134.3 3.3 %collective-permute-done.31 = f32[256,128]{0,1:T(8,128)S(1)} collective-permute-done((f32[256,128]{0,1:T(8,128)S(1)}, f32[256,128]{0,1:T(8,128)S(1)}, u32[]{:S(2)}, u32[]{:S(2)}) %collective-permute-start.31) | collective-permute-done | bytes 131104 | tf_op jit(solution)/shard_map/ppermute | solution.py:26
  139.3 3.3 %collective-permute-done.48 = f32[256,128]{0,1:T(8,128)S(1)} collective-permute-done((f32[256,128]{0,1:T(8,128)S(1)}, f32[256,128]{0,1:T(8,128)S(1)}, u32[]{:S(2)}, u32[]{:S(2)}) %collective-permute-start.48) | collective-permute-done | bytes 131104 | tf_op jit(solution)/shard_map/ppermute | solution.py:26
  143.8 1.8 fusion.76
  147.3 8.7 %collective-permute-done.43 = bf16[128,2048]{1,0:T(8,128)(2,1)S(1)} collective-permute-done((bf16[128,2048]{1,0:T(8,128)(2,1)S(1)}, bf16[128,2048]{1,0:T(8,128)(2,1)S(1)}, u32[]{:S(2)}, u32[]{:S(2)}) %collective-permute-start.43) | collective-permute-done | bytes 524320 | tf_op jit(solution)/shard_map/ppermute | solution.py:38
  157.8 1.2 collective-permute-start.34
  159.2 1.4 collective-permute-start.49
  162.3 1.2 collective-permute-start.45
  163.5 1.3 collective-permute-start.37
  165.3 6.4 %collective-permute-done.37 = f32[256,128]{0,1:T(8,128)S(1)} collective-permute-done((f32[256,128]{0,1:T(8,128)S(1)}, f32[256,128]{0,1:T(8,128)S(1)}, u32[]{:S(2)}, u32[]{:S(2)}) %collective-permute-start.37) | collective-permute-done | bytes 131104 | tf_op jit(solution)/shard_map/ppermute | solution.py:26
  172.2 2.2 %fusion.8 = f32[256,2048]{1,0:T(8,128)} fusion(f32[256,2048]{1,0:T(8,128)S(1)} %fusion.70, f32[256,2048]{1,0:T(8,128)S(1)} %fusion.68, f32[256,2048]{1,0:T(8,128)S(1)} %fusion.66, f32[256,2048]{1,0:T(8,128)S(1)} %fusion.64, f32[256,2048]{1,0:T(8,128)S(1)} %fusion.12, bf16[128,2048]{1,0:T(8,128)(2,1)S(1)} %broadcast_select_fusion.3, ...), kind=kOutput, calls=%fused_computation.14 | convolution fusion | flops 136970240 | bytes 13434888 | tf_op jit(solution)/shard_map/dot_general | solution.py:157
  174.4 1.8 fusion.74
  176.8 7.2 %collective-permute-done.52 = bf16[128,2048]{1,0:T(8,128)(2,1)S(1)} collective-permute-done((bf16[128,2048]{1,0:T(8,128)(2,1)S(1)}, bf16[128,2048]{1,0:T(8,128)(2,1)S(1)}, u32[]{:S(2)}, u32[]{:S(2)}) %collective-permute-start.52) | collective-permute-done | bytes 524320 | tf_op jit(solution)/shard_map/ppermute | solution.py:42
  187.1 4.0 %collective-permute-done.51 = f32[256,128]{0,1:T(8,128)S(1)} collective-permute-done((f32[256,128]{0,1:T(8,128)S(1)}, f32[256,128]{0,1:T(8,128)S(1)}, u32[]{:S(2)}, u32[]{:S(2)}) %collective-permute-start.51) | collective-permute-done | bytes 131104 | tf_op jit(solution)/shard_map/ppermute | solution.py:26
  191.2 2.4 %collective-permute-done.54 = f32[256,128]{0,1:T(8,128)S(1)} collective-permute-done((f32[256,128]{0,1:T(8,128)S(1)}, f32[256,128]{0,1:T(8,128)S(1)}, u32[]{:S(2)}, u32[]{:S(2)}) %collective-permute-start.54) | collective-permute-done | bytes 131104 | tf_op jit(solution)/shard_map/ppermute | solution.py:26
  193.8 1.8 fusion.78
  195.5 1.8 fusion.80
  197.3 7.2 %convolution_convert_fusion = bf16[512,2048]{1,0:T(8,128)(2,1)} fusion(f32[256,2048]{1,0:T(8,128)} %fusion.80, f32[256,2048]{1,0:T(8,128)} %fusion.78, f32[256,2048]{1,0:T(8,128)} %fusion.76, f32[256,2048]{1,0:T(8,128)} %fusion.74, f32[256,2048]{1,0:T(8,128)} %fusion.8, bf16[128,2048]{1,0:T(8,128)(2,1)S(1)} %copy-done.3, ...), kind=kOutput, calls=%fused_computation.3 | convolution fusion | flops 678166528 | bytes 14494728 | tf_op jit(solution)/shard_map/dot_general | solution.py:19
  (176 shorter events, 45.0 us)
Async XLA Ops:
  25.1 6.8 %collective-permute-start.1 = (f32[256,1]{0,1:T(1,128)S(1)}, f32[256,1]{0,1:T(1,128)S(1)}, u32[]{:S(2)}, u32[]{:S(2)}) collective-permute-start(f32[256,1]{0,1:T(1,128)S(1)} %add.564), channel_id=1, source_target_pairs={{0,2},{1,3},{2,0},{3,1},{4,6},{5,7},{6,4},{7,5},{8,10},{9,11},{10,... | collective-permute-start | bytes 3080 | tf_op jit(solution)/shard_map/ppermute | solution.py:26
  27.7 41.3 %collective-permute-start.21 = (bf16[128,2048]{1,0:T(8,128)(2,1)}, bf16[128,2048]{1,0:T(8,128)(2,1)}, u32[]{:S(2)}, u32[]{:S(2)}) collective-permute-start(bf16[128,2048]{1,0:T(8,128)(2,1)} %get-tuple-element.21), channel_id=1, source_target_pairs={{4,8},{8,4},{5,9},{9,5},{6,10},{10,6},{7,11},{11,7},{20,24},{24,20... | collective-permute-start | bytes 1572872 | tf_op jit(solution)/shard_map/ppermute | solution.py:38
  29.2 15.1 %collective-permute-start.15 = (bf16[128,2048]{1,0:T(8,128)(2,1)}, bf16[128,2048]{1,0:T(8,128)(2,1)}, u32[]{:S(2)}, u32[]{:S(2)}) collective-permute-start(bf16[128,2048]{1,0:T(8,128)(2,1)} %get-tuple-element.21), channel_id=1, source_target_pairs={{0,4},{4,0},{8,12},{12,8},{1,5},{5,1},{9,13},{13,9},{2,6},{6,2},{1... | collective-permute-start | bytes 1572872 | tf_op jit(solution)/shard_map/ppermute | solution.py:38
  30.8 15.2 %collective-permute-start.12 = (bf16[128,2048]{1,0:T(8,128)(2,1)}, bf16[128,2048]{1,0:T(8,128)(2,1)}, u32[]{:S(2)}, u32[]{:S(2)}) collective-permute-start(bf16[128,2048]{1,0:T(8,128)(2,1)} %get-tuple-element.22), channel_id=1, source_target_pairs={{0,16},{16,0},{1,17},{17,1},{2,18},{18,2},{3,19},{19,3},{4,20},{20... | collective-permute-start | bytes 1572872 | tf_op jit(solution)/shard_map/ppermute | solution.py:42
  31.4 23.0 %collective-permute-start.18 = (bf16[128,2048]{1,0:T(8,128)(2,1)}, bf16[128,2048]{1,0:T(8,128)(2,1)}, u32[]{:S(2)}, u32[]{:S(2)}) collective-permute-start(bf16[128,2048]{1,0:T(8,128)(2,1)} %get-tuple-element.22), channel_id=1, source_target_pairs={{0,4},{4,0},{8,12},{12,8},{1,5},{5,1},{9,13},{13,9},{2,6},{6,2},{1... | collective-permute-start | bytes 1572872 | tf_op jit(solution)/shard_map/ppermute | solution.py:38
  31.9 24.2 %collective-permute-start.9 = (bf16[128,2048]{1,0:T(8,128)(2,1)}, bf16[128,2048]{1,0:T(8,128)(2,1)S(1)}, u32[]{:S(2)}, u32[]{:S(2)}) collective-permute-start(bf16[128,2048]{1,0:T(8,128)(2,1)} %get-tuple-element.21), channel_id=1, source_target_pairs={{0,16},{16,0},{1,17},{17,1},{2,18},{18,2},{3,19},{19,3},{4,20},{20... | collective-permute-start | bytes 1572872 | tf_op jit(solution)/shard_map/ppermute | solution.py:42
  45.8 11.9 %collective-permute-start.16 = (f32[256,128]{0,1:T(8,128)S(1)}, f32[256,128]{0,1:T(8,128)S(1)}, u32[]{:S(2)}, u32[]{:S(2)}) collective-permute-start(f32[256,128]{0,1:T(8,128)S(1)} %fusion.113), channel_id=1, source_target_pairs={{0,1},{1,0},{2,3},{3,2},{4,5},{5,4},{6,7},{7,6},{8,9},{9,8},{10,11... | collective-permute-start | bytes 393224 | tf_op jit(solution)/shard_map/ppermute | solution.py:26
  47.5 10.4 %collective-permute-start.13 = (f32[256,128]{0,1:T(8,128)S(1)}, f32[256,128]{0,1:T(8,128)S(1)}, u32[]{:S(2)}, u32[]{:S(2)}) collective-permute-start(f32[256,128]{0,1:T(8,128)S(1)} %fusion.112), channel_id=1, source_target_pairs={{0,1},{1,0},{2,3},{3,2},{4,5},{5,4},{6,7},{7,6},{8,9},{9,8},{10,11... | collective-permute-start | bytes 393224 | tf_op jit(solution)/shard_map/ppermute | solution.py:26
  57.7 12.0 %collective-permute-start.6 = (bf16[256,512]{0,1:T(8,128)(2,1)S(1)}, bf16[256,512]{0,1:T(8,128)(2,1)}, u32[]{:S(2)}, u32[]{:S(2)}) collective-permute-start(bf16[256,512]{0,1:T(8,128)(2,1)S(1)} %copy.15), channel_id=1, source_target_pairs={{0,3},{1,2},{2,1},{3,0},{4,7},{5,6},{6,5},{7,4},{8,11},{9,10},{10,... | collective-permute-start | bytes 786440 | tf_op jit(solution)/shard_map/ppermute | solution.py:26
  58.0 12.4 %collective-permute-start.4 = (bf16[256,512]{0,1:T(8,128)(2,1)S(1)}, bf16[256,512]{0,1:T(8,128)(2,1)}, u32[]{:S(2)}, u32[]{:S(2)}) collective-permute-start(bf16[256,512]{0,1:T(8,128)(2,1)S(1)} %copy.15), channel_id=1, source_target_pairs={{0,1},{1,0},{2,3},{3,2},{4,5},{5,4},{6,7},{7,6},{8,9},{9,8},{10,11... | collective-permute-start | bytes 786440 | tf_op jit(solution)/shard_map/ppermute | solution.py:26
  58.5 13.7 %collective-permute-start.5 = (bf16[256,512]{0,1:T(8,128)(2,1)S(1)}, bf16[256,512]{0,1:T(8,128)(2,1)}, u32[]{:S(2)}, u32[]{:S(2)}) collective-permute-start(bf16[256,512]{0,1:T(8,128)(2,1)S(1)} %copy.15), channel_id=1, source_target_pairs={{0,2},{1,3},{2,0},{3,1},{4,6},{5,7},{6,4},{7,5},{8,10},{9,11},{10,... | collective-permute-start | bytes 786440 | tf_op jit(solution)/shard_map/ppermute | solution.py:26
  61.3 6.0 %collective-permute-start.7 = (f32[256,128]{0,1:T(8,128)}, f32[256,128]{0,1:T(8,128)}, u32[]{:S(2)}, u32[]{:S(2)}) collective-permute-start(f32[256,128]{0,1:T(8,128)} %fusion.105), channel_id=1, source_target_pairs={{0,1},{1,0},{2,3},{3,2},{4,5},{5,4},{6,7},{7,6},{8,9},{9,8},{10,11... | collective-permute-start | bytes 393224 | tf_op jit(solution)/shard_map/ppermute | solution.py:26
  67.4 28.0 %collective-permute-start.25 = (bf16[128,2048]{1,0:T(8,128)(2,1)}, bf16[128,2048]{1,0:T(8,128)(2,1)S(1)}, u32[]{:S(2)}, u32[]{:S(2)}) collective-permute-start(bf16[128,2048]{1,0:T(8,128)(2,1)} %get-tuple-element.22), channel_id=1, source_target_pairs={{4,8},{8,4},{5,9},{9,5},{6,10},{10,6},{7,11},{11,7},{20,24},{24,20... | collective-permute-start | bytes 1572872 | tf_op jit(solution)/shard_map/ppermute | solution.py:38
  69.1 51.2 %collective-permute-start.29 = (bf16[128,2048]{1,0:T(8,128)(2,1)}, bf16[128,2048]{1,0:T(8,128)(2,1)S(1)}, u32[]{:S(2)}, u32[]{:S(2)}) collective-permute-start(bf16[128,2048]{1,0:T(8,128)(2,1)} %collective-permute-done.15), channel_id=1, source_target_pairs={{0,16},{16,0},{1,17},{17,1},{2,18},{18,2},{3,19},{19,3},{4,20},{20... | collective-permute-start | bytes 1572872 | tf_op jit(solution)/shard_map/ppermute | solution.py:42
  69.7 59.5 %collective-permute-start.38 = (bf16[128,2048]{1,0:T(8,128)(2,1)}, bf16[128,2048]{1,0:T(8,128)(2,1)S(1)}, u32[]{:S(2)}, u32[]{:S(2)}) collective-permute-start(bf16[128,2048]{1,0:T(8,128)(2,1)} %collective-permute-done.15), channel_id=1, source_target_pairs={{4,8},{8,4},{5,9},{9,5},{6,10},{10,6},{7,11},{11,7},{20,24},{24,20... | collective-permute-start | bytes 1572872 | tf_op jit(solution)/shard_map/ppermute | solution.py:38
  70.4 30.7 %collective-permute-start.22 = (bf16[128,2048]{1,0:T(8,128)(2,1)}, bf16[128,2048]{1,0:T(8,128)(2,1)S(1)}, u32[]{:S(2)}, u32[]{:S(2)}) collective-permute-start(bf16[128,2048]{1,0:T(8,128)(2,1)} %collective-permute-done.21), channel_id=1, source_target_pairs={{4,0},{8,12},{5,1},{9,13},{6,2},{10,14},{7,3},{11,15},{20,16},{24,... | collective-permute-start | bytes 1572872 | tf_op jit(solution)/shard_map/ppermute | solution.py:38
  72.1 5.3 %collective-permute-start.11 = (f32[256,128]{0,1:T(8,128)S(1)}, f32[256,128]{0,1:T(8,128)S(1)}, u32[]{:S(2)}, u32[]{:S(2)}) collective-permute-start(f32[256,128]{0,1:T(8,128)S(1)} %add.581), channel_id=1, source_target_pairs={{0,2},{1,3},{2,0},{3,1},{4,6},{5,7},{6,4},{7,5},{8,10},{9,11},{10,... | collective-permute-start | bytes 393224 | tf_op jit(solution)/shard_map/ppermute | solution.py:26
  77.4 5.0 %collective-permute-start.14 = (f32[256,128]{0,1:T(8,128)S(1)}, f32[256,128]{0,1:T(8,128)S(1)}, u32[]{:S(2)}, u32[]{:S(2)}) collective-permute-start(f32[256,128]{0,1:T(8,128)S(1)} %add.588), channel_id=1, source_target_pairs={{0,2},{1,3},{2,0},{3,1},{4,6},{5,7},{6,4},{7,5},{8,10},{9,11},{10,... | collective-permute-start | bytes 393224 | tf_op jit(solution)/shard_map/ppermute | solution.py:26
  82.4 5.0 %collective-permute-start.8 = (f32[256,128]{0,1:T(8,128)S(1)}, f32[256,128]{0,1:T(8,128)S(1)}, u32[]{:S(2)}, u32[]{:S(2)}) collective-permute-start(f32[256,128]{0,1:T(8,128)S(1)} %add.574), channel_id=1, source_target_pairs={{0,2},{1,3},{2,0},{3,1},{4,6},{5,7},{6,4},{7,5},{8,10},{9,11},{10,... | collective-permute-start | bytes 393224 | tf_op jit(solution)/shard_map/ppermute | solution.py:26
  87.4 5.9 %collective-permute-start.17 = (f32[256,128]{0,1:T(8,128)S(1)}, f32[256,128]{0,1:T(8,128)S(1)}, u32[]{:S(2)}, u32[]{:S(2)}) collective-permute-start(f32[256,128]{0,1:T(8,128)S(1)} %add.595), channel_id=1, source_target_pairs={{0,2},{1,3},{2,0},{3,1},{4,6},{5,7},{6,4},{7,5},{8,10},{9,11},{10,... | collective-permute-start | bytes 393224 | tf_op jit(solution)/shard_map/ppermute | solution.py:26
  93.3 5.0 %collective-permute-start.20 = (f32[256,128]{0,1:T(8,128)S(1)}, f32[256,128]{0,1:T(8,128)S(1)}, u32[]{:S(2)}, u32[]{:S(2)}) collective-permute-start(f32[256,128]{0,1:T(8,128)S(1)} %add.602), channel_id=1, source_target_pairs={{0,2},{1,3},{2,0},{3,1},{4,6},{5,7},{6,4},{7,5},{8,10},{9,11},{10,... | collective-permute-start | bytes 393224 | tf_op jit(solution)/shard_map/ppermute | solution.py:26
  95.3 34.5 %collective-permute-start.42 = (bf16[128,2048]{1,0:T(8,128)(2,1)}, bf16[128,2048]{1,0:T(8,128)(2,1)S(1)}, u32[]{:S(2)}, u32[]{:S(2)}) collective-permute-start(bf16[128,2048]{1,0:T(8,128)(2,1)} %collective-permute-done.18), channel_id=1, source_target_pairs={{4,8},{8,4},{5,9},{9,5},{6,10},{10,6},{7,11},{11,7},{20,24},{24,20... | collective-permute-start | bytes 1572872 | tf_op jit(solution)/shard_map/ppermute | solution.py:38
  98.3 20.1 %collective-permute-start.26 = (bf16[128,2048]{1,0:T(8,128)(2,1)S(1)}, bf16[128,2048]{1,0:T(8,128)(2,1)S(1)}, u32[]{:S(2)}, u32[]{:S(2)}) collective-permute-start(bf16[128,2048]{1,0:T(8,128)(2,1)S(1)} %collective-permute-done.25), channel_id=1, source_target_pairs={{4,0},{8,12},{5,1},{9,13},{6,2},{10,14},{7,3},{11,15},{20,16},{24,... | collective-permute-start | bytes 1572872 | tf_op jit(solution)/shard_map/ppermute | solution.py:38
  101.1 22.9 %collective-permute-start.46 = (bf16[128,2048]{1,0:T(8,128)(2,1)}, bf16[128,2048]{1,0:T(8,128)(2,1)S(1)}, u32[]{:S(2)}, u32[]{:S(2)}) collective-permute-start(bf16[128,2048]{1,0:T(8,128)(2,1)} %collective-permute-done.12), channel_id=1, source_target_pairs={{0,4},{4,0},{8,12},{12,8},{1,5},{5,1},{9,13},{13,9},{2,6},{6,2},{1... | collective-permute-start | bytes 1572872 | tf_op jit(solution)/shard_map/ppermute | solution.py:38
  118.3 7.1 %collective-permute-start.3 = (f32[256,128]{0,1:T(8,128)S(1)}, f32[256,128]{0,1:T(8,128)S(1)}, u32[]{:S(2)}, u32[]{:S(2)}) collective-permute-start(f32[256,128]{0,1:T(8,128)S(1)} %add.568), channel_id=1, source_target_pairs={{0,2},{1,3},{2,0},{3,1},{4,6},{5,7},{6,4},{7,5},{8,10},{9,11},{10,... | collective-permute-start | bytes 393224 | tf_op jit(solution)/shard_map/ppermute | solution.py:26
  120.3 5.6 %collective-permute-start.23 = (f32[256,128]{0,1:T(8,128)S(1)}, f32[256,128]{0,1:T(8,128)S(1)}, u32[]{:S(2)}, u32[]{:S(2)}) collective-permute-start(f32[256,128]{0,1:T(8,128)S(1)} %fusion.115), channel_id=1, source_target_pairs={{0,1},{1,0},{2,3},{3,2},{4,5},{5,4},{6,7},{7,6},{8,9},{9,8},{10,11... | collective-permute-start | bytes 393224 | tf_op jit(solution)/shard_map/ppermute | solution.py:26
  125.5 5.6 %collective-permute-start.47 = (f32[256,128]{0,1:T(8,128)S(1)}, f32[256,128]{0,1:T(8,128)S(1)}, u32[]{:S(2)}, u32[]{:S(2)}) collective-permute-start(f32[256,128]{0,1:T(8,128)S(1)} %fusion.122), channel_id=1, source_target_pairs={{0,1},{1,0},{2,3},{3,2},{4,5},{5,4},{6,7},{7,6},{8,9},{9,8},{10,11... | collective-permute-start | bytes 393224 | tf_op jit(solution)/shard_map/ppermute | solution.py:26
  125.9 6.7 %collective-permute-start.28 = (f32[256,128]{0,1:T(8,128)S(1)}, f32[256,128]{0,1:T(8,128)S(1)}, u32[]{:S(2)}, u32[]{:S(2)}) collective-permute-start(f32[256,128]{0,1:T(8,128)S(1)} %add.616), channel_id=1, source_target_pairs={{0,2},{1,3},{2,0},{3,1},{4,6},{5,7},{6,4},{7,5},{8,10},{9,11},{10,... | collective-permute-start | bytes 393224 | tf_op jit(solution)/shard_map/ppermute | solution.py:26
  127.6 18.0 %collective-permute-start.32 = (bf16[128,2048]{1,0:T(8,128)(2,1)S(1)}, bf16[128,2048]{1,0:T(8,128)(2,1)S(1)}, u32[]{:S(2)}, u32[]{:S(2)}) collective-permute-start(bf16[128,2048]{1,0:T(8,128)(2,1)S(1)} %broadcast_select_fusion.3), channel_id=1, source_target_pairs={{0,16},{16,0},{1,17},{17,1},{2,18},{18,2},{3,19},{19,3},{4,20},{20... | collective-permute-start | bytes 1572872 | tf_op jit(solution)/shard_map/ppermute | solution.py:42
  129.2 27.5 %collective-permute-start.35 = (bf16[128,2048]{1,0:T(8,128)(2,1)S(1)}, bf16[128,2048]{1,0:T(8,128)(2,1)S(1)}, u32[]{:S(2)}, u32[]{:S(2)}) collective-permute-start(bf16[128,2048]{1,0:T(8,128)(2,1)S(1)} %broadcast_select_fusion.2), channel_id=1, source_target_pairs={{0,16},{16,0},{1,17},{17,1},{2,18},{18,2},{3,19},{19,3},{4,20},{20... | collective-permute-start | bytes 1572872 | tf_op jit(solution)/shard_map/ppermute | solution.py:42
  129.8 16.7 %collective-permute-start.39 = (bf16[128,2048]{1,0:T(8,128)(2,1)S(1)}, bf16[128,2048]{1,0:T(8,128)(2,1)S(1)}, u32[]{:S(2)}, u32[]{:S(2)}) collective-permute-start(bf16[128,2048]{1,0:T(8,128)(2,1)S(1)} %collective-permute-done.38), channel_id=1, source_target_pairs={{4,0},{8,12},{5,1},{9,13},{6,2},{10,14},{7,3},{11,15},{20,16},{24,... | collective-permute-start | bytes 1572872 | tf_op jit(solution)/shard_map/ppermute | solution.py:38
  131.1 25.0 %collective-permute-start.43 = (bf16[128,2048]{1,0:T(8,128)(2,1)S(1)}, bf16[128,2048]{1,0:T(8,128)(2,1)S(1)}, u32[]{:S(2)}, u32[]{:S(2)}) collective-permute-start(bf16[128,2048]{1,0:T(8,128)(2,1)S(1)} %collective-permute-done.42), channel_id=1, source_target_pairs={{4,0},{8,12},{5,1},{9,13},{6,2},{10,14},{7,3},{11,15},{20,16},{24,... | collective-permute-start | bytes 1572872 | tf_op jit(solution)/shard_map/ppermute | solution.py:38
  132.6 5.0 %collective-permute-start.31 = (f32[256,128]{0,1:T(8,128)S(1)}, f32[256,128]{0,1:T(8,128)S(1)}, u32[]{:S(2)}, u32[]{:S(2)}) collective-permute-start(f32[256,128]{0,1:T(8,128)S(1)} %add.623), channel_id=1, source_target_pairs={{0,2},{1,3},{2,0},{3,1},{4,6},{5,7},{6,4},{7,5},{8,10},{9,11},{10,... | collective-permute-start | bytes 393224 | tf_op jit(solution)/shard_map/ppermute | solution.py:26
  137.7 5.0 %collective-permute-start.48 = (f32[256,128]{0,1:T(8,128)S(1)}, f32[256,128]{0,1:T(8,128)S(1)}, u32[]{:S(2)}, u32[]{:S(2)}) collective-permute-start(f32[256,128]{0,1:T(8,128)S(1)} %add.658), channel_id=1, source_target_pairs={{0,2},{1,3},{2,0},{3,1},{4,6},{5,7},{6,4},{7,5},{8,10},{9,11},{10,... | collective-permute-start | bytes 393224 | tf_op jit(solution)/shard_map/ppermute | solution.py:26
  142.6 16.4 %collective-permute-start.24 = (f32[256,128]{0,1:T(8,128)S(1)}, f32[256,128]{0,1:T(8,128)S(1)}, u32[]{:S(2)}, u32[]{:S(2)}) collective-permute-start(f32[256,128]{0,1:T(8,128)S(1)} %add.609), channel_id=1, source_target_pairs={{0,2},{1,3},{2,0},{3,1},{4,6},{5,7},{6,4},{7,5},{8,10},{9,11},{10,... | collective-permute-start | bytes 393224 | tf_op jit(solution)/shard_map/ppermute | solution.py:26
  146.1 11.7 %collective-permute-start.33 = (f32[256,128]{0,1:T(8,128)S(1)}, f32[256,128]{0,1:T(8,128)S(1)}, u32[]{:S(2)}, u32[]{:S(2)}) collective-permute-start(f32[256,128]{0,1:T(8,128)S(1)} %fusion.118), channel_id=1, source_target_pairs={{0,1},{1,0},{2,3},{3,2},{4,5},{5,4},{6,7},{7,6},{8,9},{9,8},{10,11... | collective-permute-start | bytes 393224 | tf_op jit(solution)/shard_map/ppermute | solution.py:26
  147.2 13.5 %collective-permute-start.40 = (f32[256,128]{0,1:T(8,128)S(1)}, f32[256,128]{0,1:T(8,128)S(1)}, u32[]{:S(2)}, u32[]{:S(2)}) collective-permute-start(f32[256,128]{0,1:T(8,128)S(1)} %fusion.120), channel_id=1, source_target_pairs={{0,1},{1,0},{2,3},{3,2},{4,5},{5,4},{6,7},{7,6},{8,9},{9,8},{10,11... | collective-permute-start | bytes 393224 | tf_op jit(solution)/shard_map/ppermute | solution.py:26
  156.6 4.7 %collective-permute-start.44 = (f32[256,128]{0,1:T(8,128)S(1)}, f32[256,128]{0,1:T(8,128)S(1)}, u32[]{:S(2)}, u32[]{:S(2)}) collective-permute-start(f32[256,128]{0,1:T(8,128)S(1)} %fusion.121), channel_id=1, source_target_pairs={{0,1},{1,0},{2,3},{3,2},{4,5},{5,4},{6,7},{7,6},{8,9},{9,8},{10,11... | collective-permute-start | bytes 393224 | tf_op jit(solution)/shard_map/ppermute | solution.py:26
  157.2 5.0 %collective-permute-start.36 = (f32[256,128]{0,1:T(8,128)S(1)}, f32[256,128]{0,1:T(8,128)S(1)}, u32[]{:S(2)}, u32[]{:S(2)}) collective-permute-start(f32[256,128]{0,1:T(8,128)S(1)} %fusion.119), channel_id=1, source_target_pairs={{0,1},{1,0},{2,3},{3,2},{4,5},{5,4},{6,7},{7,6},{8,9},{9,8},{10,11... | collective-permute-start | bytes 393224 | tf_op jit(solution)/shard_map/ppermute | solution.py:26
  157.8 5.7 %collective-permute-start.34 = (f32[256,128]{0,1:T(8,128)S(1)}, f32[256,128]{0,1:T(8,128)S(1)}, u32[]{:S(2)}, u32[]{:S(2)}) collective-permute-start(f32[256,128]{0,1:T(8,128)S(1)} %add.630), channel_id=1, source_target_pairs={{0,2},{1,3},{2,0},{3,1},{4,6},{5,7},{6,4},{7,5},{8,10},{9,11},{10,... | collective-permute-start | bytes 393224 | tf_op jit(solution)/shard_map/ppermute | solution.py:26
  159.2 17.1 %collective-permute-start.49 = (bf16[128,2048]{1,0:T(8,128)(2,1)S(1)}, bf16[128,2048]{1,0:T(8,128)(2,1)S(1)}, u32[]{:S(2)}, u32[]{:S(2)}) collective-permute-start(bf16[128,2048]{1,0:T(8,128)(2,1)S(1)} %broadcast_select_fusion.1), channel_id=1, source_target_pairs={{0,16},{16,0},{1,17},{17,1},{2,18},{18,2},{3,19},{19,3},{4,20},{20... | collective-permute-start | bytes 1572872 | tf_op jit(solution)/shard_map/ppermute | solution.py:42
  160.6 23.4 %collective-permute-start.52 = (bf16[128,2048]{1,0:T(8,128)(2,1)S(1)}, bf16[128,2048]{1,0:T(8,128)(2,1)S(1)}, u32[]{:S(2)}, u32[]{:S(2)}) collective-permute-start(bf16[128,2048]{1,0:T(8,128)(2,1)S(1)} %broadcast_select_fusion), channel_id=1, source_target_pairs={{0,16},{16,0},{1,17},{17,1},{2,18},{18,2},{3,19},{19,3},{4,20},{20... | collective-permute-start | bytes 1572872 | tf_op jit(solution)/shard_map/ppermute | solution.py:42
  161.3 25.7 %collective-permute-start.41 = (f32[256,128]{0,1:T(8,128)S(1)}, f32[256,128]{0,1:T(8,128)S(1)}, u32[]{:S(2)}, u32[]{:S(2)}) collective-permute-start(f32[256,128]{0,1:T(8,128)S(1)} %add.644), channel_id=1, source_target_pairs={{0,2},{1,3},{2,0},{3,1},{4,6},{5,7},{6,4},{7,5},{8,10},{9,11},{10,... | collective-permute-start | bytes 393224 | tf_op jit(solution)/shard_map/ppermute | solution.py:26
  162.3 12.1 %collective-permute-start.45 = (f32[256,128]{0,1:T(8,128)S(1)}, f32[256,128]{0,1:T(8,128)S(1)}, u32[]{:S(2)}, u32[]{:S(2)}) collective-permute-start(f32[256,128]{0,1:T(8,128)S(1)} %add.651), channel_id=1, source_target_pairs={{0,2},{1,3},{2,0},{3,1},{4,6},{5,7},{6,4},{7,5},{8,10},{9,11},{10,... | collective-permute-start | bytes 393224 | tf_op jit(solution)/shard_map/ppermute | solution.py:26
  163.5 8.2 %collective-permute-start.37 = (f32[256,128]{0,1:T(8,128)S(1)}, f32[256,128]{0,1:T(8,128)S(1)}, u32[]{:S(2)}, u32[]{:S(2)}) collective-permute-start(f32[256,128]{0,1:T(8,128)S(1)} %add.637), channel_id=1, source_target_pairs={{0,2},{1,3},{2,0},{3,1},{4,6},{5,7},{6,4},{7,5},{8,10},{9,11},{10,... | collective-permute-start | bytes 393224 | tf_op jit(solution)/shard_map/ppermute | solution.py:26
  176.8 8.0 %collective-permute-start.50 = (f32[256,128]{0,1:T(8,128)S(1)}, f32[256,128]{0,1:T(8,128)S(1)}, u32[]{:S(2)}, u32[]{:S(2)}) collective-permute-start(f32[256,128]{0,1:T(8,128)S(1)} %fusion.123), channel_id=1, source_target_pairs={{0,1},{1,0},{2,3},{3,2},{4,5},{5,4},{6,7},{7,6},{8,9},{9,8},{10,11... | collective-permute-start | bytes 393224 | tf_op jit(solution)/shard_map/ppermute | solution.py:26
  184.8 6.4 %collective-permute-start.51 = (f32[256,128]{0,1:T(8,128)S(1)}, f32[256,128]{0,1:T(8,128)S(1)}, u32[]{:S(2)}, u32[]{:S(2)}) collective-permute-start(f32[256,128]{0,1:T(8,128)S(1)} %add.665), channel_id=1, source_target_pairs={{0,2},{1,3},{2,0},{3,1},{4,6},{5,7},{6,4},{7,5},{8,10},{9,11},{10,... | collective-permute-start | bytes 393224 | tf_op jit(solution)/shard_map/ppermute | solution.py:26
  186.0 7.6 %collective-permute-start.54 = (f32[256,128]{0,1:T(8,128)S(1)}, f32[256,128]{0,1:T(8,128)S(1)}, u32[]{:S(2)}, u32[]{:S(2)}) collective-permute-start(f32[256,128]{0,1:T(8,128)S(1)} %add.672), channel_id=1, source_target_pairs={{0,2},{1,3},{2,0},{3,1},{4,6},{5,7},{6,4},{7,5},{8,10},{9,11},{10,... | collective-permute-start | bytes 393224 | tf_op jit(solution)/shard_map/ppermute | solution.py:26
  (26 other events, 262.0 us)

commit v2 on v0

v2 whole, which is shorter than its diff:
```python
import functools

import jax
import jax.numpy as jnp
from jax import lax
from jax.experimental import pallas as pl
from jax.experimental.pallas import tpu as pltpu
from jax.sharding import PartitionSpec as P

EPSILON = 1e-05

HOLDERS = ("section", "wide")
LANES = 128
COLUMNS = 512
SMALL_COST = pl.CostEstimate(flops=1000, bytes_accessed=1000, transcendentals=0)


def contract_last(left, right):
    return lax.dot_general(
        left, right, (((1,), (1,)), ((), ())), preferred_element_type=jnp.float32
    )


def dot(left, right):
    return jnp.dot(left, right, preferred_element_type=jnp.float32)


def local_kernel(body, out_shape, mebibytes=8, **kwargs):
    return pl.pallas_call(
        body,
        out_shape=out_shape,
        compiler_params=pltpu.CompilerParams(vmem_limit_bytes=mebibytes * 1024 * 1024),
        cost_estimate=SMALL_COST,
        **kwargs,
    )


def anywhere(count):
    return [pl.BlockSpec(memory_space=pl.ANY)] * count


def gate(values, after):
    count = len(values)
    return pl.pallas_call(
        lambda *refs: None,
        out_shape=[jax.ShapeDtypeStruct(v.shape, v.dtype) for v in values],
        in_specs=anywhere(count + len(after)),
        out_specs=anywhere(count),
        input_output_aliases={i: i for i in range(count)},
        cost_estimate=SMALL_COST,
    )(*values, *after)


def in_vmem(count):
    return [pl.BlockSpec(memory_space=pltpu.VMEM)] * count


def slots_body(slot_count, shard_row, token_row, target, _, sent):
    tokens, width = target.shape
    slots = sent.shape[0]
    shard_here = shard_row[...]
    earlier = lax.broadcasted_iota(jnp.int32, (tokens, tokens), 0) < lax.broadcasted_iota(
        jnp.int32, (tokens, tokens), 1
    )
    shard_column = jnp.broadcast_to(shard_here.astype(jnp.float32), (tokens, tokens)).T
    same = (shard_column.astype(jnp.int32) == shard_here) & earlier
    rank = jnp.sum(jnp.where(same, 1.0, 0.0), axis=0, keepdims=True).astype(jnp.int32)
    position = shard_here * slot_count + rank
    here = lax.broadcasted_iota(jnp.int32, (slots, tokens), 0) == position
    to_slot = jnp.where(here, 1.0, 0.0)
    sent[:, :width] = dot(to_slot.astype(jnp.bfloat16), target[...]).astype(jnp.bfloat16)
    row = token_row[...]
    high = jnp.sum(to_slot * (row >> 8).astype(jnp.float32), axis=1, keepdims=True)
    low = jnp.sum(to_slot * (row & 255).astype(jnp.float32), axis=1, keepdims=True)
    taken = jnp.sum(to_slot, axis=1, keepdims=True)
    lane = lax.broadcasted_iota(jnp.int32, (slots, LANES), 1)
    numbers = jnp.where(
        lane == 0, high, jnp.where(lane == 1, low, jnp.where(lane == 2, taken, 0.0))
    )
    sent[:, width:] = numbers.astype(jnp.bfloat16)


def pick_body(arrived, table, hidden, squares, target, place, rows_buffer, copied):
    vocab_rows, width = table.shape
    target_width = target.shape[0] * LANES
    parts = [slice(at, at + COLUMNS) for at in range(0, width, COLUMNS)]
    copies = [
        pltpu.make_async_copy(table.at[:, part], rows_buffer.at[:, part], copied.at[i])
        for i, part in enumerate(parts)
    ]
    for copy in copies:
        copy.start()
    here = arrived[...]
    slots = here.shape[0]
    numbers = here[:, target_width:].astype(jnp.float32)
    row = jnp.where(numbers[:, 2:3] > 0.5, numbers[:, 0:1] * 256.0 + numbers[:, 1:2], -1.0)
    picks = jnp.where(
        row.astype(jnp.int32) == lax.broadcasted_iota(jnp.int32, (slots, vocab_rows), 1), 1.0, 0.0
    )
    place[...] = picks.T.astype(jnp.bfloat16)
    picks = picks.astype(jnp.bfloat16)
    for i in range(target.shape[0]):
        target[i] = here[:, i * LANES : (i + 1) * LANES]
    total = jnp.zeros((slots, LANES), jnp.float32)
    for copy, part in zip(copies, parts):
        copy.wait()
        rows = dot(picks, rows_buffer[:, part])
        hidden[:, part] = rows.astype(jnp.bfloat16)
        for lane in range(0, COLUMNS, LANES):
            value = rows[:, lane : lane + LANES]
            total += value * value
    squares[...] = total


def norm_body(width, hidden, gain, squares, others, normed, scale):
    mean_square = jnp.sum(squares[...] + others[...], axis=1, keepdims=True) / width
    row_scale = lax.rsqrt(mean_square + EPSILON)
    scale[...] = jnp.broadcast_to(row_scale, scale.shape)
    for at in range(0, hidden.shape[1], COLUMNS):
        columns = slice(at, at + COLUMNS)
        rows = hidden[:, columns].astype(jnp.float32)
        normed[:, columns] = (rows * row_scale * gain[:, columns]).astype(jnp.bfloat16)


def start_pieces(pieces, buffer, copied):
    copies = []
    for i, piece in enumerate(pieces):
        there = buffer.at[pl.ds(i * LANES, LANES)]
        copies.append(pltpu.make_async_copy(piece, there, copied.at[i]))
        copies[-1].start()
    return copies


def forward_body(count, normed, *refs):
    pieces, (out, rows_buffer, buffer, copied) = refs[:count], refs[count:]
    rows = pltpu.make_async_copy(normed, rows_buffer, copied.at[count])
    rows.start()
    copies = start_pieces(pieces, buffer, copied)
    rows.wait()
    for i in range(0, count, 2):
        for copy in copies[i : i + 2]:
            copy.wait()
        part = slice(i * LANES, min(i + 2, count) * LANES)
        out[:, part] = contract_last(rows_buffer[...], buffer[part])


def target_at(places, i, targets):
    distance, block = places[0, i], places[1, i]
    value = targets[0][block].astype(jnp.float32)
    for d in range(1, len(targets)):
        value = jnp.where(distance == d, targets[d][block].astype(jnp.float32), value)
    return value


def residual_of(places, first, projected, others, targets, inner, residual):
    for i in range(projected.shape[1] // LANES):
        lanes = slice(i * LANES, (i + 1) * LANES)
        value = projected[:, lanes].astype(jnp.float32) + others[:, lanes].astype(jnp.float32)
        rounded = (value - target_at(places, first + i, targets)).astype(jnp.bfloat16)
        residual[:, (first + i) * LANES : (first + i + 1) * LANES] = rounded
        inner = inner + rounded.astype(jnp.float32) * value
    return inner


def residuals_of(places, summed, targets, inner, residual):
    first = 0
    for projected, others in zip(summed[::2], summed[1::2]):
        inner = residual_of(places, first, projected, others, targets, inner, residual)
        first += projected.shape[1] // LANES
    return inner


def back_body(count, sums, narrow, before, places, *refs):
    pieces, refs = refs[:count], refs[count:]
    summed, refs = refs[: 2 * sums], refs[2 * sums :]
    targets, refs = refs[:narrow], refs[narrow:]
    if before:
        back_in, inner_in, refs = refs[0], refs[1], refs[2:]
    back_out, inner_out, residual, buffer, copied = refs
    copies = start_pieces(pieces, buffer, copied)
    inner = inner_in[...] if before else jnp.zeros(inner_out.shape, jnp.float32)
    inner_out[...] = residuals_of(places, summed, targets, inner, residual)
    for copy in copies:
        copy.wait()
    for at in range(0, back_out.shape[1], COLUMNS):
        part = slice(at, at + COLUMNS)
        value = dot(residual[...], buffer[:, part])
        back_out[:, part] = value + back_in[:, part] if before else value


def tail_body(count, sums, narrow, width, places, *refs):
    pieces, refs = refs[:count], refs[count:]
    summed, refs = refs[: 2 * sums], refs[2 * sums :]
    targets, refs = refs[:narrow], refs[narrow:]
    back_in, inner_in, hidden, gain, scale, place, table_grad, residual, factor = refs

    @pl.when(pl.program_id(0) == 0)
    def _():
        inner = residuals_of(places, summed, targets, inner_in[...], residual)
        inner = jnp.sum(inner, axis=1, keepdims=True)
        factor[...] = scale[...] * scale[...] * (inner / width)

    back = back_in[...]
    for i, piece in enumerate(pieces):
        back += dot(residual[:, i * LANES : (i + 1) * LANES], piece[...])
    row_grad = scale[:, :1] * (back * gain[...]) - hidden[...].astype(jnp.float32) * factor[:, :1]
    table_grad[...] = dot(place[...], row_grad.astype(jnp.bfloat16)).astype(jnp.bfloat16)


def whole_block(shape):
    return pl.BlockSpec(shape, lambda i, *_: (0,) * len(shape))


def column_block(rows):
    return pl.BlockSpec((rows, COLUMNS), lambda i, *_: (0, i))


def exchange_narrow(value, distance):
    narrow = lax.axis_size("narrow")
    return lax.ppermute(value, "narrow", [(i, i ^ distance) for i in range(narrow)])


class Device:
    def __init__(self, token_shard, token_row, table, gain, kv_target):
        self.tokens = (token_shard, token_row, kv_target)
        self.table = table
        self.gain = gain.reshape(1, table.shape[1])
        self.owners = lax.axis_size(HOLDERS)
        self.slot_count = 2 * kv_target.shape[0] // self.owners
        self.slots = self.owners * self.slot_count
        self.blocks = kv_target.shape[1] // LANES
        self.width_all = table.shape[1] * lax.axis_size("narrow")
        self.before = ()

    def ask(self, after):
        token_shard, token_row, target = self.tokens
        tokens, width = target.shape
        sent = local_kernel(
            functools.partial(slots_body, self.slot_count),
            jax.ShapeDtypeStruct((self.slots, width + LANES), jnp.bfloat16),
            in_specs=in_vmem(3) + anywhere(1),
        )(token_shard.reshape(1, tokens), token_row.reshape(1, tokens), target, after)
        self.arrived = lax.all_to_all(
            sent.reshape(self.owners, self.slot_count, width + LANES),
            HOLDERS,
            split_axis=0,
            concat_axis=0,
            tiled=True,
        ).reshape(self.slots, width + LANES)
        return self.arrived

    def pick(self):
        vocab_rows, width = self.table.shape
        self.hidden, squares, self.target, self.place = local_kernel(
            pick_body,
            (
                jax.ShapeDtypeStruct((self.slots, width), jnp.bfloat16),
                jax.ShapeDtypeStruct((self.slots, LANES), jnp.float32),
                jax.ShapeDtypeStruct((self.blocks, self.slots, LANES), jnp.bfloat16),
                jax.ShapeDtypeStruct((vocab_rows, self.slots), jnp.bfloat16),
            ),
            mebibytes=12,
            in_specs=in_vmem(1) + anywhere(1),
            scratch_shapes=[
                pltpu.VMEM((vocab_rows, width), jnp.bfloat16),
                pltpu.SemaphoreType.DMA((width // COLUMNS,)),
            ],
        )(self.arrived, self.table)
        return squares

    def norm(self, squares, others):
        self.normed, self.scale = local_kernel(
            functools.partial(norm_body, self.width_all),
            (
                jax.ShapeDtypeStruct(self.hidden.shape, jnp.bfloat16),
                jax.ShapeDtypeStruct((self.slots, LANES), jnp.float32),
            ),
        )(self.hidden, self.gain, squares, others)

    def share_targets(self):
        others = [exchange_narrow(self.target, d) for d in range(1, lax.axis_size("narrow"))]
        self.targets = [self.target] + others

    def forward(self, group):
        count = len(group)
        slots, width = self.normed.shape
        return local_kernel(
            functools.partial(forward_body, count),
            jax.ShapeDtypeStruct((slots, count * LANES), jnp.float32),
            in_specs=anywhere(1 + count),
            scratch_shapes=[
                pltpu.VMEM((slots, width), jnp.bfloat16),
                pltpu.VMEM((count * LANES, width), jnp.bfloat16),
                pltpu.SemaphoreType.DMA((count + 1,)),
            ],
        )(self.normed, *[piece for _, piece in group])

    def places(self, group):
        at = jnp.stack([which for which, _ in group])
        distance = (at // self.blocks) ^ lax.axis_index("narrow")
        return jnp.stack([distance, at % self.blocks])

    def back(self, group, *summed):
        slots, width = self.normed.shape
        count, narrow = len(group), len(self.targets)
        self.before = local_kernel(
            functools.partial(back_body, count, len(summed) // 2, narrow, len(self.before) > 0),
            (
                jax.ShapeDtypeStruct((slots, width), jnp.float32),
                jax.ShapeDtypeStruct((slots, LANES), jnp.float32),
            ),
            mebibytes=16,
            in_specs=[pl.BlockSpec(memory_space=pltpu.SMEM)]
            + anywhere(count)
            + in_vmem(len(summed) + narrow + len(self.before)),
            scratch_shapes=[
                pltpu.VMEM((slots, count * LANES), jnp.bfloat16),
                pltpu.VMEM((count * LANES, width), jnp.bfloat16),
                pltpu.SemaphoreType.DMA((count,)),
            ],
        )(
            self.places(group),
            *[piece for _, piece in group],
            *summed,
            *self.targets,
            *self.before,
        )
        return self.before[1]

    def tail(self, group, *summed):
        slots, width = self.normed.shape
        vocab_rows = self.place.shape[0]
        count, narrow = len(group), len(self.targets)
        lanes = whole_block((slots, LANES))
        return local_kernel(
            functools.partial(tail_body, count, len(summed) // 2, narrow, self.width_all),
            jax.ShapeDtypeStruct((vocab_rows, width), jnp.bfloat16),
            mebibytes=16,
            grid_spec=pltpu.PrefetchScalarGridSpec(
                num_scalar_prefetch=1,
                grid=(width // COLUMNS,),
                in_specs=[column_block(LANES)] * count
                + [whole_block(value.shape) for value in summed]
                + [whole_block(self.target.shape)] * narrow
                + [column_block(slots), lanes, column_block(slots), column_block(1), lanes]
                + [whole_block(self.place.shape)],
                out_specs=column_block(vocab_rows),
                scratch_shapes=[
                    pltpu.VMEM((slots, count * LANES), jnp.bfloat16),
                    pltpu.VMEM((slots, LANES), jnp.float32),
                ],
            ),
        )(
            self.places(group),
            *[piece for _, piece in group],
            *summed,
            *self.targets,
            *self.before,
            self.hidden,
            self.gain,
            self.scale,
            self.place,
        )


SUM_TYPE = jnp.bfloat16


def sum_of_cores(value):
    return (value + exchange_narrow(value, 1)).astype(SUM_TYPE)


def plain_order(device, weight):
    device.ask(weight)
    squares = device.pick()
    squares += exchange_narrow(squares, 1)
    device.norm(squares, exchange_narrow(squares, 2))
    device.share_targets()
    whole = lax.all_gather(weight, HOLDERS, axis=0, tiled=True)
    pieces = [
        (jnp.int32(at // LANES), whole[at : at + LANES]) for at in range(0, whole.shape[0], LANES)
    ]
    groups = [pieces[i : i + 4] for i in range(0, len(pieces), 4)]
    for number, group in enumerate(groups):
        half = sum_of_cores(device.forward(group))
        step = device.back if number < len(groups) - 1 else device.tail
        result = step(group, half, exchange_narrow(half, 2))
    return result


def ring_order(device, weight):
    section, wide = lax.axis_index("section"), lax.axis_index("wide")
    holders = lax.axis_size(HOLDERS)
    at_ring = [i if i < holders // 2 else holders + holders // 2 - 1 - i for i in range(holders)]
    ring = jnp.where(section == 0, wide, holders - 1 - wide)

    def send(value, step):
        pairs = [(at_ring[i], at_ring[(i + step) % holders]) for i in range(holders)]
        return lax.ppermute(value, HOLDERS, pairs)

    def named(distance, half, piece):
        at = (ring + distance) % holders
        holder = jnp.where(at < holders // 2, at, holders + holders // 2 - 1 - at)
        return 2 * holder + half, piece

    w0, w1 = weight[:LANES], weight[LANES:]
    own = [named(0, 0, w0), named(0, 1, w1)]
    up0, down1 = send(w0, 1), send(w1, -1)
    up1, down0 = send(w1, 1), send(w0, -1)

    up0, down1 = gate([up0, down1], [])
    near = [named(-1, 0, up0), named(1, 1, down1)]
    up0, down1 = send(up0, 1), send(down1, -1)
    device.ask(near[0][1])

    up1, down0 = gate([up1, down0], [])
    near += [named(-1, 1, up1), named(1, 0, down0)]
    up1, down0 = send(up1, 1), send(down0, -1)
    squares = device.pick()
    squares += exchange_narrow(squares, 1)
    squares_other = exchange_narrow(squares, 2)

    up0, down1 = gate([up0, down1], [squares])
    second = [named(-2, 0, up0), named(2, 1, down1)]
    up0, down1 = send(up0, 1), send(down1, -1)
    device.norm(squares, squares_other)
    group0 = own + near
    sum0 = device.forward(group0)
    device.share_targets()

    up1, down0 = gate([up1, down0], [sum0])
    second += [named(-2, 1, up1), named(2, 0, down0)]
    up1, down0 = send(up1, 1), send(down0, -1)
    half0 = sum_of_cores(sum0)
    other0 = exchange_narrow(half0, 2)
    sum1 = device.forward(second)

    up0, down1 = gate([up0, down1], [sum1, half0])
    third = [named(-3, 0, up0), named(3, 1, down1)]
    up0, down1 = send(up0, 1), send(down1, -1)
    half1 = sum_of_cores(sum1)
    other1 = exchange_narrow(half1, 2)

    up1, down0 = gate([up1, down0], [half1])
    third += [named(-3, 1, up1), named(3, 0, down0)]
    sum2 = device.forward(third)
    half2 = sum_of_cores(sum2)
    other2 = exchange_narrow(half2, 2)
    done = device.back(group0 + second, half0, other0, half1, other1)

    up0, down1 = gate([up0, down1], [done, half2])
    last = [named(4, 0, up0), named(4, 1, down1)]
    half3 = sum_of_cores(device.forward(last))
    return device.tail(third + last, half2, other2, half3, exchange_narrow(half3, 2))


def on_device(token_shard, token_row, table, gain, key_value_weight, kv_target):
    device = Device(token_shard, token_row, table, gain, kv_target)
    holders = (lax.axis_size("section"), lax.axis_size("wide"))
    if holders == (2, 4) and key_value_weight.shape[0] == 2 * LANES:
        return ring_order(device, key_value_weight)
    return plain_order(device, key_value_weight)


def solution(mesh):
    return jax.shard_map(
        on_device,
        mesh=mesh,
        in_specs=(
            P(("section", "wide"), None),
            P(("section", "wide")),
            P(("section", "wide"), "narrow"),
            P("narrow"),
            P(("section", "wide"), "narrow"),
            P(("section", "wide"), "narrow"),
        ),
        out_specs=P(("section", "wide"), "narrow"),
        check_vma=False,
    )
```

time: 257 us -> 148 us (0.58)
  waiting for transfers between devices: 167 us -> 64.2 us
  blocking collectives: 32.5 us -> 0 us
  Pallas kernels: 0 us -> 27.6 us
  starting transfers between devices: 9.12 us -> 30.1 us
  matrix products: 15.2 us -> 0 us
  between operations: 13.5 us -> 0.35 us
  local copies, waits for them, and re-layouts: 8.57 us -> 19.6 us
  other arithmetic: 10.6 us -> 5.07 us
    all_to_all x2 -> x1, waiting for transfers between devices: 74.9 us -> 4.31 us  [ask(): lax.all_to_all(sent.reshape(self.owners, self.slot_count, width + LANES),...]
    all_gather x1 -> x0, waiting for transfers between devices: 69.3 us -> none  [on_device(): lax.all_gather(key_value_weight, ('section', 'wide'), axis=0, tiled=True)]
    ppermute x0 -> x27, waiting for transfers between devices: none -> 59.9 us  [the longest x14 33.1 us: send(): return lax.ppermute(value, HOLDERS, pairs)]
    pallas_call x0 -> x16, Pallas kernels: none -> 27.6 us  [the longest x4 11.7 us: forward(): local_kernel(functools.partial(forward_body, count), jax.ShapeDtypeStruct...]
    ppermute x0 -> x27, starting transfers between devices: none -> 25.1 us  [the longest x14 15.9 us: send(): return lax.ppermute(value, HOLDERS, pairs)]
    reduce_scatter x1 -> x0, waiting for transfers between devices: 22 us -> none  [on_device(): lax.psum_scatter(partial_value, 'narrow', scatter_dimension=1, tiled=True)]
    unnamed x8 -> x62, local copies, waits for them, and re-layouts: 0.02 us -> 17.1 us
    dot_general x3 -> x0, matrix products: 15.2 us -> none  [the longest x1 7.44 us: contract_last(): lax.dot_general(left, right, (((1,), (1,)), ((), ())), preferred_element_...]
  transfers between devices with their start and end apart: 4 -> 28, of which waited for: 4 -> 12; matrix products, arithmetic and copies ran while one was open for 5% -> 4% of each run, Pallas kernels for 0% -> 13%
where the time goes in v2:
time: 148 us; the launch traced here: 147 us
  waiting for transfers between devices  64.2 us (43%)
  starting transfers between devices  30.1 us (20%)
  Pallas kernels  27.6 us (19%)
  local copies, waits for them, and re-layouts  19.6 us (13%)
  other arithmetic  5.07 us (3%)
    ppermute x14, waiting for transfers between devices, send(): return lax.ppermute(value, HOLDERS, pairs)  33.1 us
    ppermute x13, waiting for transfers between devices, exchange_narrow(): lax.ppermute(value, 'narrow', [(i, i ^ distance) for i in range(narrow)])  26.8 us
    unnamed x62, local copies, waits for them, and re-layouts  17.1 us
    ppermute x14, starting transfers between devices, send(): return lax.ppermute(value, HOLDERS, pairs)  15.9 us
    pallas_call x4, Pallas kernels, forward(): local_kernel(functools.partial(forward_body, count), jax.ShapeDtypeStruct...  11.7 us
    ppermute x13, starting transfers between devices, exchange_narrow(): lax.ppermute(value, 'narrow', [(i, i ^ distance) for i in range(narrow)])  9.26 us
    pallas_call x1, Pallas kernels, tail(): local_kernel(functools.partial(tail_body, count, len(summed) // 2, narrow...  7.39 us
    convert_element_type x4, other arithmetic, sum_of_cores(): return (value + exchange_narrow(value, 1)).astype(SUM_TYPE)  5.01 us
  transfers between devices with their start and end apart: 28, of which 12 were waited for; matrix products, arithmetic and copies ran while one was open for 4% of the time, Pallas kernels for 13%

profile of v2, /device:TPU:0, one launch (start us, length us, event | category | flops | bytes accessed | tf_op | source)
XLA Modules:
  0.0 146.9 jit_solution(1574989645138608536)
XLA Ops:
  0.0 2.3 %fusion.2 = (bf16[128,2048]{1,0:T(8,128)(2,1)}, bf16[128,2048]{1,0:T(8,128)(2,1)}) fusion(bf16[256,2048]{1,0:T(8,128)(2,1)} %param.10), kind=kLoop, calls=%fused_computation.18 | loop fusion | bytes 2097152 | tf_op jit(solution)/shard_map/slice | solution.py:406
  2.3 3.0 %collective-permute-start.1 = (bf16[128,2048]{1,0:T(8,128)(2,1)}, bf16[128,2048]{1,0:T(8,128)(2,1)S(1)}, u32[]{:S(2)}, u32[]{:S(2)}) collective-permute-start(bf16[128,2048]{1,0:T(8,128)(2,1)} %get-tuple-element.49.refs_1_), channel_id=1, source_target_pairs={{0,16},{4,0},{8,4},{12,8},{28,12},{24,28},{20,24},{16,20},{1,17},{... | collective-permute-start | bytes 1572872 | tf_op jit(solution)/shard_map/ppermute | solution.py:399
  5.4 2.0 %collective-permute-start.8 = (bf16[128,2048]{1,0:T(8,128)(2,1)}, bf16[128,2048]{1,0:T(8,128)(2,1)S(1)}, u32[]{:S(2)}, u32[]{:S(2)}) collective-permute-start(bf16[128,2048]{1,0:T(8,128)(2,1)} %get-tuple-element.49.refs_1_), channel_id=1, source_target_pairs={{0,4},{4,8},{8,12},{12,28},{28,24},{24,20},{20,16},{16,0},{1,5},{5... | collective-permute-start | bytes 1572872 | tf_op jit(solution)/shard_map/ppermute | solution.py:399
  7.4 10.9 %collective-permute-done.1.refs_1_ = bf16[128,2048]{1,0:T(8,128)(2,1)S(1)} collective-permute-done((bf16[128,2048]{1,0:T(8,128)(2,1)}, bf16[128,2048]{1,0:T(8,128)(2,1)S(1)}, u32[]{:S(2)}, u32[]{:S(2)}) %collective-permute-start.1) | collective-permute-done | bytes 524320 | tf_op jit(solution)/shard_map/ppermute | solution.py:399
  18.3 2.1 %collective-permute-done.refs_0_ = bf16[128,2048]{1,0:T(8,128)(2,1)} collective-permute-done((bf16[128,2048]{1,0:T(8,128)(2,1)}, bf16[128,2048]{1,0:T(8,128)(2,1)}, u32[]{:S(2)}, u32[]{:S(2)}) %collective-permute-start) | collective-permute-done | bytes 524320 | tf_op jit(solution)/shard_map/ppermute | solution.py:399
  20.5 1.1 shard_map.65
  21.6 5.0 %all-to-all-start = ((bf16[8,32,640]{2,1,0:T(8,128)(2,1)}), bf16[8,32,640]{2,1,0:T(8,128)(2,1)S(1)}, u32[]{:S(2)}, u32[]{:S(2)}) async-start(bf16[8,32,640]{2,1,0:T(8,128)(2,1)} %bitcast.8), calls=%async_computation | async-start | bytes 655360 | tf_op jit(solution)/shard_map/all_to_all | solution.py:243
  26.5 2.0 %collective-permute-start.2 = (bf16[128,2048]{1,0:T(8,128)(2,1)}, bf16[128,2048]{1,0:T(8,128)(2,1)S(1)}, u32[]{:S(2)}, u32[]{:S(2)}) collective-permute-start(bf16[128,2048]{1,0:T(8,128)(2,1)} %get-tuple-element.27._.refs_2_), channel_id=1, source_target_pairs={{0,4},{4,8},{8,12},{12,28},{28,24},{24,20},{20,16},{16,0},{1,5},{5... | collective-permute-start | bytes 1572872 | tf_op jit(solution)/shard_map/ppermute | solution.py:399
  28.6 3.4 %collective-permute-done.8.refs_0_ = bf16[128,2048]{1,0:T(8,128)(2,1)S(1)} collective-permute-done((bf16[128,2048]{1,0:T(8,128)(2,1)}, bf16[128,2048]{1,0:T(8,128)(2,1)S(1)}, u32[]{:S(2)}, u32[]{:S(2)}) %collective-permute-start.8) | collective-permute-done | bytes 524320 | tf_op jit(solution)/shard_map/ppermute | solution.py:399
  32.0 0.8 copy-done.4
  32.9 0.8 copy-done.6
  33.7 2.6 %collective-permute-start.10 = (bf16[128,2048]{1,0:T(8,128)(2,1)}, bf16[128,2048]{1,0:T(8,128)(2,1)}, u32[]{:S(2)}, u32[]{:S(2)}) collective-permute-start(bf16[128,2048]{1,0:T(8,128)(2,1)} %get-tuple-element.34.refs_4_), channel_id=1, source_target_pairs={{0,4},{4,8},{8,12},{12,28},{28,24},{24,20},{20,16},{16,0},{1,5},{5... | collective-permute-start | bytes 1572872 | tf_op jit(solution)/shard_map/ppermute | solution.py:399
  36.3 4.3 %all-to-all-done = bf16[8,32,640]{2,1,0:T(8,128)(2,1)S(1)} async-done(((bf16[8,32,640]{2,1,0:T(8,128)(2,1)}), bf16[8,32,640]{2,1,0:T(8,128)(2,1)S(1)}, u32[]{:S(2)}, u32[]{:S(2)}) %all-to-all-start) | async-done | bytes 327712 | tf_op jit(solution)/shard_map/all_to_all | solution.py:243
  40.6 1.6 %copy-done.19 = bf16[512,2048]{1,0:T(8,128)(2,1)S(1)} copy-done((bf16[512,2048]{1,0:T(8,128)(2,1)S(1)}, bf16[512,2048]{1,0:T(8,128)(2,1)}, u32[]{:S(2)}) %copy-start.19) | copy-done | bytes 2097176
  42.2 2.5 %shard_map.66 = (bf16[256,2048]{1,0:T(8,128)(2,1)S(1)}, f32[256,128]{1,0:T(8,128)S(1)}, bf16[4,256,128]{2,1,0:T(8,128)(2,1)}, bf16[512,256]{1,0:T(8,128)(2,1)S(1)}) custom-call(bf16[256,640]{1,0:T(8,128)(2,1)S(1)} %bitcast.21, bf16[512,2048]{1,0:T(8,128)(2,1)S(1)} %copy-done.19), custom_call_target="tpu_custom_call" | custom-call | flops 1000 | bytes 1000 | tf_op jit(solution)/shard_map/pallas_call | solution.py:254
  45.5 1.3 collective-permute-done.4
  46.9 1.6 %collective-permute-start.7 = (f32[256,128]{1,0:T(8,128)S(1)}, f32[256,128]{1,0:T(8,128)S(1)}, u32[]{:S(2)}, u32[]{:S(2)}) collective-permute-start(f32[256,128]{1,0:T(8,128)S(1)} %add.152.refs_2_.squares), channel_id=1, source_target_pairs={{0,2},{1,3},{2,0},{3,1},{4,6},{5,7},{6,4},{7,5},{8,10},{9,11},{10,... | collective-permute-start | bytes 393224 | tf_op jit(solution)/shard_map/ppermute | solution.py:220
  48.4 4.1 %collective-permute-done.7.others = f32[256,128]{1,0:T(8,128)S(1)} collective-permute-done((f32[256,128]{1,0:T(8,128)S(1)}, f32[256,128]{1,0:T(8,128)S(1)}, u32[]{:S(2)}, u32[]{:S(2)}) %collective-permute-start.7) | collective-permute-done | bytes 131104 | tf_op jit(solution)/shard_map/ppermute | solution.py:220
  53.5 1.0 copy-done.9
  54.5 4.1 %shard_map.70.refs_2_ = f32[256,768]{1,0:T(8,128)} custom-call(bf16[256,2048]{1,0:T(8,128)(2,1)S(1)} %get-tuple-element.33.normed, bf16[128,2048]{1,0:T(8,128)(2,1)} %get-tuple-element.50.refs_0_, bf16[128,2048]{1,0:T(8,128)(2,1)} %get-tuple-element.49.refs_1_, bf16[128,2048]{1,0:T(8,128)(2,1)} %get-tuple-element.27._.refs_2_, ...), custom_call_target="tpu_custom_call" | custom-call | flops 1000 | bytes 1000 | tf_op jit(solution)/shard_map/pallas_call | solution.py:287
  59.6 0.8 copy-done
  60.4 1.0 copy-done.1
  61.6 2.1 %shard_map.72.refs_2_ = f32[256,512]{1,0:T(8,128)S(1)} custom-call(bf16[256,2048]{1,0:T(8,128)(2,1)S(1)} %get-tuple-element.33.normed, bf16[128,2048]{1,0:T(8,128)(2,1)S(1)} %copy-done.1, bf16[128,2048]{1,0:T(8,128)(2,1)S(1)} %copy-done.3, bf16[128,2048]{1,0:T(8,128)(2,1)} %get-tuple-element.36.refs_2_.refs_8_, ...), custom_call_target="tpu_custom_call" | custom-call | flops 1000 | bytes 1000 | tf_op jit(solution)/shard_map/pallas_call | solution.py:287
  64.3 2.0 %collective-permute-start.14 = (bf16[128,2048]{1,0:T(8,128)(2,1)}, bf16[128,2048]{1,0:T(8,128)(2,1)}, u32[]{:S(2)}, u32[]{:S(2)}) collective-permute-start(bf16[128,2048]{1,0:T(8,128)(2,1)} %get-tuple-element.37.refs_3_.refs_9_), channel_id=1, source_target_pairs={{0,16},{4,0},{8,4},{12,8},{28,12},{24,28},{20,24},{16,20},{1,17},{... | collective-permute-start | bytes 1572872 | tf_op jit(solution)/shard_map/ppermute | solution.py:399
  66.3 2.0 %collective-permute-start.6 = (bf16[128,2048]{1,0:T(8,128)(2,1)S(1)}, bf16[128,2048]{1,0:T(8,128)(2,1)}, u32[]{:S(2)}, u32[]{:S(2)}) collective-permute-start(bf16[128,2048]{1,0:T(8,128)(2,1)S(1)} %copy-done.3), channel_id=1, source_target_pairs={{0,16},{4,0},{8,4},{12,8},{28,12},{24,28},{20,24},{16,20},{1,17},{... | collective-permute-start | bytes 1572872 | tf_op jit(solution)/shard_map/ppermute | solution.py:399
  69.1 10.3 %collective-permute-done.13.refs_0_ = bf16[128,2048]{1,0:T(8,128)(2,1)} collective-permute-done((bf16[128,2048]{1,0:T(8,128)(2,1)}, bf16[128,2048]{1,0:T(8,128)(2,1)}, u32[]{:S(2)}, u32[]{:S(2)}) %collective-permute-start.13) | collective-permute-done | bytes 524320 | tf_op jit(solution)/shard_map/ppermute | solution.py:399
  79.4 1.5 %collective-permute-start.21 = (bf16[4,256,128]{2,1,0:T(8,128)(2,1)}, bf16[4,256,128]{2,1,0:T(8,128)(2,1)}, u32[]{:S(2)}, u32[]{:S(2)}) collective-permute-start(bf16[4,256,128]{2,1,0:T(8,128)(2,1)} %get-tuple-element.42.refs_14_.refs_10_), channel_id=1, source_target_pairs={{0,2},{1,3},{2,0},{3,1},{4,6},{5,7},{6,4},{7,5},{8,10},{9,11},{10,... | collective-permute-start | bytes 786440 | tf_op jit(solution)/shard_map/ppermute | solution.py:220
  81.2 2.2 %add_convert_fusion.refs_3_.refs_10_ = bf16[256,768]{1,0:T(8,128)(2,1)} fusion(f32[256,768]{1,0:T(8,128)} %shard_map.70.refs_2_, f32[256,768]{1,0:T(8,128)} %collective-permute-done.12), kind=kLoop, calls=%fused_computation | loop fusion | flops 393216 | bytes 1966080 | tf_op jit(solution)/shard_map/convert_element_type | solution.py:370
  83.4 6.3 %collective-permute-done.5.refs_0_ = bf16[128,2048]{1,0:T(8,128)(2,1)} collective-permute-done((bf16[128,2048]{1,0:T(8,128)(2,1)S(1)}, bf16[128,2048]{1,0:T(8,128)(2,1)}, u32[]{:S(2)}, u32[]{:S(2)}) %collective-permute-start.5) | collective-permute-done | bytes 524320 | tf_op jit(solution)/shard_map/ppermute | solution.py:399
  89.8 3.6 %shard_map.76 = f32[256,512]{1,0:T(8,128)} custom-call(bf16[256,2048]{1,0:T(8,128)(2,1)S(1)} %get-tuple-element.33.normed, bf16[128,2048]{1,0:T(8,128)(2,1)} %get-tuple-element.38.refs_0_, bf16[128,2048]{1,0:T(8,128)(2,1)} %get-tuple-element.39.refs_1_, bf16[128,2048]{1,0:T(8,128)(2,1)} %get-tuple-element.40.refs_2_, bf16[128,2048]{1,0:T(8,128)(2,1)} %get-tuple-element.41.refs_3_), custom_call_target="tpu_custom_call" | custom-call | flops 1000 | bytes 1000 | tf_op jit(solution)/shard_map/pallas_call | solution.py:287
  93.5 1.6 %collective-permute-start.18 = (bf16[256,768]{1,0:T(8,128)(2,1)S(1)}, bf16[256,768]{1,0:T(8,128)(2,1)}, u32[]{:S(2)}, u32[]{:S(2)}) collective-permute-start(bf16[256,768]{1,0:T(8,128)(2,1)S(1)} %copy-done.14), channel_id=1, source_target_pairs={{0,2},{1,3},{2,0},{3,1},{4,6},{5,7},{6,4},{7,5},{8,10},{9,11},{10,... | collective-permute-start | bytes 1179656 | tf_op jit(solution)/shard_map/ppermute | solution.py:220
  96.0 1.8 %collective-permute-start.17 = (bf16[128,2048]{1,0:T(8,128)(2,1)}, bf16[128,2048]{1,0:T(8,128)(2,1)}, u32[]{:S(2)}, u32[]{:S(2)}) collective-permute-start(bf16[128,2048]{1,0:T(8,128)(2,1)} %get-tuple-element.39.refs_1_), channel_id=1, source_target_pairs={{0,16},{4,0},{8,4},{12,8},{28,12},{24,28},{20,24},{16,20},{1,17},{... | collective-permute-start | bytes 1572872 | tf_op jit(solution)/shard_map/ppermute | solution.py:399
  97.8 12.8 %collective-permute-done.19.refs_13_ = bf16[256,512]{1,0:T(8,128)(2,1)S(1)} collective-permute-done((bf16[256,512]{1,0:T(8,128)(2,1)}, bf16[256,512]{1,0:T(8,128)(2,1)S(1)}, u32[]{:S(2)}, u32[]{:S(2)}) %collective-permute-start.19) | collective-permute-done | bytes 262176 | tf_op jit(solution)/shard_map/ppermute | solution.py:220
  110.7 1.0 copy-done.10
  111.7 0.9 copy-done.15
  112.7 4.6 %shard_map.75 = (f32[256,2048]{1,0:T(8,128)S(1)}, f32[256,128]{1,0:T(8,128)S(1)}) custom-call(s32[2,10]{1,0:T(2,128)S(1)} %pad_add_fusion.1.places, bf16[128,2048]{1,0:T(8,128)(2,1)} %get-tuple-element.50.refs_0_, bf16[128,2048]{1,0:T(8,128)(2,1)} %get-tuple-element.49.refs_1_, bf16[128,2048]{1,0:T(8,128)(2,1)} %get-tuple-element.27._.refs_2_, ...), custom_call_target="tpu_custom_call" | custom-call | flops 1000 | bytes 1000 | tf_op jit(solution)/shard_map/pallas_call | solution.py:306
  117.3 1.3 copy-done.17
  119.3 2.0 %add_convert_fusion.1.refs_3_.refs_6_ = bf16[256,512]{1,0:T(8,128)(2,1)} fusion(f32[256,512]{1,0:T(8,128)} %shard_map.76, f32[256,512]{1,0:T(8,128)} %collective-permute-done.23), kind=kLoop, calls=%fused_computation.1 | loop fusion | flops 262144 | bytes 1310720 | tf_op jit(solution)/shard_map/convert_element_type | solution.py:370
  121.3 1.8 %shard_map.78 = f32[256,256]{1,0:T(8,128)S(1)} custom-call(bf16[256,2048]{1,0:T(8,128)(2,1)S(1)} %get-tuple-element.33.normed, bf16[128,2048]{1,0:T(8,128)(2,1)} %get-tuple-element.44.refs_0_.refs_4_, bf16[128,2048]{1,0:T(8,128)(2,1)} %get-tuple-element.45.refs_1_.refs_5_), custom_call_target="tpu_custom_call" | custom-call | flops 1000 | bytes 1000 | tf_op jit(solution)/shard_map/pallas_call | solution.py:287
  123.4 1.5 %collective-permute-start.24 = (bf16[256,512]{1,0:T(8,128)(2,1)S(1)}, bf16[256,512]{1,0:T(8,128)(2,1)S(1)}, u32[]{:S(2)}, u32[]{:S(2)}) collective-permute-start(bf16[256,512]{1,0:T(8,128)(2,1)S(1)} %copy-done.16), channel_id=1, source_target_pairs={{0,2},{1,3},{2,0},{3,1},{4,6},{5,7},{6,4},{7,5},{8,10},{9,11},{10,... | collective-permute-start | bytes 786440 | tf_op jit(solution)/shard_map/ppermute | solution.py:220
  124.9 1.4 collective-permute-start.26
  126.3 6.2 %collective-permute-done.24.refs_7_ = bf16[256,512]{1,0:T(8,128)(2,1)S(1)} collective-permute-done((bf16[256,512]{1,0:T(8,128)(2,1)S(1)}, bf16[256,512]{1,0:T(8,128)(2,1)S(1)}, u32[]{:S(2)}, u32[]{:S(2)}) %collective-permute-start.24) | collective-permute-done | bytes 262176 | tf_op jit(solution)/shard_map/ppermute | solution.py:220
  132.5 2.3 %collective-permute-done.26.refs_9_ = bf16[256,256]{1,0:T(8,128)(2,1)S(1)} collective-permute-done((bf16[256,256]{1,0:T(8,128)(2,1)S(1)}, bf16[256,256]{1,0:T(8,128)(2,1)S(1)}, u32[]{:S(2)}, u32[]{:S(2)}) %collective-permute-start.26) | collective-permute-done | bytes 131104 | tf_op jit(solution)/shard_map/ppermute | solution.py:220
  134.9 1.2 copy-done.13
  136.1 1.6 %copy-done.18 = f32[256,2048]{1,0:T(8,128)S(1)} copy-done((f32[256,2048]{1,0:T(8,128)S(1)}, f32[256,2048]{1,0:T(8,128)}, u32[]{:S(2)}) %copy-start.18) | copy-done | bytes 2097176
  137.7 0.9 copy-done.24
  138.6 0.9 copy-done.26
  139.5 7.4 %shard_map.79 = bf16[512,2048]{1,0:T(8,128)(2,1)} custom-call(s32[2,6]{1,0:T(2,128)S(1)} %pad_add_fusion.places, bf16[128,2048]{1,0:T(8,128)(2,1)} %get-tuple-element.38.refs_0_, bf16[128,2048]{1,0:T(8,128)(2,1)} %get-tuple-element.39.refs_1_, bf16[128,2048]{1,0:T(8,128)(2,1)} %get-tuple-element.40.refs_2_, bf16[128,2048]{1,0:T(8,128)(2,1)} %get-tuple-element.41.refs_3_, ...), custom_call_target="tpu_custom_call" | custom-call | flops 1000 | bytes 1000 | tf_op jit(solution)/shard_map/pallas_call | solution.py:335
  (98 shorter events, 6.6 us)
Async XLA Ops:
  0.0 20.5 %copy-start.27 = (bf16[128,512]{1,0:T(8,128)(2,1)S(1)}, bf16[128,512]{1,0:T(8,128)(2,1)}, u32[]{:S(2)}) copy-start(bf16[128,512]{1,0:T(8,128)(2,1)} %target.1) | copy-start | bytes 393220
  0.0 20.5 %copy-start.30 = (s32[128]{0:T(128)S(1)}, s32[128]{0:T(128)}, u32[]{:S(2)}) copy-start(s32[128]{0:T(128)} %param.7) | copy-start | bytes 1540
  0.0 20.5 %copy-start.29 = (s32[128,1]{0,1:T(1,128)S(1)}, s32[128,1]{0,1:T(1,128)}, u32[]{:S(2)}) copy-start(s32[128,1]{0,1:T(1,128)} %param.6) | copy-start | bytes 1540
  2.3 16.0 %collective-permute-start.1 = (bf16[128,2048]{1,0:T(8,128)(2,1)}, bf16[128,2048]{1,0:T(8,128)(2,1)S(1)}, u32[]{:S(2)}, u32[]{:S(2)}) collective-permute-start(bf16[128,2048]{1,0:T(8,128)(2,1)} %get-tuple-element.49.refs_1_), channel_id=1, source_target_pairs={{0,16},{4,0},{8,4},{12,8},{28,12},{24,28},{20,24},{16,20},{1,17},{... | collective-permute-start | bytes 1572872 | tf_op jit(solution)/shard_map/ppermute | solution.py:399
  5.3 15.2 %collective-permute-start = (bf16[128,2048]{1,0:T(8,128)(2,1)}, bf16[128,2048]{1,0:T(8,128)(2,1)}, u32[]{:S(2)}, u32[]{:S(2)}) collective-permute-start(bf16[128,2048]{1,0:T(8,128)(2,1)} %get-tuple-element.50.refs_0_), channel_id=1, source_target_pairs={{0,4},{4,8},{8,12},{12,28},{28,24},{24,20},{20,16},{16,0},{1,5},{5... | collective-permute-start | bytes 1572872 | tf_op jit(solution)/shard_map/ppermute | solution.py:399
  5.4 26.7 %collective-permute-start.8 = (bf16[128,2048]{1,0:T(8,128)(2,1)}, bf16[128,2048]{1,0:T(8,128)(2,1)S(1)}, u32[]{:S(2)}, u32[]{:S(2)}) collective-permute-start(bf16[128,2048]{1,0:T(8,128)(2,1)} %get-tuple-element.49.refs_1_), channel_id=1, source_target_pairs={{0,4},{4,8},{8,12},{12,28},{28,24},{24,20},{20,16},{16,0},{1,5},{5... | collective-permute-start | bytes 1572872 | tf_op jit(solution)/shard_map/ppermute | solution.py:399
  7.4 24.7 %collective-permute-start.9 = (bf16[128,2048]{1,0:T(8,128)(2,1)}, bf16[128,2048]{1,0:T(8,128)(2,1)S(1)}, u32[]{:S(2)}, u32[]{:S(2)}) collective-permute-start(bf16[128,2048]{1,0:T(8,128)(2,1)} %get-tuple-element.50.refs_0_), channel_id=1, source_target_pairs={{0,16},{4,0},{8,4},{12,8},{28,12},{24,28},{20,24},{16,20},{1,17},{... | collective-permute-start | bytes 1572872 | tf_op jit(solution)/shard_map/ppermute | solution.py:399
  18.3 2.2 %copy-start.8 = (bf16[128,2048]{1,0:T(8,128)(2,1)}, bf16[128,2048]{1,0:T(8,128)(2,1)S(1)}, u32[]{:S(2)}) copy-start(bf16[128,2048]{1,0:T(8,128)(2,1)S(1)} %collective-permute-done.1.refs_1_) | copy-start | bytes 1572868
  21.6 19.1 %all-to-all-start = ((bf16[8,32,640]{2,1,0:T(8,128)(2,1)}), bf16[8,32,640]{2,1,0:T(8,128)(2,1)S(1)}, u32[]{:S(2)}, u32[]{:S(2)}) async-start(bf16[8,32,640]{2,1,0:T(8,128)(2,1)} %bitcast.8), calls=%async_computation | async-start | bytes 655360 | tf_op jit(solution)/shard_map/all_to_all | solution.py:243
  26.5 26.0 %copy-start.28 = (f32[2048]{0:T(1024)S(1)}, f32[2048]{0:T(1024)}, u32[]{:S(2)}) copy-start(f32[2048]{0:T(1024)} %param.9) | copy-start | bytes 24580
  26.5 32.3 %collective-permute-start.2 = (bf16[128,2048]{1,0:T(8,128)(2,1)}, bf16[128,2048]{1,0:T(8,128)(2,1)S(1)}, u32[]{:S(2)}, u32[]{:S(2)}) collective-permute-start(bf16[128,2048]{1,0:T(8,128)(2,1)} %get-tuple-element.27._.refs_2_), channel_id=1, source_target_pairs={{0,4},{4,8},{8,12},{12,28},{28,24},{24,20},{20,16},{16,0},{1,5},{5... | collective-permute-start | bytes 1572872 | tf_op jit(solution)/shard_map/ppermute | solution.py:399
  28.5 30.2 %collective-permute-start.3 = (bf16[128,2048]{1,0:T(8,128)(2,1)}, bf16[128,2048]{1,0:T(8,128)(2,1)S(1)}, u32[]{:S(2)}, u32[]{:S(2)}) collective-permute-start(bf16[128,2048]{1,0:T(8,128)(2,1)} %get-tuple-element.28.refs_3_), channel_id=1, source_target_pairs={{0,16},{4,0},{8,4},{12,8},{28,12},{24,28},{20,24},{16,20},{1,17},{... | collective-permute-start | bytes 1572872 | tf_op jit(solution)/shard_map/ppermute | solution.py:399
  33.7 19.8 %copy-start.5 = (bf16[128,2048]{1,0:T(8,128)(2,1)S(1)}, bf16[128,2048]{1,0:T(8,128)(2,1)}, u32[]{:S(2)}) copy-start(bf16[128,2048]{1,0:T(8,128)(2,1)} %get-tuple-element.34.refs_4_) | copy-start | bytes 1572868
  33.7 19.8 %copy-start.7 = (bf16[128,2048]{1,0:T(8,128)(2,1)S(1)}, bf16[128,2048]{1,0:T(8,128)(2,1)}, u32[]{:S(2)}) copy-start(bf16[128,2048]{1,0:T(8,128)(2,1)} %get-tuple-element.35.refs_5_) | copy-start | bytes 1572868
  33.7 26.7 %collective-permute-start.10 = (bf16[128,2048]{1,0:T(8,128)(2,1)}, bf16[128,2048]{1,0:T(8,128)(2,1)}, u32[]{:S(2)}, u32[]{:S(2)}) collective-permute-start(bf16[128,2048]{1,0:T(8,128)(2,1)} %get-tuple-element.34.refs_4_), channel_id=1, source_target_pairs={{0,4},{4,8},{8,12},{12,28},{28,24},{24,20},{20,16},{16,0},{1,5},{5... | collective-permute-start | bytes 1572872 | tf_op jit(solution)/shard_map/ppermute | solution.py:399
  36.3 24.1 %collective-permute-start.11 = (bf16[128,2048]{1,0:T(8,128)(2,1)}, bf16[128,2048]{1,0:T(8,128)(2,1)}, u32[]{:S(2)}, u32[]{:S(2)}) collective-permute-start(bf16[128,2048]{1,0:T(8,128)(2,1)} %get-tuple-element.35.refs_5_), channel_id=1, source_target_pairs={{0,16},{4,0},{8,4},{12,8},{28,12},{24,28},{20,24},{16,20},{1,17},{... | collective-permute-start | bytes 1572872 | tf_op jit(solution)/shard_map/ppermute | solution.py:399
  40.6 1.6 %copy-start.19 = (bf16[512,2048]{1,0:T(8,128)(2,1)S(1)}, bf16[512,2048]{1,0:T(8,128)(2,1)}, u32[]{:S(2)}) copy-start(bf16[512,2048]{1,0:T(8,128)(2,1)} %table.1) | copy-start | bytes 6291460
  45.5 13.2 %copy-start.12 = (bf16[256,2048]{1,0:T(8,128)(2,1)}, bf16[256,2048]{1,0:T(8,128)(2,1)S(1)}, u32[]{:S(2)}) copy-start(bf16[256,2048]{1,0:T(8,128)(2,1)S(1)} %get-tuple-element.32.hidden.refs_16_) | copy-start | bytes 3145732
  45.5 1.3 collective-permute-start.4
  46.9 11.8 %copy-start.20 = (f32[256,128]{1,0:T(8,128)}, f32[256,128]{1,0:T(8,128)S(1)}, u32[]{:S(2)}) copy-start(f32[256,128]{1,0:T(8,128)S(1)} %add.152.refs_2_.squares) | copy-start | bytes 393220
  46.9 5.6 %collective-permute-start.7 = (f32[256,128]{1,0:T(8,128)S(1)}, f32[256,128]{1,0:T(8,128)S(1)}, u32[]{:S(2)}, u32[]{:S(2)}) collective-permute-start(f32[256,128]{1,0:T(8,128)S(1)} %add.152.refs_2_.squares), channel_id=1, source_target_pairs={{0,2},{1,3},{2,0},{3,1},{4,6},{5,7},{6,4},{7,5},{8,10},{9,11},{10,... | collective-permute-start | bytes 393224 | tf_op jit(solution)/shard_map/ppermute | solution.py:220
  53.5 1.0 copy-start.9
  58.7 22.2 %collective-permute-start.12 = (f32[256,768]{1,0:T(8,128)}, f32[256,768]{1,0:T(8,128)}, u32[]{:S(2)}, u32[]{:S(2)}) collective-permute-start(f32[256,768]{1,0:T(8,128)} %shard_map.70.refs_2_), channel_id=1, source_target_pairs={{0,1},{1,0},{2,3},{3,2},{4,5},{5,4},{6,7},{7,6},{8,9},{9,8},{10,11... | collective-permute-start | bytes 2359304 | tf_op jit(solution)/shard_map/ppermute | solution.py:220
  60.4 1.2 copy-start.3
  63.7 4.6 %copy-start.11 = (f32[256,512]{1,0:T(8,128)}, f32[256,512]{1,0:T(8,128)S(1)}, u32[]{:S(2)}) copy-start(f32[256,512]{1,0:T(8,128)S(1)} %shard_map.72.refs_2_) | copy-start | bytes 1572868
  63.7 2.6 %collective-permute-start.15 = (f32[256,512]{1,0:T(8,128)S(1)}, f32[256,512]{1,0:T(8,128)S(1)}, u32[]{:S(2)}, u32[]{:S(2)}) collective-permute-start(f32[256,512]{1,0:T(8,128)S(1)} %shard_map.72.refs_2_), channel_id=1, source_target_pairs={{0,1},{1,0},{2,3},{3,2},{4,5},{5,4},{6,7},{7,6},{8,9},{9,8},{10,11... | collective-permute-start | bytes 1572872 | tf_op jit(solution)/shard_map/ppermute | solution.py:220
  64.3 15.1 %collective-permute-start.13 = (bf16[128,2048]{1,0:T(8,128)(2,1)}, bf16[128,2048]{1,0:T(8,128)(2,1)}, u32[]{:S(2)}, u32[]{:S(2)}) collective-permute-start(bf16[128,2048]{1,0:T(8,128)(2,1)} %get-tuple-element.36.refs_2_.refs_8_), channel_id=1, source_target_pairs={{0,4},{4,8},{8,12},{12,28},{28,24},{24,20},{20,16},{16,0},{1,5},{5... | collective-permute-start | bytes 1572872 | tf_op jit(solution)/shard_map/ppermute | solution.py:399
  64.3 15.1 %collective-permute-start.14 = (bf16[128,2048]{1,0:T(8,128)(2,1)}, bf16[128,2048]{1,0:T(8,128)(2,1)}, u32[]{:S(2)}, u32[]{:S(2)}) collective-permute-start(bf16[128,2048]{1,0:T(8,128)(2,1)} %get-tuple-element.37.refs_3_.refs_9_), channel_id=1, source_target_pairs={{0,16},{4,0},{8,4},{12,8},{28,12},{24,28},{20,24},{16,20},{1,17},{... | collective-permute-start | bytes 1572872 | tf_op jit(solution)/shard_map/ppermute | solution.py:399
  66.3 23.4 %collective-permute-start.5 = (bf16[128,2048]{1,0:T(8,128)(2,1)S(1)}, bf16[128,2048]{1,0:T(8,128)(2,1)}, u32[]{:S(2)}, u32[]{:S(2)}) collective-permute-start(bf16[128,2048]{1,0:T(8,128)(2,1)S(1)} %copy-done.1), channel_id=1, source_target_pairs={{0,4},{4,8},{8,12},{12,28},{28,24},{24,20},{20,16},{16,0},{1,5},{5... | collective-permute-start | bytes 1572872 | tf_op jit(solution)/shard_map/ppermute | solution.py:399
  66.3 23.5 %collective-permute-start.6 = (bf16[128,2048]{1,0:T(8,128)(2,1)S(1)}, bf16[128,2048]{1,0:T(8,128)(2,1)}, u32[]{:S(2)}, u32[]{:S(2)}) collective-permute-start(bf16[128,2048]{1,0:T(8,128)(2,1)S(1)} %copy-done.3), channel_id=1, source_target_pairs={{0,16},{4,0},{8,4},{12,8},{28,12},{24,28},{20,24},{16,20},{1,17},{... | collective-permute-start | bytes 1572872 | tf_op jit(solution)/shard_map/ppermute | solution.py:399
  79.4 15.8 %collective-permute-start.22 = (bf16[4,256,128]{2,1,0:T(8,128)(2,1)}, bf16[4,256,128]{2,1,0:T(8,128)(2,1)}, u32[]{:S(2)}, u32[]{:S(2)}) collective-permute-start(bf16[4,256,128]{2,1,0:T(8,128)(2,1)} %get-tuple-element.42.refs_14_.refs_10_), channel_id=1, source_target_pairs={{0,3},{1,2},{2,1},{3,0},{4,7},{5,6},{6,5},{7,4},{8,11},{9,10},{10,... | collective-permute-start | bytes 786440 | tf_op jit(solution)/shard_map/ppermute | solution.py:220
  79.4 16.4 %collective-permute-start.21 = (bf16[4,256,128]{2,1,0:T(8,128)(2,1)}, bf16[4,256,128]{2,1,0:T(8,128)(2,1)}, u32[]{:S(2)}, u32[]{:S(2)}) collective-permute-start(bf16[4,256,128]{2,1,0:T(8,128)(2,1)} %get-tuple-element.42.refs_14_.refs_10_), channel_id=1, source_target_pairs={{0,2},{1,3},{2,0},{3,1},{4,6},{5,7},{6,4},{7,5},{8,10},{9,11},{10,... | collective-permute-start | bytes 786440 | tf_op jit(solution)/shard_map/ppermute | solution.py:220
  80.9 15.1 %collective-permute-start.20 = (bf16[4,256,128]{2,1,0:T(8,128)(2,1)}, bf16[4,256,128]{2,1,0:T(8,128)(2,1)}, u32[]{:S(2)}, u32[]{:S(2)}) collective-permute-start(bf16[4,256,128]{2,1,0:T(8,128)(2,1)} %get-tuple-element.42.refs_14_.refs_10_), channel_id=1, source_target_pairs={{0,1},{1,0},{2,3},{3,2},{4,5},{5,4},{6,7},{7,6},{8,9},{9,8},{10,11... | collective-permute-start | bytes 786440 | tf_op jit(solution)/shard_map/ppermute | solution.py:220
  89.8 3.7 %copy-start.14 = (bf16[256,768]{1,0:T(8,128)(2,1)S(1)}, bf16[256,768]{1,0:T(8,128)(2,1)}, u32[]{:S(2)}) copy-start(bf16[256,768]{1,0:T(8,128)(2,1)} %add_convert_fusion.refs_3_.refs_10_) | copy-start | bytes 1179652
  93.4 25.9 %collective-permute-start.23 = (f32[256,512]{1,0:T(8,128)}, f32[256,512]{1,0:T(8,128)}, u32[]{:S(2)}, u32[]{:S(2)}) collective-permute-start(f32[256,512]{1,0:T(8,128)} %shard_map.76), channel_id=1, source_target_pairs={{0,1},{1,0},{2,3},{3,2},{4,5},{5,4},{6,7},{7,6},{8,9},{9,8},{10,11... | collective-permute-start | bytes 1572872 | tf_op jit(solution)/shard_map/ppermute | solution.py:220
  93.5 17.1 %collective-permute-start.18 = (bf16[256,768]{1,0:T(8,128)(2,1)S(1)}, bf16[256,768]{1,0:T(8,128)(2,1)}, u32[]{:S(2)}, u32[]{:S(2)}) collective-permute-start(bf16[256,768]{1,0:T(8,128)(2,1)S(1)} %copy-done.14), channel_id=1, source_target_pairs={{0,2},{1,3},{2,0},{3,1},{4,6},{5,7},{6,4},{7,5},{8,10},{9,11},{10,... | collective-permute-start | bytes 1179656 | tf_op jit(solution)/shard_map/ppermute | solution.py:220
  95.2 15.5 %collective-permute-start.19 = (bf16[256,512]{1,0:T(8,128)(2,1)}, bf16[256,512]{1,0:T(8,128)(2,1)S(1)}, u32[]{:S(2)}, u32[]{:S(2)}) collective-permute-start(bf16[256,512]{1,0:T(8,128)(2,1)} %add_convert_fusion.2.refs_2_.refs_12_), channel_id=1, source_target_pairs={{0,2},{1,3},{2,0},{3,1},{4,6},{5,7},{6,4},{7,5},{8,10},{9,11},{10,... | collective-permute-start | bytes 786440 | tf_op jit(solution)/shard_map/ppermute | solution.py:220
  95.8 25.5 %collective-permute-start.16 = (bf16[128,2048]{1,0:T(8,128)(2,1)}, bf16[128,2048]{1,0:T(8,128)(2,1)}, u32[]{:S(2)}, u32[]{:S(2)}) collective-permute-start(bf16[128,2048]{1,0:T(8,128)(2,1)} %get-tuple-element.38.refs_0_), channel_id=1, source_target_pairs={{0,4},{4,8},{8,12},{12,28},{28,24},{24,20},{20,16},{16,0},{1,5},{5... | collective-permute-start | bytes 1572872 | tf_op jit(solution)/shard_map/ppermute | solution.py:399
  96.0 25.3 %collective-permute-start.17 = (bf16[128,2048]{1,0:T(8,128)(2,1)}, bf16[128,2048]{1,0:T(8,128)(2,1)}, u32[]{:S(2)}, u32[]{:S(2)}) collective-permute-start(bf16[128,2048]{1,0:T(8,128)(2,1)} %get-tuple-element.39.refs_1_), channel_id=1, source_target_pairs={{0,16},{4,0},{8,4},{12,8},{28,12},{24,28},{20,24},{16,20},{1,17},{... | collective-permute-start | bytes 1572872 | tf_op jit(solution)/shard_map/ppermute | solution.py:399
  110.7 1.0 copy-start.10
  117.3 1.3 copy-start.17
  121.3 2.1 %copy-start.16 = (bf16[256,512]{1,0:T(8,128)(2,1)S(1)}, bf16[256,512]{1,0:T(8,128)(2,1)}, u32[]{:S(2)}) copy-start(bf16[256,512]{1,0:T(8,128)(2,1)} %add_convert_fusion.1.refs_3_.refs_6_) | copy-start | bytes 786436
  121.3 13.6 %copy-start.22 = (f32[256,128]{1,0:T(8,128)S(1)}, f32[256,128]{1,0:T(8,128)}, u32[]{:S(2)}) copy-start(f32[256,128]{1,0:T(8,128)} %copy-done.21) | copy-start | bytes 393220
  123.1 1.8 %collective-permute-start.25 = (f32[256,256]{1,0:T(8,128)S(1)}, f32[256,256]{1,0:T(8,128)S(1)}, u32[]{:S(2)}, u32[]{:S(2)}) collective-permute-start(f32[256,256]{1,0:T(8,128)S(1)} %shard_map.78), channel_id=1, source_target_pairs={{0,1},{1,0},{2,3},{3,2},{4,5},{5,4},{6,7},{7,6},{8,9},{9,8},{10,11... | collective-permute-start | bytes 786440 | tf_op jit(solution)/shard_map/ppermute | solution.py:220
  123.4 9.2 %collective-permute-start.24 = (bf16[256,512]{1,0:T(8,128)(2,1)S(1)}, bf16[256,512]{1,0:T(8,128)(2,1)S(1)}, u32[]{:S(2)}, u32[]{:S(2)}) collective-permute-start(bf16[256,512]{1,0:T(8,128)(2,1)S(1)} %copy-done.16), channel_id=1, source_target_pairs={{0,2},{1,3},{2,0},{3,1},{4,6},{5,7},{6,4},{7,5},{8,10},{9,11},{10,... | collective-permute-start | bytes 786440 | tf_op jit(solution)/shard_map/ppermute | solution.py:220
  124.9 9.9 %collective-permute-start.26 = (bf16[256,256]{1,0:T(8,128)(2,1)S(1)}, bf16[256,256]{1,0:T(8,128)(2,1)S(1)}, u32[]{:S(2)}, u32[]{:S(2)}) collective-permute-start(bf16[256,256]{1,0:T(8,128)(2,1)S(1)} %add_convert_fusion.3.refs_8_), channel_id=1, source_target_pairs={{0,2},{1,3},{2,0},{3,1},{4,6},{5,7},{6,4},{7,5},{8,10},{9,11},{10,... | collective-permute-start | bytes 393224 | tf_op jit(solution)/shard_map/ppermute | solution.py:220
  134.9 1.2 copy-start.13
  136.1 1.6 %copy-start.18 = (f32[256,2048]{1,0:T(8,128)S(1)}, f32[256,2048]{1,0:T(8,128)}, u32[]{:S(2)}) copy-start(f32[256,2048]{1,0:T(8,128)} %copy-done.17) | copy-start | bytes 6291460
  (11 other events, 9.1 us)

commit v3 on v2

v3 whole, which is shorter than its diff:
```python
import functools

import jax
import jax.numpy as jnp
from jax import lax
from jax.experimental import pallas as pl
from jax.experimental.pallas import tpu as pltpu
from jax.sharding import PartitionSpec as P

EPSILON = 1e-05

HOLDERS = ("section", "wide")
LANES = 128
COLUMNS = 512
SMALL_COST = pl.CostEstimate(flops=1000, bytes_accessed=1000, transcendentals=0)


def contract_last(left, right):
    return lax.dot_general(
        left, right, (((1,), (1,)), ((), ())), preferred_element_type=jnp.float32
    )


def dot(left, right):
    return jnp.dot(left, right, preferred_element_type=jnp.float32)


VMEM_BYTES = 63 * 1024 * 1024


def local_kernel(body, out_shape, **kwargs):
    return pl.pallas_call(
        body,
        out_shape=out_shape,
        compiler_params=pltpu.CompilerParams(vmem_limit_bytes=VMEM_BYTES),
        cost_estimate=SMALL_COST,
        **kwargs,
    )


def in_hbm(count):
    return [pl.BlockSpec(memory_space=pltpu.HBM)] * count


TOKEN = jax.ShapeDtypeStruct((8, LANES), jnp.float32)


def gate(values, *after):
    count = len(values)
    *values, token = local_kernel(
        lambda *refs: None,
        [jax.ShapeDtypeStruct(v.shape, v.dtype) for v in values] + [TOKEN],
        in_specs=in_hbm(count + len(after)),
        out_specs=in_hbm(count + 1),
        input_output_aliases={i: i for i in range(count)},
    )(*values, *after)
    return values, token


def halves_body(up, down, *refs):
    up_half, down_half, _, buffer, copied = refs[-5:]
    rows = up_half.shape[0]
    ends = [(up.at[pl.ds(0, rows)], up_half), (down.at[pl.ds(rows, rows)], down_half)]
    copies = [
        [
            pltpu.make_async_copy(source, buffer.at[i], copied.at[2 * i]),
            pltpu.make_async_copy(buffer.at[i], result, copied.at[2 * i + 1]),
        ]
        for i, (source, result) in enumerate(ends)
    ]
    for first, _ in copies:
        first.start()
    for first, second in copies:
        first.wait()
        second.start()
    for _, second in copies:
        second.wait()


def gate_halves(up, down, *after):
    half = jax.ShapeDtypeStruct((up.shape[0] // 2, up.shape[1]), up.dtype)
    return local_kernel(
        halves_body,
        [half, half, TOKEN],
        in_specs=in_hbm(2 + len(after)),
        out_specs=in_hbm(3),
        scratch_shapes=[
            pltpu.VMEM((2, *half.shape), half.dtype),
            pltpu.SemaphoreType.DMA((4,)),
        ],
    )(up, down, *after)


def in_vmem(count):
    return [pl.BlockSpec(memory_space=pltpu.VMEM)] * count


def slots_body(slot_count, shard_row, token_row, target, sent):
    tokens, width = target.shape
    slots = sent.shape[0]
    shard_here = shard_row[...]
    earlier = lax.broadcasted_iota(jnp.int32, (tokens, tokens), 0) < lax.broadcasted_iota(
        jnp.int32, (tokens, tokens), 1
    )
    shard_column = jnp.broadcast_to(shard_here.astype(jnp.float32), (tokens, tokens)).T
    same = (shard_column.astype(jnp.int32) == shard_here) & earlier
    rank = jnp.sum(jnp.where(same, 1.0, 0.0), axis=0, keepdims=True).astype(jnp.int32)
    position = shard_here * slot_count + rank
    here = lax.broadcasted_iota(jnp.int32, (slots, tokens), 0) == position
    to_slot = jnp.where(here, 1.0, 0.0)
    sent[:, :width] = dot(to_slot.astype(jnp.bfloat16), target[...]).astype(jnp.bfloat16)
    row = token_row[...]
    high = jnp.sum(to_slot * (row >> 8).astype(jnp.float32), axis=1, keepdims=True)
    low = jnp.sum(to_slot * (row & 255).astype(jnp.float32), axis=1, keepdims=True)
    taken = jnp.sum(to_slot, axis=1, keepdims=True)
    lane = lax.broadcasted_iota(jnp.int32, (slots, LANES), 1)
    numbers = jnp.where(
        lane == 0, high, jnp.where(lane == 1, low, jnp.where(lane == 2, taken, 0.0))
    )
    sent[:, width:] = numbers.astype(jnp.bfloat16)


def pick_body(arrived, table, gain, _, hidden, scaled, squares, target, place, rows_buffer, copied):
    vocab_rows, width = table.shape
    target_width = target.shape[0] * LANES
    blocks = [slice(at, at + COLUMNS) for at in range(0, width, COLUMNS)]
    copies = [
        pltpu.make_async_copy(table.at[:, block], rows_buffer.at[:, block], copied.at[i])
        for i, block in enumerate(blocks)
    ]
    for copy in copies:
        copy.start()
    here = arrived[...]
    slots = here.shape[0]
    numbers = here[:, target_width:].astype(jnp.float32)
    row = jnp.where(numbers[:, 2:3] > 0.5, numbers[:, 0:1] * 256.0 + numbers[:, 1:2], -1.0)
    picks = jnp.where(
        row.astype(jnp.int32) == lax.broadcasted_iota(jnp.int32, (slots, vocab_rows), 1), 1.0, 0.0
    )
    place[...] = picks.T.astype(jnp.bfloat16)
    picks = picks.astype(jnp.bfloat16)
    for i in range(target.shape[0]):
        target[i] = here[:, i * LANES : (i + 1) * LANES]
    total = jnp.zeros((slots, LANES), jnp.float32)
    for copy, block in zip(copies, blocks):
        copy.wait()
        rows = dot(picks, rows_buffer[:, block])
        hidden[:, block] = rows.astype(jnp.bfloat16)
        scaled[:, block] = (rows * gain[:, block]).astype(jnp.bfloat16)
        for lane in range(0, COLUMNS, LANES):
            value = rows[:, lane : lane + LANES]
            total += value * value
    high = total.astype(jnp.bfloat16)
    squares[:, :LANES] = high
    squares[:, LANES:] = (total - high.astype(jnp.float32)).astype(jnp.bfloat16)


def start_pieces(pieces, buffer, copied):
    copies, first = [], 0
    for i, piece in enumerate(pieces):
        rows = pl.ds(first, piece.shape[0])
        copies.append(pltpu.make_async_copy(piece, buffer.at[rows], copied.at[i]))
        copies[-1].start()
        first += piece.shape[0]
    return copies


def forward_body(count, with_squares, scaled, *refs):
    pieces, refs = refs[:count], refs[count:]
    if with_squares:
        squares, refs = refs[0], refs[1:]
    _, out, _, rows_buffer, buffer, copied = refs
    rows = pltpu.make_async_copy(scaled, rows_buffer, copied.at[count])
    rows.start()
    copies = start_pieces(pieces, buffer, copied)
    if with_squares:
        out[:, buffer.shape[0] :] = squares[...]
    rows.wait()
    first = 0
    for piece, copy in zip(pieces, copies):
        copy.wait()
        part = slice(first, first + piece.shape[0])
        out[:, part] = contract_last(rows_buffer[...], buffer[part]).astype(out.dtype)
        first += piece.shape[0]


def scale_of(shares, width):
    total = jnp.zeros((shares[0].shape[0], LANES), jnp.float32)
    for share in shares:
        end = share.shape[1]
        for lanes in (slice(end - 2 * LANES, end - LANES), slice(end - LANES, end)):
            total += share[:, lanes].astype(jnp.float32)
    return lax.rsqrt(jnp.sum(total, axis=1, keepdims=True) / width + EPSILON)


def target_at(places, i, targets):
    distance, block = places[0, i], places[1, i]
    value = targets[0][block]
    for d in range(1, len(targets)):
        value = jnp.where(distance == d, targets[d][block], value)
    return value.astype(jnp.float32)


def residual_of(places, scale, shares, targets, inner, residual, first=0, last=None):
    last = residual.shape[1] // LANES if last is None else last
    for i in range(first, last):
        lanes = slice((i - first) * LANES, (i - first + 1) * LANES)
        value = shares[0][:, lanes].astype(jnp.float32)
        for share in shares[1:]:
            value += share[:, lanes].astype(jnp.float32)
        value *= scale
        rounded = (value - target_at(places, i, targets)).astype(jnp.bfloat16)
        residual[:, i * LANES : (i + 1) * LANES] = rounded
        inner = inner + rounded.astype(jnp.float32) * value
    return inner


def back_body(count, shared, features, narrow, width, before, places, *refs):
    pieces, refs = refs[:count], refs[count:]
    shares = []
    for size in shared:
        shares.append(refs[:size])
        refs = refs[size:]
    targets, refs = refs[:narrow], refs[narrow:]
    if before:
        back_in, inner_in, scale_in, refs = *refs[:3], refs[3:]
    _, back_out, inner_out, *scale_out, _, residual, buffer, copied = refs
    copies = start_pieces(pieces, buffer, copied)
    if before:
        scale, inner = scale_in[:, :1], inner_in[...]
    else:
        scale, inner = scale_of(shares[0], width), jnp.zeros(inner_out.shape, jnp.float32)
        scale_out[0][...] = jnp.broadcast_to(scale, scale_out[0].shape)
    first = 0
    for group, size in zip(shares, features):
        last = first + size // LANES
        inner = residual_of(places, scale, group, targets, inner, residual, first, last)
        first = last
    inner_out[...] = inner
    for copy in copies:
        copy.wait()
    for at in range(0, back_out.shape[1], COLUMNS):
        part = slice(at, at + COLUMNS)
        value = dot(residual[...], buffer[:, part])
        back_out[:, part] = value + back_in[:, part] if before else value


def tail_body(count, shared, narrow, width, places, *refs):
    pieces, refs = refs[:count], refs[count:]
    shares, refs = refs[:shared], refs[shared:]
    targets, refs = refs[:narrow], refs[narrow:]
    back_in, inner_in, scale, hidden, gain, place, table_grad, residual, factor = refs

    @pl.when(pl.program_id(0) == 0)
    def _():
        inner = residual_of(places, scale[:, :1], shares, targets, inner_in[...], residual)
        inner = jnp.sum(inner, axis=1, keepdims=True)
        factor[...] = scale[...] * scale[...] * (inner / width)

    back, first = back_in[...], 0
    for piece in pieces:
        back += dot(residual[:, first : first + piece.shape[0]], piece[...])
        first += piece.shape[0]
    row_grad = scale[:, :1] * (back * gain[...]) - hidden[...].astype(jnp.float32) * factor[:, :1]
    table_grad[...] = dot(place[...], row_grad.astype(jnp.bfloat16)).astype(jnp.bfloat16)


def whole_block(shape):
    return pl.BlockSpec(shape, lambda i, *_: (0,) * len(shape))


def column_block(rows):
    return pl.BlockSpec((rows, COLUMNS), lambda i, *_: (0, i))


def exchange_narrow(value, distance):
    narrow = lax.axis_size("narrow")
    return lax.ppermute(value, "narrow", [(i, i ^ distance) for i in range(narrow)])


def in_one_step(value):
    return [value] + [exchange_narrow(value, d) for d in range(1, lax.axis_size("narrow"))]


def in_two_steps(value):
    half = value.astype(jnp.float32) + exchange_narrow(value, 1).astype(jnp.float32)
    half = half.astype(jnp.bfloat16)
    return [half, exchange_narrow(half, 2)]


class Device:
    def __init__(self, token_shard, token_row, table, gain, kv_target):
        self.tokens = (token_shard, token_row, kv_target)
        self.table = table
        self.gain = gain.reshape(1, table.shape[1])
        self.owners = lax.axis_size(HOLDERS)
        self.slot_count = 2 * kv_target.shape[0] // self.owners
        self.slots = self.owners * self.slot_count
        self.blocks = kv_target.shape[1] // LANES
        self.width_all = table.shape[1] * lax.axis_size("narrow")
        self.before = ()

    def ask(self):
        token_shard, token_row, target = self.tokens
        tokens, width = target.shape
        sent = local_kernel(
            functools.partial(slots_body, self.slot_count),
            jax.ShapeDtypeStruct((self.slots, width + LANES), jnp.bfloat16),
        )(token_shard.reshape(1, tokens), token_row.reshape(1, tokens), target)
        self.arrived = lax.all_to_all(
            sent.reshape(self.owners, self.slot_count, width + LANES),
            HOLDERS,
            split_axis=0,
            concat_axis=0,
            tiled=True,
        ).reshape(self.slots, width + LANES)

    def pick(self, after):
        vocab_rows, width = self.table.shape
        rows = jax.ShapeDtypeStruct((self.slots, width), jnp.bfloat16)
        self.hidden, self.scaled, self.squares, target, self.place = local_kernel(
            pick_body,
            (
                rows,
                rows,
                jax.ShapeDtypeStruct((self.slots, 2 * LANES), jnp.bfloat16),
                jax.ShapeDtypeStruct((self.blocks, self.slots, LANES), jnp.bfloat16),
                jax.ShapeDtypeStruct((vocab_rows, self.slots), jnp.bfloat16),
            ),
            in_specs=in_vmem(1) + in_hbm(1) + in_vmem(1) + in_hbm(1),
            scratch_shapes=[
                pltpu.VMEM((vocab_rows, width), jnp.bfloat16),
                pltpu.SemaphoreType.DMA((width // COLUMNS,)),
            ],
        )(self.arrived, self.table, self.gain, after)
        self.target = target

    def share_targets(self):
        self.targets = in_one_step(self.target)

    def forward(self, group, after, with_squares=False):
        count = len(group)
        features = sum(piece.shape[0] for _, piece in group)
        slots, width = self.scaled.shape
        squares = [self.squares] if with_squares else []
        out_width = features + 2 * LANES * len(squares)
        return local_kernel(
            functools.partial(forward_body, count, with_squares),
            (jax.ShapeDtypeStruct((slots, out_width), jnp.bfloat16), TOKEN),
            in_specs=in_hbm(1 + count) + in_vmem(len(squares)) + in_hbm(1),
            out_specs=in_vmem(1) + in_hbm(1),
            scratch_shapes=[
                pltpu.VMEM((slots, width), jnp.bfloat16),
                pltpu.VMEM((features, width), jnp.bfloat16),
                pltpu.SemaphoreType.DMA((count + 1,)),
            ],
        )(self.scaled, *[piece for _, piece in group], *squares, after)

    def places(self, group):
        at = [which + i for which, piece in group for i in range(piece.shape[0] // LANES)]
        at = jnp.stack(at)
        distance = (at // self.blocks) ^ lax.axis_index("narrow")
        return jnp.stack([distance, at % self.blocks])

    def back(self, group, after, *shares):
        slots, width = self.scaled.shape
        count, narrow = len(group), len(self.targets)
        features = sum(piece.shape[0] for _, piece in group)
        lanes = jax.ShapeDtypeStruct((slots, LANES), jnp.float32)
        firsts = 0 if self.before else 1
        sizes = [share[0].shape[1] for share in shares]
        sizes[0] -= 2 * LANES * firsts
        back, inner, *scale, token = local_kernel(
            functools.partial(
                back_body, count, [len(share) for share in shares], sizes, narrow, self.width_all, not firsts
            ),
            [jax.ShapeDtypeStruct((slots, width), jnp.float32)] + [lanes] * (1 + firsts) + [TOKEN],
            in_specs=[pl.BlockSpec(memory_space=pltpu.SMEM)]
            + in_hbm(count)
            + in_vmem(sum(len(share) for share in shares) + narrow + len(self.before))
            + in_hbm(1),
            out_specs=in_vmem(2 + firsts) + in_hbm(1),
            scratch_shapes=[
                pltpu.VMEM((slots, features), jnp.bfloat16),
                pltpu.VMEM((features, width), jnp.bfloat16),
                pltpu.SemaphoreType.DMA((count,)),
            ],
        )(
            self.places(group),
            *[piece for _, piece in group],
            *[value for share in shares for value in share],
            *self.targets,
            *self.before,
            after,
        )
        self.before = (back, inner, *(scale or self.before[2:]))
        return token

    def tail(self, group, shares):
        slots, width = self.scaled.shape
        vocab_rows = self.place.shape[0]
        count, narrow = len(group), len(self.targets)
        features = sum(piece.shape[0] for _, piece in group)
        lanes = whole_block((slots, LANES))
        return local_kernel(
            functools.partial(tail_body, count, len(shares), narrow, self.width_all),
            jax.ShapeDtypeStruct((vocab_rows, width), jnp.bfloat16),
            grid_spec=pltpu.PrefetchScalarGridSpec(
                num_scalar_prefetch=1,
                grid=(width // COLUMNS,),
                in_specs=[column_block(piece.shape[0]) for _, piece in group]
                + [whole_block(share.shape) for share in shares]
                + [whole_block(self.target.shape)] * narrow
                + [column_block(slots), lanes, lanes, column_block(slots), column_block(1)]
                + [whole_block(self.place.shape)],
                out_specs=column_block(vocab_rows),
                scratch_shapes=[
                    pltpu.VMEM((slots, features), jnp.bfloat16),
                    pltpu.VMEM((slots, LANES), jnp.float32),
                ],
            ),
        )(
            self.places(group),
            *[piece for _, piece in group],
            *shares,
            *self.targets,
            *self.before,
            self.hidden,
            self.gain,
            self.place,
        )


def plain_order(device, weight):
    device.ask()
    device.pick(weight)
    device.share_targets()
    whole = lax.all_gather(weight, HOLDERS, axis=0, tiled=True)
    size = 4 * LANES
    groups = [
        [(jnp.int32(at // LANES), whole[at : at + size])] for at in range(0, whole.shape[0], size)
    ]
    token = weight
    for i, group in enumerate(groups[:-1]):
        projected, token = device.forward(group, token, i == 0)
        token = device.back(group, token, in_two_steps(projected))
    return device.tail(groups[-1], in_two_steps(device.forward(groups[-1], token)[0]))


def ring_order(device, weight):
    section, wide = lax.axis_index("section"), lax.axis_index("wide")
    holders = lax.axis_size(HOLDERS)
    at_ring = [i if i < holders // 2 else holders + holders // 2 - 1 - i for i in range(holders)]
    ring = jnp.where(section == 0, wide, holders - 1 - wide)

    def send(value, step):
        pairs = [(at_ring[i], at_ring[(i + step) % holders]) for i in range(holders)]
        return lax.ppermute(value, HOLDERS, pairs)

    def named(distance, piece, half=0):
        at = (ring + distance) % holders
        holder = jnp.where(at < holders // 2, at, holders + holders // 2 - 1 - at)
        return 2 * holder + half, piece

    up, down = send(weight, 1), send(weight, -1)
    device.ask()

    (up, down), token = gate([up, down], device.arrived)
    near = [named(0, weight), named(-1, up), named(1, down)]
    up, down = send(up, 1), send(down, -1)
    device.pick(token)
    sum0, done = device.forward(near, token, True)
    shares0 = in_two_steps(sum0)

    (up, down, device.target), token = gate([up, down, device.target], done)
    second = [named(-2, up), named(2, down)]
    up, down = send(up, 1), send(down, -1)
    device.share_targets()
    sum1, done = device.forward(second, token)
    shares1 = in_two_steps(sum1)

    third = [named(-3, up), named(3, down)]
    up, down, token = gate_halves(up, down, done, *device.targets)
    up, down = send(up, 1), send(down, -1)
    sum2, done = device.forward(third, token)
    shares2 = in_one_step(sum2)
    done = device.back(near + second, done, shares0, shares1)

    (up, down), token = gate([up, down], done)
    last = [named(4, up), named(4, down, 1)]
    sum3, done = device.forward(last, token)
    shares3 = in_one_step(sum3)
    device.back(third, done, shares2)
    return device.tail(last, shares3)


def on_device(token_shard, token_row, table, gain, key_value_weight, kv_target):
    device = Device(token_shard, token_row, table, gain, kv_target)
    holders = (lax.axis_size("section"), lax.axis_size("wide"))
    if holders == (2, 4) and key_value_weight.shape[0] == 2 * LANES:
        return ring_order(device, key_value_weight)
    return plain_order(device, key_value_weight)


def solution(mesh):
    return jax.shard_map(
        on_device,
        mesh=mesh,
        in_specs=(
            P(("section", "wide"), None),
            P(("section", "wide")),
            P(("section", "wide"), "narrow"),
            P("narrow"),
            P(("section", "wide"), "narrow"),
            P(("section", "wide"), "narrow"),
        ),
        out_specs=P(("section", "wide"), "narrow"),
        check_vma=False,
    )
```

time: 148 us -> 126 us (0.85)
  waiting for transfers between devices: 64.2 us -> 22.2 us
  blocking collectives: 0 us -> 30.9 us
  local copies, waits for them, and re-layouts: 19.6 us -> 2.31 us
  Pallas kernels: 27.6 us -> 44.8 us
  starting transfers between devices: 30.1 us -> 19.5 us
    all_to_all x0 -> x1, blocking collectives: none -> 30.9 us  [ask(): lax.all_to_all(sent.reshape(self.owners, self.slot_count, width + LANES),...]
    ppermute x13, waiting for transfers between devices: 26.8 us -> 4.2 us  [exchange_narrow(): lax.ppermute(value, 'narrow', [(i, i ^ distance) for i in range(narrow)])]
    pallas_call x15 -> x12, Pallas kernels: 26.6 us -> 42.8 us  [the longest x4 16 us: forward(): local_kernel(functools.partial(forward_body, count, with_squares), (jax.S...]
    ppermute x14 -> x8, waiting for transfers between devices: 33.1 us -> 18 us  [send(): return lax.ppermute(value, HOLDERS, pairs)]
    unnamed x62 -> x18, local copies, waits for them, and re-layouts: 17.1 us -> 2.2 us
    ppermute x14 -> x8, starting transfers between devices: 15.9 us -> 9.2 us  [send(): return lax.ppermute(value, HOLDERS, pairs)]
    all_to_all x1 -> x0, starting transfers between devices: 4.97 us -> none  [ask(): lax.all_to_all(sent.reshape(self.owners, self.slot_count, width + LANES),...]
    all_to_all x1 -> x0, waiting for transfers between devices: 4.31 us -> none  [ask(): lax.all_to_all(sent.reshape(self.owners, self.slot_count, width + LANES),...]
  transfers between devices with their start and end apart: 28 -> 21, of which waited for: 12 -> 7; matrix products, arithmetic and copies ran while one was open for 4% -> 4% of each run, Pallas kernels for 13% -> 30%
where the time goes in v3:
time: 126 us; the launch traced here: 125 us
  Pallas kernels  44.8 us (36%)
  blocking collectives  30.9 us (25%)
  waiting for transfers between devices  22.2 us (18%)
  starting transfers between devices  19.5 us (15%)
  other arithmetic  5.24 us (4%)
  local copies, waits for them, and re-layouts  2.31 us (2%)
    all_to_all x1, blocking collectives, ask(): lax.all_to_all(sent.reshape(self.owners, self.slot_count, width + LANES),...  30.9 us
    ppermute x8, waiting for transfers between devices, send(): return lax.ppermute(value, HOLDERS, pairs)  18 us
    pallas_call x4, Pallas kernels, forward(): local_kernel(functools.partial(forward_body, count, with_squares), (jax.S...  16 us
    pallas_call x2, Pallas kernels, back(): local_kernel(functools.partial(back_body, count, [len(share) for share in...  13 us
    ppermute x13, starting transfers between devices, exchange_narrow(): lax.ppermute(value, 'narrow', [(i, i ^ distance) for i in range(narrow)])  10.3 us
    ppermute x8, starting transfers between devices, send(): return lax.ppermute(value, HOLDERS, pairs)  9.2 us
    pallas_call x1, Pallas kernels, tail(): local_kernel(functools.partial(tail_body, count, len(shares), narrow, sel...  7.06 us
    pallas_call x1, Pallas kernels, pick(): local_kernel(pick_body, (rows, rows, jax.ShapeDtypeStruct((self.slots, 2...  4.71 us
  transfers between devices with their start and end apart: 21, of which 7 were waited for; matrix products, arithmetic and copies ran while one was open for 4% of the time, Pallas kernels for 30%

profile of v3, /device:TPU:0, one launch (start us, length us, event | category | flops | bytes accessed | tf_op | source)
XLA Modules:
  0.0 125.2 jit_solution(13557261774572537752)
XLA Ops:
  0.0 3.0 %collective-permute-start = (bf16[256,2048]{1,0:T(8,128)(2,1)}, bf16[256,2048]{1,0:T(8,128)(2,1)}, u32[]{:S(2)}, u32[]{:S(2)}) collective-permute-start(bf16[256,2048]{1,0:T(8,128)(2,1)} %refs_0_.3), channel_id=1, source_target_pairs={{0,4},{4,8},{8,12},{12,28},{28,24},{24,20},{20,16},{16,0},{1,5},{5... | collective-permute-start | bytes 3145736 | tf_op jit(solution)/shard_map/ppermute | solution.py:458
  3.0 2.0 %shard_map.64 = bf16[256,640]{1,0:T(8,128)(2,1)} custom-call(s32[1,128]{1,0:T(1,128)} %bitcast.26, s32[1,128]{1,0:T(1,128)} %bitcast.27, bf16[128,512]{1,0:T(8,128)(2,1)} %target.1), custom_call_target="tpu_custom_call" | custom-call | flops 1000 | bytes 1000 | tf_op jit(solution)/shard_map/pallas_call | solution.py:306
  5.0 30.9 %all_to_all.5 = bf16[8,32,640]{2,1,0:T(8,128)(2,1)} all-to-all(bf16[8,32,640]{2,1,0:T(8,128)(2,1)} %bitcast.23), channel_id=1, replica_groups=mesh['section'=2,'wide'=4,'narrow'=4] {'section','wide'}, dimensions={0} | all-to-all | bytes 655360 | tf_op jit(solution)/shard_map/all_to_all | solution.py:310
  35.9 0.4 collective-permute-start.2
  36.4 1.6 %collective-permute-start.3 = (bf16[256,2048]{1,0:T(8,128)(2,1)}, bf16[256,2048]{1,0:T(8,128)(2,1)}, u32[]{:S(2)}, u32[]{:S(2)}) collective-permute-start(bf16[256,2048]{1,0:T(8,128)(2,1)} %get-tuple-element.38.refs_2_), channel_id=1, source_target_pairs={{0,16},{4,0},{8,4},{12,8},{28,12},{24,28},{20,24},{16,20},{1,17},{... | collective-permute-start | bytes 3145736 | tf_op jit(solution)/shard_map/ppermute | solution.py:458
  38.0 4.7 %shard_map.66 = (bf16[256,2048]{1,0:T(8,128)(2,1)}, bf16[256,2048]{1,0:T(8,128)(2,1)}, bf16[256,256]{1,0:T(8,128)(2,1)}, bf16[4,256,128]{2,1,0:T(8,128)(2,1)}, bf16[512,256]{1,0:T(8,128)(2,1)}) custom-call(bf16[256,640]{1,0:T(8,128)(2,1)} %bitcast.22, bf16[512,2048]{1,0:T(8,128)(2,1)} %table.1, f32[1,2048]{1,0:T(1,128)} %bitcast.24, ...), custom_call_target="tpu_custom_call" | custom-call | flops 1000 | bytes 1000 | tf_op jit(solution)/shard_map/pallas_call | solution.py:321
  42.7 5.2 %shard_map.67 = (bf16[256,1024]{1,0:T(8,128)(2,1)}, f32[8,128]{1,0:T(8,128)}) custom-call(bf16[256,2048]{1,0:T(8,128)(2,1)} %get-tuple-element.41.scaled, bf16[256,2048]{1,0:T(8,128)(2,1)} %refs_0_.3, bf16[256,2048]{1,0:T(8,128)(2,1)} %get-tuple-element.37.refs_1_, bf16[256,2048]{1,0:T(8,128)(2,1)} %get-tuple-element.38.refs_2_, ...), custom_call_target="tpu_custom_call" | custom-call | flops 1000 | bytes 1000 | tf_op jit(solution)/shard_map/pallas_call | solution.py:347
  47.9 11.1 %collective-permute-done.2.refs_0_ = bf16[256,2048]{1,0:T(8,128)(2,1)} collective-permute-done((bf16[256,2048]{1,0:T(8,128)(2,1)}, bf16[256,2048]{1,0:T(8,128)(2,1)}, u32[]{:S(2)}, u32[]{:S(2)}) %collective-permute-start.2) | collective-permute-done | bytes 1048608 | tf_op jit(solution)/shard_map/ppermute | solution.py:458
  59.0 0.5 collective-permute-done.3.refs_1_
  59.6 1.7 %collective-permute-start.4 = (bf16[256,2048]{1,0:T(8,128)(2,1)}, bf16[256,2048]{1,0:T(8,128)(2,1)}, u32[]{:S(2)}, u32[]{:S(2)}) collective-permute-start(bf16[256,2048]{1,0:T(8,128)(2,1)} %get-tuple-element.44.refs_0_.refs_3_), channel_id=1, source_target_pairs={{0,4},{4,8},{8,12},{12,28},{28,24},{24,20},{20,16},{16,0},{1,5},{5... | collective-permute-start | bytes 3145736 | tf_op jit(solution)/shard_map/ppermute | solution.py:458
  61.3 0.3 collective-permute-start.5
  61.6 0.1 fusion.2
  61.7 0.5 collective-permute-start.6
  62.2 0.1 stack.86
  62.3 1.6 %collective-permute-start.7 = (bf16[4,256,128]{2,1,0:T(8,128)(2,1)}, bf16[4,256,128]{2,1,0:T(8,128)(2,1)S(1)}, u32[]{:S(2)}, u32[]{:S(2)}) collective-permute-start(bf16[4,256,128]{2,1,0:T(8,128)(2,1)} %get-tuple-element.48.refs_1_.refs_9_.refs_6_), channel_id=1, source_target_pairs={{0,2},{1,3},{2,0},{3,1},{4,6},{5,7},{6,4},{7,5},{8,10},{9,11},{10,... | collective-permute-start | bytes 786440 | tf_op jit(solution)/shard_map/ppermute | solution.py:278
  63.9 3.7 %shard_map.69 = (bf16[256,512]{1,0:T(8,128)(2,1)}, f32[8,128]{1,0:T(8,128)}) custom-call(bf16[256,2048]{1,0:T(8,128)(2,1)} %get-tuple-element.41.scaled, bf16[256,2048]{1,0:T(8,128)(2,1)} %get-tuple-element.44.refs_0_.refs_3_, bf16[256,2048]{1,0:T(8,128)(2,1)} %get-tuple-element.45.refs_1_.refs_4_, f32[8,128]{1,0:T(8,128)} %get-tuple-element.46.refs_2_), custom_call_target="tpu_custom_call" | custom-call | flops 1000 | bytes 1000 | tf_op jit(solution)/shard_map/pallas_call | solution.py:347
  67.7 0.1 collective-permute-start.8
  67.8 0.6 collective-permute-start.13
  68.4 2.2 %add_convert_fusion.refs_5_ = bf16[256,1024]{1,0:T(8,128)(2,1)} fusion(bf16[256,1024]{1,0:T(8,128)(2,1)} %collective-permute-done.11, bf16[256,1024]{1,0:T(8,128)(2,1)} %get-tuple-element.51), kind=kLoop, calls=%fused_computation | loop fusion | flops 1048576 | bytes 1572864 | tf_op jit(solution)/shard_map/convert_element_type | solution.py:287
  70.6 0.6 collective-permute-done.7.refs_3_.refs_11_.refs_8_
  71.1 2.1 %collective-permute-start.12 = (bf16[256,1024]{1,0:T(8,128)(2,1)}, bf16[256,1024]{1,0:T(8,128)(2,1)}, u32[]{:S(2)}, u32[]{:S(2)}) collective-permute-start(bf16[256,1024]{1,0:T(8,128)(2,1)} %add_convert_fusion.refs_5_), channel_id=1, source_target_pairs={{0,2},{1,3},{2,0},{3,1},{4,6},{5,7},{6,4},{7,5},{8,10},{9,11},{10,... | collective-permute-start | bytes 1572872 | tf_op jit(solution)/shard_map/ppermute | solution.py:278
  73.3 3.1 %collective-permute-done.8.refs_4_.refs_12_.refs_9_ = bf16[4,256,128]{2,1,0:T(8,128)(2,1)S(1)} collective-permute-done((bf16[4,256,128]{2,1,0:T(8,128)(2,1)S(1)}, bf16[4,256,128]{2,1,0:T(8,128)(2,1)S(1)}, u32[]{:S(2)}, u32[]{:S(2)}) %collective-permute-start.8) | collective-permute-done | bytes 262176 | tf_op jit(solution)/shard_map/ppermute | solution.py:278
  76.4 0.7 copy-done.4
  77.1 4.7 %collective-permute-done.4.up.refs_0_ = bf16[256,2048]{1,0:T(8,128)(2,1)} collective-permute-done((bf16[256,2048]{1,0:T(8,128)(2,1)}, bf16[256,2048]{1,0:T(8,128)(2,1)}, u32[]{:S(2)}, u32[]{:S(2)}) %collective-permute-start.4) | collective-permute-done | bytes 1048608 | tf_op jit(solution)/shard_map/ppermute | solution.py:458
  81.8 1.6 %collective-permute-done.5.down.refs_1_ = bf16[256,2048]{1,0:T(8,128)(2,1)} collective-permute-done((bf16[256,2048]{1,0:T(8,128)(2,1)}, bf16[256,2048]{1,0:T(8,128)(2,1)}, u32[]{:S(2)}, u32[]{:S(2)}) %collective-permute-start.5) | collective-permute-done | bytes 1048608 | tf_op jit(solution)/shard_map/ppermute | solution.py:458
  83.5 2.0 %shard_map.70 = (bf16[128,2048]{1,0:T(8,128)(2,1)}, bf16[128,2048]{1,0:T(8,128)(2,1)}, f32[8,128]{1,0:T(8,128)}) custom-call(bf16[256,2048]{1,0:T(8,128)(2,1)} %collective-permute-done.4.up.refs_0_, bf16[256,2048]{1,0:T(8,128)(2,1)} %collective-permute-done.5.down.refs_1_, f32[8,128]{1,0:T(8,128)} %get-tuple-element.47.refs_0_, ...), custom_call_target="tpu_custom_call" | custom-call | flops 1000 | bytes 1000 | tf_op jit(solution)/shard_map/pallas_call | solution.py:82
  85.5 0.3 collective-permute-start.10
  85.8 1.7 %collective-permute-start.9 = (bf16[128,2048]{1,0:T(8,128)(2,1)}, bf16[128,2048]{1,0:T(8,128)(2,1)}, u32[]{:S(2)}, u32[]{:S(2)}) collective-permute-start(bf16[128,2048]{1,0:T(8,128)(2,1)} %get-tuple-element.49), channel_id=1, source_target_pairs={{0,4},{4,8},{8,12},{12,28},{28,24},{24,20},{20,16},{16,0},{1,5},{5... | collective-permute-start | bytes 1572872 | tf_op jit(solution)/shard_map/ppermute | solution.py:458
  87.6 1.1 add_convert_fusion.1.refs_7_
  88.7 1.6 %collective-permute-start.14 = (bf16[256,512]{1,0:T(8,128)(2,1)S(1)}, bf16[256,512]{1,0:T(8,128)(2,1)}, u32[]{:S(2)}, u32[]{:S(2)}) collective-permute-start(bf16[256,512]{1,0:T(8,128)(2,1)S(1)} %add_convert_fusion.1.refs_7_), channel_id=1, source_target_pairs={{0,2},{1,3},{2,0},{3,1},{4,6},{5,7},{6,4},{7,5},{8,10},{9,11},{10,... | collective-permute-start | bytes 786440 | tf_op jit(solution)/shard_map/ppermute | solution.py:278
  90.2 0.1 fusion
  90.3 3.7 %shard_map.71 = (bf16[256,512]{1,0:T(8,128)(2,1)}, f32[8,128]{1,0:T(8,128)}) custom-call(bf16[256,2048]{1,0:T(8,128)(2,1)} %get-tuple-element.41.scaled, bf16[256,2048]{1,0:T(8,128)(2,1)} %collective-permute-done.4.up.refs_0_, bf16[256,2048]{1,0:T(8,128)(2,1)} %collective-permute-done.5.down.refs_1_, f32[8,128]{1,0:T(8,128)} %get-tuple-element.53.refs_2_), custom_call_target="tpu_custom_call" | custom-call | flops 1000 | bytes 1000 | tf_op jit(solution)/shard_map/pallas_call | solution.py:347
  94.1 0.1 collective-permute-start.18
  94.2 0.6 collective-permute-start.19
  94.8 0.5 collective-permute-done.14.refs_8_
  95.2 0.8 collective-permute-start.20
  96.0 0.6 pad_add_fusion.1.places
  96.6 7.0 %shard_map.72 = (f32[256,2048]{1,0:T(8,128)}, f32[256,128]{1,0:T(8,128)}, f32[256,128]{1,0:T(8,128)}, f32[8,128]{1,0:T(8,128)}) custom-call(s32[2,10]{1,0:T(2,128)} %pad_add_fusion.1.places, bf16[256,2048]{1,0:T(8,128)(2,1)} %refs_0_.3, bf16[256,2048]{1,0:T(8,128)(2,1)} %get-tuple-element.37.refs_1_, bf16[256,2048]{1,0:T(8,128)(2,1)} %get-tuple-element.38.refs_2_, ...), custom_call_target="tpu_custom_call" | custom-call | flops 1000 | bytes 1000 | tf_op jit(solution)/shard_map/pallas_call | solution.py:373
  103.7 0.8 copy-done.1
  104.4 3.4 %shard_map.74 = (bf16[256,256]{1,0:T(8,128)(2,1)}, f32[8,128]{1,0:T(8,128)}) custom-call(bf16[256,2048]{1,0:T(8,128)(2,1)} %get-tuple-element.41.scaled, bf16[128,2048]{1,0:T(8,128)(2,1)} %get-tuple-element.56.refs_0_, bf16[128,2048]{1,0:T(8,128)(2,1)} %get-tuple-element.57.refs_1_, f32[8,128]{1,0:T(8,128)} %get-tuple-element.58.refs_2_), custom_call_target="tpu_custom_call" | custom-call | flops 1000 | bytes 1000 | tf_op jit(solution)/shard_map/pallas_call | solution.py:347
  107.9 0.9 collective-permute-start.15
  108.8 0.5 collective-permute-start.16
  109.3 0.9 collective-permute-start.17
  110.2 0.6 pad_add_fusion.2.places
  110.8 0.6 pad_add_fusion.places
  111.4 6.0 %shard_map.75 = (f32[256,2048]{1,0:T(8,128)}, f32[256,128]{1,0:T(8,128)}, f32[8,128]{1,0:T(8,128)}) custom-call(s32[2,4]{1,0:T(2,128)} %pad_add_fusion.2.places, bf16[256,2048]{1,0:T(8,128)(2,1)} %collective-permute-done.4.up.refs_0_, bf16[256,2048]{1,0:T(8,128)(2,1)} %collective-permute-done.5.down.refs_1_, bf16[256,512]{1,0:T(8,128)(2,1)} %get-tuple-element.60.refs_2_, ...), custom_call_target="tpu_custom_call" | custom-call | flops 1000 | bytes 1000 | tf_op jit(solution)/shard_map/pallas_call | solution.py:373
  117.4 0.6 copy-done.6
  118.1 7.1 %shard_map.76 = bf16[512,2048]{1,0:T(8,128)(2,1)} custom-call(s32[2,2]{1,0:T(2,128)} %pad_add_fusion.places, bf16[128,2048]{1,0:T(8,128)(2,1)} %get-tuple-element.56.refs_0_, bf16[128,2048]{1,0:T(8,128)(2,1)} %get-tuple-element.57.refs_1_, bf16[256,256]{1,0:T(8,128)(2,1)} %get-tuple-element.59.refs_2_, bf16[256,256]{1,0:T(8,128)(2,1)} %copy-done.6, ...), custom_call_target="tpu_custom_call" | custom-call | flops 1000 | bytes 1000 | tf_op jit(solution)/shard_map/pallas_call | solution.py:405
  (37 shorter events, 0.2 us)
Async XLA Ops:
  0.0 35.9 %collective-permute-start = (bf16[256,2048]{1,0:T(8,128)(2,1)}, bf16[256,2048]{1,0:T(8,128)(2,1)}, u32[]{:S(2)}, u32[]{:S(2)}) collective-permute-start(bf16[256,2048]{1,0:T(8,128)(2,1)} %refs_0_.3), channel_id=1, source_target_pairs={{0,4},{4,8},{8,12},{12,28},{28,24},{24,20},{20,16},{16,0},{1,5},{5... | collective-permute-start | bytes 3145736 | tf_op jit(solution)/shard_map/ppermute | solution.py:458
  3.0 32.9 %collective-permute-start.1 = (bf16[256,2048]{1,0:T(8,128)(2,1)}, bf16[256,2048]{1,0:T(8,128)(2,1)}, u32[]{:S(2)}, u32[]{:S(2)}) collective-permute-start(bf16[256,2048]{1,0:T(8,128)(2,1)} %refs_0_.3), channel_id=1, source_target_pairs={{0,16},{4,0},{8,4},{12,8},{28,12},{24,28},{20,24},{16,20},{1,17},{... | collective-permute-start | bytes 3145736 | tf_op jit(solution)/shard_map/ppermute | solution.py:458
  35.9 23.1 %collective-permute-start.2 = (bf16[256,2048]{1,0:T(8,128)(2,1)}, bf16[256,2048]{1,0:T(8,128)(2,1)}, u32[]{:S(2)}, u32[]{:S(2)}) collective-permute-start(bf16[256,2048]{1,0:T(8,128)(2,1)} %get-tuple-element.37.refs_1_), channel_id=1, source_target_pairs={{0,4},{4,8},{8,12},{12,28},{28,24},{24,20},{20,16},{16,0},{1,5},{5... | collective-permute-start | bytes 3145736 | tf_op jit(solution)/shard_map/ppermute | solution.py:458
  36.4 23.2 %collective-permute-start.3 = (bf16[256,2048]{1,0:T(8,128)(2,1)}, bf16[256,2048]{1,0:T(8,128)(2,1)}, u32[]{:S(2)}, u32[]{:S(2)}) collective-permute-start(bf16[256,2048]{1,0:T(8,128)(2,1)} %get-tuple-element.38.refs_2_), channel_id=1, source_target_pairs={{0,16},{4,0},{8,4},{12,8},{28,12},{24,28},{20,24},{16,20},{1,17},{... | collective-permute-start | bytes 3145736 | tf_op jit(solution)/shard_map/ppermute | solution.py:458
  59.6 8.1 %copy-start = (bf16[4,256,128]{2,1,0:T(8,128)(2,1)S(1)}, bf16[4,256,128]{2,1,0:T(8,128)(2,1)}, u32[]{:S(2)}) copy-start(bf16[4,256,128]{2,1,0:T(8,128)(2,1)} %get-tuple-element.48.refs_1_.refs_9_.refs_6_) | copy-start | bytes 786436
  59.6 22.3 %collective-permute-start.4 = (bf16[256,2048]{1,0:T(8,128)(2,1)}, bf16[256,2048]{1,0:T(8,128)(2,1)}, u32[]{:S(2)}, u32[]{:S(2)}) collective-permute-start(bf16[256,2048]{1,0:T(8,128)(2,1)} %get-tuple-element.44.refs_0_.refs_3_), channel_id=1, source_target_pairs={{0,4},{4,8},{8,12},{12,28},{28,24},{24,20},{20,16},{16,0},{1,5},{5... | collective-permute-start | bytes 3145736 | tf_op jit(solution)/shard_map/ppermute | solution.py:458
  61.3 22.2 %collective-permute-start.5 = (bf16[256,2048]{1,0:T(8,128)(2,1)}, bf16[256,2048]{1,0:T(8,128)(2,1)}, u32[]{:S(2)}, u32[]{:S(2)}) collective-permute-start(bf16[256,2048]{1,0:T(8,128)(2,1)} %get-tuple-element.45.refs_1_.refs_4_), channel_id=1, source_target_pairs={{0,16},{4,0},{8,4},{12,8},{28,12},{24,28},{20,24},{16,20},{1,17},{... | collective-permute-start | bytes 3145736 | tf_op jit(solution)/shard_map/ppermute | solution.py:458
  61.6 6.1 %collective-permute-start.11 = (bf16[256,1024]{1,0:T(8,128)(2,1)}, bf16[256,1024]{1,0:T(8,128)(2,1)}, u32[]{:S(2)}, u32[]{:S(2)}) collective-permute-start(bf16[256,1024]{1,0:T(8,128)(2,1)} %get-tuple-element.51), channel_id=1, source_target_pairs={{0,1},{1,0},{2,3},{3,2},{4,5},{5,4},{6,7},{7,6},{8,9},{9,8},{10,11... | collective-permute-start | bytes 1572872 | tf_op jit(solution)/shard_map/ppermute | solution.py:278
  61.7 6.1 %collective-permute-start.6 = (bf16[4,256,128]{2,1,0:T(8,128)(2,1)}, bf16[4,256,128]{2,1,0:T(8,128)(2,1)S(1)}, u32[]{:S(2)}, u32[]{:S(2)}) collective-permute-start(bf16[4,256,128]{2,1,0:T(8,128)(2,1)} %get-tuple-element.48.refs_1_.refs_9_.refs_6_), channel_id=1, source_target_pairs={{0,1},{1,0},{2,3},{3,2},{4,5},{5,4},{6,7},{7,6},{8,9},{9,8},{10,11... | collective-permute-start | bytes 786440 | tf_op jit(solution)/shard_map/ppermute | solution.py:278
  62.3 8.8 %collective-permute-start.7 = (bf16[4,256,128]{2,1,0:T(8,128)(2,1)}, bf16[4,256,128]{2,1,0:T(8,128)(2,1)S(1)}, u32[]{:S(2)}, u32[]{:S(2)}) collective-permute-start(bf16[4,256,128]{2,1,0:T(8,128)(2,1)} %get-tuple-element.48.refs_1_.refs_9_.refs_6_), channel_id=1, source_target_pairs={{0,2},{1,3},{2,0},{3,1},{4,6},{5,7},{6,4},{7,5},{8,10},{9,11},{10,... | collective-permute-start | bytes 786440 | tf_op jit(solution)/shard_map/ppermute | solution.py:278
  67.7 8.8 %collective-permute-start.8 = (bf16[4,256,128]{2,1,0:T(8,128)(2,1)S(1)}, bf16[4,256,128]{2,1,0:T(8,128)(2,1)S(1)}, u32[]{:S(2)}, u32[]{:S(2)}) collective-permute-start(bf16[4,256,128]{2,1,0:T(8,128)(2,1)S(1)} %copy-done), channel_id=1, source_target_pairs={{0,3},{1,2},{2,1},{3,0},{4,7},{5,6},{6,5},{7,4},{8,11},{9,10},{10,... | collective-permute-start | bytes 786440 | tf_op jit(solution)/shard_map/ppermute | solution.py:278
  67.7 15.7 %copy-start.2 = (bf16[4,256,128]{2,1,0:T(8,128)(2,1)}, bf16[4,256,128]{2,1,0:T(8,128)(2,1)S(1)}, u32[]{:S(2)}) copy-start(bf16[4,256,128]{2,1,0:T(8,128)(2,1)S(1)} %collective-permute-done.6.refs_2_.refs_10_.refs_7_) | copy-start | bytes 786436
  67.8 19.8 %collective-permute-start.13 = (bf16[256,512]{1,0:T(8,128)(2,1)}, bf16[256,512]{1,0:T(8,128)(2,1)}, u32[]{:S(2)}, u32[]{:S(2)}) collective-permute-start(bf16[256,512]{1,0:T(8,128)(2,1)} %get-tuple-element.52), channel_id=1, source_target_pairs={{0,1},{1,0},{2,3},{3,2},{4,5},{5,4},{6,7},{7,6},{8,9},{9,8},{10,11... | collective-permute-start | bytes 786440 | tf_op jit(solution)/shard_map/ppermute | solution.py:278
  71.1 12.3 %copy-start.3 = (bf16[4,256,128]{2,1,0:T(8,128)(2,1)}, bf16[4,256,128]{2,1,0:T(8,128)(2,1)S(1)}, u32[]{:S(2)}) copy-start(bf16[4,256,128]{2,1,0:T(8,128)(2,1)S(1)} %collective-permute-done.7.refs_3_.refs_11_.refs_8_) | copy-start | bytes 786436
  71.1 23.0 %collective-permute-start.12 = (bf16[256,1024]{1,0:T(8,128)(2,1)}, bf16[256,1024]{1,0:T(8,128)(2,1)}, u32[]{:S(2)}, u32[]{:S(2)}) collective-permute-start(bf16[256,1024]{1,0:T(8,128)(2,1)} %add_convert_fusion.refs_5_), channel_id=1, source_target_pairs={{0,2},{1,3},{2,0},{3,1},{4,6},{5,7},{6,4},{7,5},{8,10},{9,11},{10,... | collective-permute-start | bytes 1572872 | tf_op jit(solution)/shard_map/ppermute | solution.py:278
  76.4 0.7 copy-start.4
  85.5 18.2 %collective-permute-start.10 = (bf16[128,2048]{1,0:T(8,128)(2,1)}, bf16[128,2048]{1,0:T(8,128)(2,1)S(1)}, u32[]{:S(2)}, u32[]{:S(2)}) collective-permute-start(bf16[128,2048]{1,0:T(8,128)(2,1)} %get-tuple-element.50), channel_id=1, source_target_pairs={{0,16},{4,0},{8,4},{12,8},{28,12},{24,28},{20,24},{16,20},{1,17},{... | collective-permute-start | bytes 1572872 | tf_op jit(solution)/shard_map/ppermute | solution.py:458
  85.8 17.8 %collective-permute-start.9 = (bf16[128,2048]{1,0:T(8,128)(2,1)}, bf16[128,2048]{1,0:T(8,128)(2,1)}, u32[]{:S(2)}, u32[]{:S(2)}) collective-permute-start(bf16[128,2048]{1,0:T(8,128)(2,1)} %get-tuple-element.49), channel_id=1, source_target_pairs={{0,4},{4,8},{8,12},{12,28},{28,24},{24,20},{20,16},{16,0},{1,5},{5... | collective-permute-start | bytes 1572872 | tf_op jit(solution)/shard_map/ppermute | solution.py:458
  88.7 7.9 %copy-start.5 = (bf16[256,512]{1,0:T(8,128)(2,1)}, bf16[256,512]{1,0:T(8,128)(2,1)S(1)}, u32[]{:S(2)}) copy-start(bf16[256,512]{1,0:T(8,128)(2,1)S(1)} %add_convert_fusion.1.refs_7_) | copy-start | bytes 786436
  88.7 6.5 %collective-permute-start.14 = (bf16[256,512]{1,0:T(8,128)(2,1)S(1)}, bf16[256,512]{1,0:T(8,128)(2,1)}, u32[]{:S(2)}, u32[]{:S(2)}) collective-permute-start(bf16[256,512]{1,0:T(8,128)(2,1)S(1)} %add_convert_fusion.1.refs_7_), channel_id=1, source_target_pairs={{0,2},{1,3},{2,0},{3,1},{4,6},{5,7},{6,4},{7,5},{8,10},{9,11},{10,... | collective-permute-start | bytes 786440 | tf_op jit(solution)/shard_map/ppermute | solution.py:278
  94.1 15.2 %collective-permute-start.18 = (bf16[256,512]{1,0:T(8,128)(2,1)}, bf16[256,512]{1,0:T(8,128)(2,1)}, u32[]{:S(2)}, u32[]{:S(2)}) collective-permute-start(bf16[256,512]{1,0:T(8,128)(2,1)} %get-tuple-element.60.refs_2_), channel_id=1, source_target_pairs={{0,1},{1,0},{2,3},{3,2},{4,5},{5,4},{6,7},{7,6},{8,9},{9,8},{10,11... | collective-permute-start | bytes 786440 | tf_op jit(solution)/shard_map/ppermute | solution.py:278
  94.2 17.2 %collective-permute-start.19 = (bf16[256,512]{1,0:T(8,128)(2,1)}, bf16[256,512]{1,0:T(8,128)(2,1)}, u32[]{:S(2)}, u32[]{:S(2)}) collective-permute-start(bf16[256,512]{1,0:T(8,128)(2,1)} %get-tuple-element.60.refs_2_), channel_id=1, source_target_pairs={{0,2},{1,3},{2,0},{3,1},{4,6},{5,7},{6,4},{7,5},{8,10},{9,11},{10,... | collective-permute-start | bytes 786440 | tf_op jit(solution)/shard_map/ppermute | solution.py:278
  95.2 16.1 %collective-permute-start.20 = (bf16[256,512]{1,0:T(8,128)(2,1)}, bf16[256,512]{1,0:T(8,128)(2,1)}, u32[]{:S(2)}, u32[]{:S(2)}) collective-permute-start(bf16[256,512]{1,0:T(8,128)(2,1)} %get-tuple-element.60.refs_2_), channel_id=1, source_target_pairs={{0,3},{1,2},{2,1},{3,0},{4,7},{5,6},{6,5},{7,4},{8,11},{9,10},{10,... | collective-permute-start | bytes 786440 | tf_op jit(solution)/shard_map/ppermute | solution.py:278
  103.7 0.8 copy-start.1
  107.9 9.5 %collective-permute-start.15 = (bf16[256,256]{1,0:T(8,128)(2,1)}, bf16[256,256]{1,0:T(8,128)(2,1)S(1)}, u32[]{:S(2)}, u32[]{:S(2)}) collective-permute-start(bf16[256,256]{1,0:T(8,128)(2,1)} %get-tuple-element.59.refs_2_), channel_id=1, source_target_pairs={{0,1},{1,0},{2,3},{3,2},{4,5},{5,4},{6,7},{7,6},{8,9},{9,8},{10,11... | collective-permute-start | bytes 393224 | tf_op jit(solution)/shard_map/ppermute | solution.py:278
  108.8 8.6 %collective-permute-start.16 = (bf16[256,256]{1,0:T(8,128)(2,1)}, bf16[256,256]{1,0:T(8,128)(2,1)S(1)}, u32[]{:S(2)}, u32[]{:S(2)}) collective-permute-start(bf16[256,256]{1,0:T(8,128)(2,1)} %get-tuple-element.59.refs_2_), channel_id=1, source_target_pairs={{0,2},{1,3},{2,0},{3,1},{4,6},{5,7},{6,4},{7,5},{8,10},{9,11},{10,... | collective-permute-start | bytes 393224 | tf_op jit(solution)/shard_map/ppermute | solution.py:278
  109.3 8.1 %collective-permute-start.17 = (bf16[256,256]{1,0:T(8,128)(2,1)}, bf16[256,256]{1,0:T(8,128)(2,1)S(1)}, u32[]{:S(2)}, u32[]{:S(2)}) collective-permute-start(bf16[256,256]{1,0:T(8,128)(2,1)} %get-tuple-element.59.refs_2_), channel_id=1, source_target_pairs={{0,3},{1,2},{2,1},{3,0},{4,7},{5,6},{6,5},{7,4},{8,11},{9,10},{10,... | collective-permute-start | bytes 393224 | tf_op jit(solution)/shard_map/ppermute | solution.py:278
  117.3 0.6 copy-start.6
  117.4 0.7 copy-start.7
  117.4 0.7 copy-start.8

commit v4 on v3

--- a/solution.py
+++ b/solution.py
@@ -26,13 +26,14 @@
 
 
 VMEM_BYTES = 63 * 1024 * 1024
-
-
-def local_kernel(body, out_shape, **kwargs):
+END_VMEM_BYTES = 24 * 1024 * 1024
+
+
+def local_kernel(body, out_shape, vmem_bytes=VMEM_BYTES, **kwargs):
     return pl.pallas_call(
         body,
         out_shape=out_shape,
-        compiler_params=pltpu.CompilerParams(vmem_limit_bytes=VMEM_BYTES),
+        compiler_params=pltpu.CompilerParams(vmem_limit_bytes=vmem_bytes),
         cost_estimate=SMALL_COST,
         **kwargs,
     )
@@ -120,7 +121,29 @@
     sent[:, width:] = numbers.astype(jnp.bfloat16)
 
 
-def pick_body(arrived, table, gain, _, hidden, scaled, squares, target, place, rows_buffer, copied):
+def squares_body(table, _, squares, rows_buffer, copied):
+    vocab_rows, width = table.shape
+    count = copied.shape[0]
+    per_copy = vocab_rows // count
+    copies = []
+    for i in range(count):
+        rows = pl.ds(i * per_copy, per_copy)
+        copies.append(pltpu.make_async_copy(table.at[rows], rows_buffer.at[rows], copied.at[i]))
+        copies[-1].start()
+    for i, copy in enumerate(copies):
+        copy.wait()
+        rows = slice(i * per_copy, (i + 1) * per_copy)
+        total = jnp.zeros((per_copy, LANES), jnp.float32)
+        for at in range(0, width, LANES):
+            value = rows_buffer[rows, at : at + LANES].astype(jnp.float32)
+            total += value * value
+        total = jnp.broadcast_to(jnp.sum(total, axis=1, keepdims=True), total.shape)
+        squares[:, rows] = total.T[: squares.shape[0]]
+
+
+def pick_body(width_all, arrived, table, gain, *refs):
+    shares, refs = refs[:-8], refs[-8:]
+    _, hidden, normed, scale, target, place, rows_buffer, copied = refs
     vocab_rows, width = table.shape
     target_width = target.shape[0] * LANES
     blocks = [slice(at, at + COLUMNS) for at in range(0, width, COLUMNS)]
@@ -137,22 +160,20 @@
     picks = jnp.where(
         row.astype(jnp.int32) == lax.broadcasted_iota(jnp.int32, (slots, vocab_rows), 1), 1.0, 0.0
     )
+    total = shares[0][:1]
+    for share in shares[1:]:
+        total += share[:1]
+    row_scale = jnp.sum(picks * lax.rsqrt(total / width_all + EPSILON), axis=1, keepdims=True)
+    scale[...] = jnp.broadcast_to(row_scale, scale.shape)
     place[...] = picks.T.astype(jnp.bfloat16)
     picks = picks.astype(jnp.bfloat16)
     for i in range(target.shape[0]):
         target[i] = here[:, i * LANES : (i + 1) * LANES]
-    total = jnp.zeros((slots, LANES), jnp.float32)
     for copy, block in zip(copies, blocks):
         copy.wait()
         rows = dot(picks, rows_buffer[:, block])
         hidden[:, block] = rows.astype(jnp.bfloat16)
-        scaled[:, block] = (rows * gain[:, block]).astype(jnp.bfloat16)
-        for lane in range(0, COLUMNS, LANES):
-            value = rows[:, lane : lane + LANES]
-            total += value * value
-    high = total.astype(jnp.bfloat16)
-    squares[:, :LANES] = high
-    squares[:, LANES:] = (total - high.astype(jnp.float32)).astype(jnp.bfloat16)
+        normed[:, block] = (rows * row_scale * gain[:, block]).astype(jnp.bfloat16)
 
 
 def start_pieces(pieces, buffer, copied):
@@ -165,32 +186,21 @@
     return copies
 
 
-def forward_body(count, with_squares, scaled, *refs):
+def forward_body(count, normed, *refs):
     pieces, refs = refs[:count], refs[count:]
-    if with_squares:
-        squares, refs = refs[0], refs[1:]
     _, out, _, rows_buffer, buffer, copied = refs
-    rows = pltpu.make_async_copy(scaled, rows_buffer, copied.at[count])
+    rows = pltpu.make_async_copy(normed, rows_buffer, copied.at[count])
     rows.start()
     copies = start_pieces(pieces, buffer, copied)
-    if with_squares:
-        out[:, buffer.shape[0] :] = squares[...]
     rows.wait()
-    first = 0
+    first = last = 0
     for piece, copy in zip(pieces, copies):
         copy.wait()
-        part = slice(first, first + piece.shape[0])
-        out[:, part] = contract_last(rows_buffer[...], buffer[part]).astype(out.dtype)
-        first += piece.shape[0]
-
-
-def scale_of(shares, width):
-    total = jnp.zeros((shares[0].shape[0], LANES), jnp.float32)
-    for share in shares:
-        end = share.shape[1]
-        for lanes in (slice(end - 2 * LANES, end - LANES), slice(end - LANES, end)):
-            total += share[:, lanes].astype(jnp.float32)
-    return lax.rsqrt(jnp.sum(total, axis=1, keepdims=True) / width + EPSILON)
+        last += piece.shape[0]
+        if last - first >= 2 * LANES or last == buffer.shape[0]:
+            part = slice(first, last)
+            out[:, part] = contract_last(rows_buffer[...], buffer[part]).astype(out.dtype)
+            first = last
 
 
 def target_at(places, i, targets):
@@ -201,21 +211,20 @@
     return value.astype(jnp.float32)
 
 
-def residual_of(places, scale, shares, targets, inner, residual, first=0, last=None):
+def residual_of(places, shares, targets, inner, residual, first=0, last=None):
     last = residual.shape[1] // LANES if last is None else last
     for i in range(first, last):
         lanes = slice((i - first) * LANES, (i - first + 1) * LANES)
         value = shares[0][:, lanes].astype(jnp.float32)
         for share in shares[1:]:
             value += share[:, lanes].astype(jnp.float32)
-        value *= scale
         rounded = (value - target_at(places, i, targets)).astype(jnp.bfloat16)
         residual[:, i * LANES : (i + 1) * LANES] = rounded
         inner = inner + rounded.astype(jnp.float32) * value
     return inner
 
 
-def back_body(count, shared, features, narrow, width, before, places, *refs):
+def back_body(count, shared, features, narrow, before, ahead, places, *refs):
     pieces, refs = refs[:count], refs[count:]
     shares = []
     for size in shared:
@@ -223,20 +232,19 @@
         refs = refs[size:]
     targets, refs = refs[:narrow], refs[narrow:]
     if before:
-        back_in, inner_in, scale_in, refs = *refs[:3], refs[3:]
-    _, back_out, inner_out, *scale_out, _, residual, buffer, copied = refs
+        back_in, inner_in, refs = refs[0], refs[1], refs[2:]
+    _, back_out, inner_out, *target_out, _, residual, buffer, copied = refs
     copies = start_pieces(pieces, buffer, copied)
-    if before:
-        scale, inner = scale_in[:, :1], inner_in[...]
-    else:
-        scale, inner = scale_of(shares[0], width), jnp.zeros(inner_out.shape, jnp.float32)
-        scale_out[0][...] = jnp.broadcast_to(scale, scale_out[0].shape)
+    inner = inner_in[...] if before else jnp.zeros(inner_out.shape, jnp.float32)
     first = 0
     for group, size in zip(shares, features):
         last = first + size // LANES
-        inner = residual_of(places, scale, group, targets, inner, residual, first, last)
+        inner = residual_of(places, group, targets, inner, residual, first, last)
         first = last
     inner_out[...] = inner
+    for i in range(ahead):
+        lanes = slice(i * LANES, (i + 1) * LANES)
+        target_out[0][:, lanes] = target_at(places, first + i, targets).astype(jnp.bfloat16)
     for copy in copies:
         copy.wait()
     for at in range(0, back_out.shape[1], COLUMNS):
@@ -245,32 +253,36 @@
         back_out[:, part] = value + back_in[:, part] if before else value
 
 
-def tail_body(count, shared, narrow, width, places, *refs):
+def tail_body(count, width, *refs):
     pieces, refs = refs[:count], refs[count:]
-    shares, refs = refs[:shared], refs[shared:]
-    targets, refs = refs[:narrow], refs[narrow:]
-    back_in, inner_in, scale, hidden, gain, place, table_grad, residual, factor = refs
-
-    @pl.when(pl.program_id(0) == 0)
-    def _():
-        inner = residual_of(places, scale[:, :1], shares, targets, inner_in[...], residual)
-        inner = jnp.sum(inner, axis=1, keepdims=True)
-        factor[...] = scale[...] * scale[...] * (inner / width)
-
-    back, first = back_in[...], 0
-    for piece in pieces:
-        back += dot(residual[:, first : first + piece.shape[0]], piece[...])
-        first += piece.shape[0]
-    row_grad = scale[:, :1] * (back * gain[...]) - hidden[...].astype(jnp.float32) * factor[:, :1]
-    table_grad[...] = dot(place[...], row_grad.astype(jnp.bfloat16)).astype(jnp.bfloat16)
-
-
-def whole_block(shape):
-    return pl.BlockSpec(shape, lambda i, *_: (0,) * len(shape))
-
-
-def column_block(rows):
-    return pl.BlockSpec((rows, COLUMNS), lambda i, *_: (0, i))
+    shares, refs = refs[:-12], refs[-12:]
+    target, back_in, inner_in, hidden, gain, scale, place, table_grad, *refs = refs
+    residual, buffer, row_grad, copied = refs
+    inner = inner_in[...]
+    for at in range(0, residual.shape[1], LANES):
+        lanes = slice(at, at + LANES)
+        value = shares[0][:, lanes].astype(jnp.float32)
+        for share in shares[1:]:
+            value += share[:, lanes].astype(jnp.float32)
+        rounded = (value - target[:, lanes].astype(jnp.float32)).astype(jnp.bfloat16)
+        residual[:, lanes] = rounded
+        inner += rounded.astype(jnp.float32) * value
+    row_scale = scale[:, :1]
+    factor = row_scale * row_scale * (jnp.sum(inner, axis=1, keepdims=True) / width)
+    copies = []
+    for i in range(copied.shape[0]):
+        block = slice(i * COLUMNS, (i + 1) * COLUMNS)
+        back, first = back_in[:, block], 0
+        weights = jnp.concatenate([piece[:, block] for piece in pieces], axis=0)
+        back += dot(residual[...], weights)
+        row_grad[...] = (
+            row_scale * (back * gain[:, block]) - hidden[:, block].astype(jnp.float32) * factor
+        ).astype(jnp.bfloat16)
+        buffer[i] = dot(place[...], row_grad[...]).astype(jnp.bfloat16)
+        copies.append(pltpu.make_async_copy(buffer.at[i], table_grad.at[:, block], copied.at[i]))
+        copies[-1].start()
+    for copy in copies:
+        copy.wait()
 
 
 def exchange_narrow(value, distance):
@@ -303,58 +315,69 @@
     def ask(self):
         token_shard, token_row, target = self.tokens
         tokens, width = target.shape
-        sent = local_kernel(
+        self.sent = local_kernel(
             functools.partial(slots_body, self.slot_count),
             jax.ShapeDtypeStruct((self.slots, width + LANES), jnp.bfloat16),
         )(token_shard.reshape(1, tokens), token_row.reshape(1, tokens), target)
         self.arrived = lax.all_to_all(
-            sent.reshape(self.owners, self.slot_count, width + LANES),
+            self.sent.reshape(self.owners, self.slot_count, width + LANES),
             HOLDERS,
             split_axis=0,
             concat_axis=0,
             tiled=True,
         ).reshape(self.slots, width + LANES)
 
+    def square(self, after):
+        vocab_rows, width = self.table.shape
+        squares = local_kernel(
+            squares_body,
+            jax.ShapeDtypeStruct((8, vocab_rows), jnp.float32),
+            in_specs=in_hbm(2),
+            scratch_shapes=[
+                pltpu.VMEM((vocab_rows, width), jnp.bfloat16),
+                pltpu.SemaphoreType.DMA((vocab_rows // LANES,)),
+            ],
+        )(self.table, after)
+        self.squares = in_one_step(squares)
+
     def pick(self, after):
         vocab_rows, width = self.table.shape
         rows = jax.ShapeDtypeStruct((self.slots, width), jnp.bfloat16)
-        self.hidden, self.scaled, self.squares, target, self.place = local_kernel(
-            pick_body,
+        self.hidden, self.normed, self.scale, self.target, self.place = local_kernel(
+            functools.partial(pick_body, self.width_all),
             (
                 rows,
                 rows,
-                jax.ShapeDtypeStruct((self.slots, 2 * LANES), jnp.bfloat16),
+                jax.ShapeDtypeStruct((self.slots, LANES), jnp.float32),
                 jax.ShapeDtypeStruct((self.blocks, self.slots, LANES), jnp.bfloat16),
                 jax.ShapeDtypeStruct((vocab_rows, self.slots), jnp.bfloat16),
             ),
-            in_specs=in_vmem(1) + in_hbm(1) + in_vmem(1) + in_hbm(1),
+            in_specs=in_vmem(1) + in_hbm(1) + in_vmem(1 + len(self.squares)) + in_hbm(1),
             scratch_shapes=[
                 pltpu.VMEM((vocab_rows, width), jnp.bfloat16),
                 pltpu.SemaphoreType.DMA((width // COLUMNS,)),
             ],
-        )(self.arrived, self.table, self.gain, after)
-        self.target = target
+        )(self.arrived, self.table, self.gain, *self.squares, after)
 
     def share_targets(self):
         self.targets = in_one_step(self.target)
 
-    def forward(self, group, after, with_squares=False):
+    def forward(self, group, after, vmem_bytes=VMEM_BYTES):
         count = len(group)
         features = sum(piece.shape[0] for _, piece in group)
-        slots, width = self.scaled.shape
-        squares = [self.squares] if with_squares else []
-        out_width = features + 2 * LANES * len(squares)
+        slots, width = self.normed.shape
         return local_kernel(
-            functools.partial(forward_body, count, with_squares),
-            (jax.ShapeDtypeStruct((slots, out_width), jnp.bfloat16), TOKEN),
-            in_specs=in_hbm(1 + count) + in_vmem(len(squares)) + in_hbm(1),
+            functools.partial(forward_body, count),
+            (jax.ShapeDtypeStruct((slots, features), jnp.bfloat16), TOKEN),
+            vmem_bytes=vmem_bytes,
+            in_specs=in_hbm(2 + count),
             out_specs=in_vmem(1) + in_hbm(1),
             scratch_shapes=[
                 pltpu.VMEM((slots, width), jnp.bfloat16),
                 pltpu.VMEM((features, width), jnp.bfloat16),
                 pltpu.SemaphoreType.DMA((count + 1,)),
             ],
-        )(self.scaled, *[piece for _, piece in group], *squares, after)
+        )(self.normed, *[piece for _, piece in group], after)
 
     def places(self, group):
         at = [which + i for which, piece in group for i in range(piece.shape[0] // LANES)]
@@ -362,77 +385,76 @@
         distance = (at // self.blocks) ^ lax.axis_index("narrow")
         return jnp.stack([distance, at % self.blocks])
 
-    def back(self, group, after, *shares):
-        slots, width = self.scaled.shape
+    def back(self, group, after, *shares, ahead=(), vmem_bytes=VMEM_BYTES):
+        slots, width = self.normed.shape
         count, narrow = len(group), len(self.targets)
         features = sum(piece.shape[0] for _, piece in group)
         lanes = jax.ShapeDtypeStruct((slots, LANES), jnp.float32)
-        firsts = 0 if self.before else 1
+        blocks_ahead = sum(piece.shape[0] for _, piece in ahead) // LANES
+        targets = [jax.ShapeDtypeStruct((slots, blocks_ahead * LANES), jnp.bfloat16)]
+        targets = targets if ahead else []
         sizes = [share[0].shape[1] for share in shares]
-        sizes[0] -= 2 * LANES * firsts
-        back, inner, *scale, token = local_kernel(
+        shared = [len(share) for share in shares]
+        back, inner, *targets, token = local_kernel(
             functools.partial(
-                back_body, count, [len(share) for share in shares], sizes, narrow, self.width_all, not firsts
+                back_body, count, shared, sizes, narrow, len(self.before) > 0, blocks_ahead
             ),
-            [jax.ShapeDtypeStruct((slots, width), jnp.float32)] + [lanes] * (1 + firsts) + [TOKEN],
+            [jax.ShapeDtypeStruct((slots, width), jnp.float32), lanes] + targets + [TOKEN],
+            vmem_bytes=vmem_bytes,
             in_specs=[pl.BlockSpec(memory_space=pltpu.SMEM)]
             + in_hbm(count)
-            + in_vmem(sum(len(share) for share in shares) + narrow + len(self.before))
+            + in_vmem(sum(shared) + narrow + len(self.before))
             + in_hbm(1),
-            out_specs=in_vmem(2 + firsts) + in_hbm(1),
+            out_specs=in_vmem(2 + len(targets)) + in_hbm(1),
             scratch_shapes=[
                 pltpu.VMEM((slots, features), jnp.bfloat16),
                 pltpu.VMEM((features, width), jnp.bfloat16),
                 pltpu.SemaphoreType.DMA((count,)),
             ],
         )(
-            self.places(group),
+            self.places(group + list(ahead)),
             *[piece for _, piece in group],
             *[value for share in shares for value in share],
             *self.targets,
             *self.before,
             after,
         )
-        self.before = (back, inner, *(scale or self.before[2:]))
+        self.before = (back, inner)
+        self.last_target = targets
         return token
 
     def tail(self, group, shares):
-        slots, width = self.scaled.shape
+        slots, width = self.normed.shape
         vocab_rows = self.place.shape[0]
-        count, narrow = len(group), len(self.targets)
+        count = len(group)
         features = sum(piece.shape[0] for _, piece in group)
-        lanes = whole_block((slots, LANES))
         return local_kernel(
-            functools.partial(tail_body, count, len(shares), narrow, self.width_all),
+            functools.partial(tail_body, count, self.width_all),
             jax.ShapeDtypeStruct((vocab_rows, width), jnp.bfloat16),
-            grid_spec=pltpu.PrefetchScalarGridSpec(
-                num_scalar_prefetch=1,
-                grid=(width // COLUMNS,),
-                in_specs=[column_block(piece.shape[0]) for _, piece in group]
-                + [whole_block(share.shape) for share in shares]
-                + [whole_block(self.target.shape)] * narrow
-                + [column_block(slots), lanes, lanes, column_block(slots), column_block(1)]
-                + [whole_block(self.place.shape)],
-                out_specs=column_block(vocab_rows),
-                scratch_shapes=[
-                    pltpu.VMEM((slots, features), jnp.bfloat16),
-                    pltpu.VMEM((slots, LANES), jnp.float32),
-                ],
-            ),
+            vmem_bytes=END_VMEM_BYTES,
+            in_specs=in_vmem(count + len(shares) + 7),
+            out_specs=in_hbm(1)[0],
+            scratch_shapes=[
+                pltpu.VMEM((slots, features), jnp.bfloat16),
+                pltpu.VMEM((width // COLUMNS, vocab_rows, COLUMNS), jnp.bfloat16),
+                pltpu.VMEM((slots, COLUMNS), jnp.bfloat16),
+                pltpu.SemaphoreType.DMA((width // COLUMNS,)),
+            ],
         )(
-            self.places(group),
             *[piece for _, piece in group],
             *shares,
-            *self.targets,
+            *self.last_target,
             *self.before,
             self.hidden,
             self.gain,
+            self.scale,
             self.place,
         )
 
 
 def plain_order(device, weight):
     device.ask()
+    device.square(device.sent)
     device.pick(weight)
     device.share_targets()
     whole = lax.all_gather(weight, HOLDERS, axis=0, tiled=True)
@@ -442,8 +464,9 @@
     ]
     token = weight
     for i, group in enumerate(groups[:-1]):
-        projected, token = device.forward(group, token, i == 0)
-        token = device.back(group, token, in_two_steps(projected))
+        projected, token = device.forward(group, token)
+        ahead = groups[-1] if i == len(groups) - 2 else ()
+        token = device.back(group, token, in_two_steps(projected), ahead=ahead)
     return device.tail(groups[-1], in_two_steps(device.forward(groups[-1], token)[0]))
 
 
@@ -464,12 +487,13 @@
 
     up, down = send(weight, 1), send(weight, -1)
     device.ask()
+    device.square(device.sent)
 
     (up, down), token = gate([up, down], device.arrived)
     near = [named(0, weight), named(-1, up), named(1, down)]
     up, down = send(up, 1), send(down, -1)
     device.pick(token)
-    sum0, done = device.forward(near, token, True)
+    sum0, done = device.forward(near, token)
     shares0 = in_two_steps(sum0)
 
     (up, down, device.target), token = gate([up, down, device.target], done)
@@ -482,15 +506,14 @@
     third = [named(-3, up), named(3, down)]
     up, down, token = gate_halves(up, down, done, *device.targets)
     up, down = send(up, 1), send(down, -1)
-    sum2, done = device.forward(third, token)
+    sum2, done = device.forward(third, token, END_VMEM_BYTES)
     shares2 = in_one_step(sum2)
-    done = device.back(near + second, done, shares0, shares1)
-
-    (up, down), token = gate([up, down], done)
+    done = device.back(near + second, done, shares0, shares1, vmem_bytes=END_VMEM_BYTES)
+
     last = [named(4, up), named(4, down, 1)]
-    sum3, done = device.forward(last, token)
+    sum3, done = device.forward(last, done, END_VMEM_BYTES)
     shares3 = in_one_step(sum3)
-    device.back(third, done, shares2)
+    device.back(third, done, shares2, ahead=last, vmem_bytes=END_VMEM_BYTES)
     return device.tail(last, shares3)
 
 

time: 126 us -> 117 us (0.929)
  Pallas kernels: 44.8 us -> 33.3 us
  other arithmetic: 5.24 us -> 3.13 us
  starting transfers between devices: 19.5 us -> 21.4 us
  waiting for transfers between devices: 22.2 us -> 23.6 us
    pallas_call x8 -> x9, Pallas kernels: 40.8 us -> 29.2 us  [the longest x4 11.5 us: forward(): local_kernel(functools.partial(forward_body, count), (jax.ShapeDtypeStruc...]
    ppermute x13 -> x16, waiting for transfers between devices: 4.2 us -> 12.9 us  [exchange_narrow(): lax.ppermute(value, 'narrow', [(i, i ^ distance) for i in range(narrow)])]
    ppermute x8, waiting for transfers between devices: 18 us -> 10.7 us  [send(): return lax.ppermute(value, HOLDERS, pairs)]
    ppermute x13 -> x16, starting transfers between devices: 10.3 us -> 12.2 us  [exchange_narrow(): lax.ppermute(value, 'narrow', [(i, i ^ distance) for i in range(narrow)])]
    another operation x3 -> x2, other arithmetic: 1.75 us -> 0.02 us  [places(): return jnp.stack([distance, at % self.blocks])]
    unnamed x18 -> x36, local copies, waits for them, and re-layouts: 2.2 us -> 2.55 us
  transfers between devices with their start and end apart: 21 -> 24, of which waited for: 7 -> 10; matrix products, arithmetic and copies ran while one was open for 4% -> 3% of each run, Pallas kernels for 30% -> 26%
where the time goes in v4:
time: 117 us; the launch traced here: 116 us
  Pallas kernels  33.3 us (28%)
  blocking collectives  31.9 us (27%)
  waiting for transfers between devices  23.6 us (20%)
  starting transfers between devices  21.4 us (18%)
  other arithmetic  3.13 us (3%)
  local copies, waits for them, and re-layouts  2.76 us (2%)
    all_to_all x1, blocking collectives, ask(): lax.all_to_all(self.sent.reshape(self.owners, self.slot_count, width + LA...  31.9 us
    ppermute x16, waiting for transfers between devices, exchange_narrow(): lax.ppermute(value, 'narrow', [(i, i ^ distance) for i in range(narrow)])  12.9 us
    ppermute x16, starting transfers between devices, exchange_narrow(): lax.ppermute(value, 'narrow', [(i, i ^ distance) for i in range(narrow)])  12.2 us
    pallas_call x4, Pallas kernels, forward(): local_kernel(functools.partial(forward_body, count), (jax.ShapeDtypeStruc...  11.5 us
    ppermute x8, waiting for transfers between devices, send(): return lax.ppermute(value, HOLDERS, pairs)  10.7 us
    ppermute x8, starting transfers between devices, send(): return lax.ppermute(value, HOLDERS, pairs)  9.2 us
    pallas_call x2, Pallas kernels, back(): local_kernel(functools.partial(back_body, count, shared, sizes, narrow, l...  7.86 us
    pallas_call x1, Pallas kernels, pick(): local_kernel(functools.partial(pick_body, self.width_all), (rows, rows, j...  4.7 us
  transfers between devices with their start and end apart: 24, of which 10 were waited for; matrix products, arithmetic and copies ran while one was open for 3% of the time, Pallas kernels for 26%

profile of v4, /device:TPU:0, one launch (start us, length us, event | category | flops | bytes accessed | tf_op | source)
XLA Modules:
  0.0 116.3 jit_solution(9802146982155180005)
XLA Ops:
  0.0 3.0 %collective-permute-start.1 = (bf16[256,2048]{1,0:T(8,128)(2,1)}, bf16[256,2048]{1,0:T(8,128)(2,1)}, u32[]{:S(2)}, u32[]{:S(2)}) collective-permute-start(bf16[256,2048]{1,0:T(8,128)(2,1)} %refs_0_.3), channel_id=1, source_target_pairs={{0,16},{4,0},{8,4},{12,8},{28,12},{24,28},{20,24},{16,20},{1,17},{... | collective-permute-start | bytes 3145736 | tf_op jit(solution)/shard_map/ppermute | solution.py:481
  3.0 2.0 %shard_map.64._ = bf16[256,640]{1,0:T(8,128)(2,1)} custom-call(s32[1,128]{1,0:T(1,128)} %bitcast.26, s32[1,128]{1,0:T(1,128)} %bitcast.27, bf16[128,512]{1,0:T(8,128)(2,1)} %target.1), custom_call_target="tpu_custom_call" | custom-call | flops 1000 | bytes 1000 | tf_op jit(solution)/shard_map/pallas_call | solution.py:318
  5.0 31.9 %all_to_all.5 = bf16[8,32,640]{2,1,0:T(8,128)(2,1)} all-to-all(bf16[8,32,640]{2,1,0:T(8,128)(2,1)} %bitcast.25), channel_id=1, replica_groups=mesh['section'=2,'wide'=4,'narrow'=4] {'section','wide'}, dimensions={0} | all-to-all | bytes 655360 | tf_op jit(solution)/shard_map/all_to_all | solution.py:322
  37.0 0.4 collective-permute-start.2
  37.4 1.6 %collective-permute-start.3 = (bf16[256,2048]{1,0:T(8,128)(2,1)}, bf16[256,2048]{1,0:T(8,128)(2,1)}, u32[]{:S(2)}, u32[]{:S(2)}) collective-permute-start(bf16[256,2048]{1,0:T(8,128)(2,1)} %get-tuple-element.35.refs_2_), channel_id=1, source_target_pairs={{0,16},{4,0},{8,4},{12,8},{28,12},{24,28},{20,24},{16,20},{1,17},{... | collective-permute-start | bytes 3145736 | tf_op jit(solution)/shard_map/ppermute | solution.py:481
  39.0 2.6 %shard_map.66.refs_0_ = f32[8,512]{1,0:T(8,128)} custom-call(bf16[512,2048]{1,0:T(8,128)(2,1)} %table.3, bf16[256,640]{1,0:T(8,128)(2,1)} %shard_map.64._), custom_call_target="tpu_custom_call" | custom-call | flops 1000 | bytes 1000 | tf_op jit(solution)/shard_map/pallas_call | solution.py:332
  41.7 1.6 %collective-permute-start.5 = (f32[8,512]{1,0:T(8,128)}, f32[8,512]{1,0:T(8,128)S(1)}, u32[]{:S(2)}, u32[]{:S(2)}) collective-permute-start(f32[8,512]{1,0:T(8,128)} %shard_map.66.refs_0_), channel_id=1, source_target_pairs={{0,2},{1,3},{2,0},{3,1},{4,6},{5,7},{6,4},{7,5},{8,10},{9,11},{10,... | collective-permute-start | bytes 49160 | tf_op jit(solution)/shard_map/ppermute | solution.py:290
  43.2 0.3 collective-permute-start.4
  43.5 1.6 %collective-permute-done.6.refs_3_ = f32[8,512]{1,0:T(8,128)S(1)} collective-permute-done((f32[8,512]{1,0:T(8,128)}, f32[8,512]{1,0:T(8,128)S(1)}, u32[]{:S(2)}, u32[]{:S(2)}) %collective-permute-start.6) | collective-permute-done | bytes 16416 | tf_op jit(solution)/shard_map/ppermute | solution.py:290
  45.2 0.5 collective-permute-done.5.refs_2_
  45.8 0.5 copy-done.16
  46.3 4.7 %shard_map.67 = (bf16[256,2048]{1,0:T(8,128)(2,1)}, bf16[256,2048]{1,0:T(8,128)(2,1)}, f32[256,128]{1,0:T(8,128)}, bf16[4,256,128]{2,1,0:T(8,128)(2,1)}, bf16[512,256]{1,0:T(8,128)(2,1)}) custom-call(bf16[256,640]{1,0:T(8,128)(2,1)} %bitcast.24, bf16[512,2048]{1,0:T(8,128)(2,1)} %table.3, f32[1,2048]{1,0:T(1,128)} %bitcast.21, f32[8,512]{1,0:T(8,128)} %shard_map.66.refs_0_, ...), custom_call_target="tpu_custom_call" | custom-call | flops 1000 | bytes 1000 | tf_op jit(solution)/shard_map/pallas_call | solution.py:346
  51.0 4.3 %shard_map.68 = (bf16[256,768]{1,0:T(8,128)(2,1)}, f32[8,128]{1,0:T(8,128)}) custom-call(bf16[256,2048]{1,0:T(8,128)(2,1)} %get-tuple-element.38.normed, bf16[256,2048]{1,0:T(8,128)(2,1)} %refs_0_.3, bf16[256,2048]{1,0:T(8,128)(2,1)} %get-tuple-element.34.refs_1_, bf16[256,2048]{1,0:T(8,128)(2,1)} %get-tuple-element.35.refs_2_, ...), custom_call_target="tpu_custom_call" | custom-call | flops 1000 | bytes 1000 | tf_op jit(solution)/shard_map/pallas_call | solution.py:369
  55.3 5.0 %collective-permute-done.2.refs_0_ = bf16[256,2048]{1,0:T(8,128)(2,1)} collective-permute-done((bf16[256,2048]{1,0:T(8,128)(2,1)}, bf16[256,2048]{1,0:T(8,128)(2,1)}, u32[]{:S(2)}, u32[]{:S(2)}) %collective-permute-start.2) | collective-permute-done | bytes 1048608 | tf_op jit(solution)/shard_map/ppermute | solution.py:481
  60.3 1.1 collective-permute-start.7
  61.4 0.9 collective-permute-start.8
  62.4 1.6 %collective-permute-start.11 = (bf16[4,256,128]{2,1,0:T(8,128)(2,1)}, bf16[4,256,128]{2,1,0:T(8,128)(2,1)S(1)}, u32[]{:S(2)}, u32[]{:S(2)}) collective-permute-start(bf16[4,256,128]{2,1,0:T(8,128)(2,1)} %get-tuple-element.44.refs_1_.refs_9_.refs_6_), channel_id=1, source_target_pairs={{0,3},{1,2},{2,1},{3,0},{4,7},{5,6},{6,5},{7,4},{8,11},{9,10},{10,... | collective-permute-start | bytes 786440 | tf_op jit(solution)/shard_map/ppermute | solution.py:290
  64.0 0.5 collective-permute-start.10
  64.6 3.7 %shard_map.70 = (bf16[256,512]{1,0:T(8,128)(2,1)}, f32[8,128]{1,0:T(8,128)}) custom-call(bf16[256,2048]{1,0:T(8,128)(2,1)} %get-tuple-element.38.normed, bf16[256,2048]{1,0:T(8,128)(2,1)} %get-tuple-element.40.refs_0_.refs_3_, bf16[256,2048]{1,0:T(8,128)(2,1)} %get-tuple-element.41.refs_1_.refs_4_, f32[8,128]{1,0:T(8,128)} %get-tuple-element.42.refs_2_), custom_call_target="tpu_custom_call" | custom-call | flops 1000 | bytes 1000 | tf_op jit(solution)/shard_map/pallas_call | solution.py:369
  68.3 2.7 %collective-permute-done.11.refs_4_.refs_12_.refs_9_ = bf16[4,256,128]{2,1,0:T(8,128)(2,1)S(1)} collective-permute-done((bf16[4,256,128]{2,1,0:T(8,128)(2,1)}, bf16[4,256,128]{2,1,0:T(8,128)(2,1)S(1)}, u32[]{:S(2)}, u32[]{:S(2)}) %collective-permute-start.11) | collective-permute-done | bytes 262176 | tf_op jit(solution)/shard_map/ppermute | solution.py:290
  70.9 1.1 collective-permute-start.16
  72.0 0.1 stack.82
  72.1 0.1 stack.74
  72.2 2.0 %add_convert_fusion.refs_5_ = bf16[256,768]{1,0:T(8,128)(2,1)} fusion(bf16[256,768]{1,0:T(8,128)(2,1)} %collective-permute-done.14, bf16[256,768]{1,0:T(8,128)(2,1)} %get-tuple-element.47), kind=kLoop, calls=%fused_computation | loop fusion | flops 786432 | bytes 1179648 | tf_op jit(solution)/shard_map/convert_element_type | solution.py:299
  74.2 2.6 %collective-permute-done.10.refs_3_.refs_11_.refs_8_ = bf16[4,256,128]{2,1,0:T(8,128)(2,1)S(1)} collective-permute-done((bf16[4,256,128]{2,1,0:T(8,128)(2,1)}, bf16[4,256,128]{2,1,0:T(8,128)(2,1)S(1)}, u32[]{:S(2)}, u32[]{:S(2)}) %collective-permute-start.10) | collective-permute-done | bytes 262176 | tf_op jit(solution)/shard_map/ppermute | solution.py:290
  76.8 1.5 %collective-permute-start.15 = (bf16[256,768]{1,0:T(8,128)(2,1)}, bf16[256,768]{1,0:T(8,128)(2,1)}, u32[]{:S(2)}, u32[]{:S(2)}) collective-permute-start(bf16[256,768]{1,0:T(8,128)(2,1)} %add_convert_fusion.refs_5_), channel_id=1, source_target_pairs={{0,2},{1,3},{2,0},{3,1},{4,6},{5,7},{6,4},{7,5},{8,10},{9,11},{10,... | collective-permute-start | bytes 1179656 | tf_op jit(solution)/shard_map/ppermute | solution.py:290
  78.3 4.3 %collective-permute-done.7.up.refs_0_ = bf16[256,2048]{1,0:T(8,128)(2,1)} collective-permute-done((bf16[256,2048]{1,0:T(8,128)(2,1)}, bf16[256,2048]{1,0:T(8,128)(2,1)}, u32[]{:S(2)}, u32[]{:S(2)}) %collective-permute-start.7) | collective-permute-done | bytes 1048608 | tf_op jit(solution)/shard_map/ppermute | solution.py:481
  82.6 1.4 %collective-permute-done.8.down.refs_1_ = bf16[256,2048]{1,0:T(8,128)(2,1)} collective-permute-done((bf16[256,2048]{1,0:T(8,128)(2,1)}, bf16[256,2048]{1,0:T(8,128)(2,1)}, u32[]{:S(2)}, u32[]{:S(2)}) %collective-permute-start.8) | collective-permute-done | bytes 1048608 | tf_op jit(solution)/shard_map/ppermute | solution.py:481
  83.9 2.1 %shard_map.71 = (bf16[128,2048]{1,0:T(8,128)(2,1)}, bf16[128,2048]{1,0:T(8,128)(2,1)}, f32[8,128]{1,0:T(8,128)}) custom-call(bf16[256,2048]{1,0:T(8,128)(2,1)} %collective-permute-done.7.up.refs_0_, bf16[256,2048]{1,0:T(8,128)(2,1)} %collective-permute-done.8.down.refs_1_, f32[8,128]{1,0:T(8,128)} %get-tuple-element.43.refs_0_, ...), custom_call_target="tpu_custom_call" | custom-call | flops 1000 | bytes 1000 | tf_op jit(solution)/shard_map/pallas_call | solution.py:83
  86.1 1.6 %collective-permute-start.12 = (bf16[128,2048]{1,0:T(8,128)(2,1)}, bf16[128,2048]{1,0:T(8,128)(2,1)S(1)}, u32[]{:S(2)}, u32[]{:S(2)}) collective-permute-start(bf16[128,2048]{1,0:T(8,128)(2,1)} %get-tuple-element.45), channel_id=1, source_target_pairs={{0,4},{4,8},{8,12},{12,28},{28,24},{24,20},{20,16},{16,0},{1,5},{5... | collective-permute-start | bytes 1572872 | tf_op jit(solution)/shard_map/ppermute | solution.py:481
  87.7 0.5 collective-permute-start.13
  88.2 1.1 add_convert_fusion.1.refs_7_
  89.3 1.6 %collective-permute-start.17 = (bf16[256,512]{1,0:T(8,128)(2,1)S(1)}, bf16[256,512]{1,0:T(8,128)(2,1)S(1)}, u32[]{:S(2)}, u32[]{:S(2)}) collective-permute-start(bf16[256,512]{1,0:T(8,128)(2,1)S(1)} %add_convert_fusion.1.refs_7_), channel_id=1, source_target_pairs={{0,2},{1,3},{2,0},{3,1},{4,6},{5,7},{6,4},{7,5},{8,10},{9,11},{10,... | collective-permute-start | bytes 786440 | tf_op jit(solution)/shard_map/ppermute | solution.py:290
  90.8 1.2 %copy-done = bf16[256,2048]{1,0:T(8,128)(2,1)S(1)} copy-done((bf16[256,2048]{1,0:T(8,128)(2,1)S(1)}, bf16[256,2048]{1,0:T(8,128)(2,1)}, u32[]{:S(2)}) %copy-start) | copy-done | bytes 1048600
  92.0 0.7 copy-done.14
  92.7 2.9 %shard_map.72 = (bf16[256,512]{1,0:T(8,128)(2,1)S(1)}, f32[8,128]{1,0:T(8,128)S(1)}) custom-call(bf16[256,2048]{1,0:T(8,128)(2,1)S(1)} %copy-done, bf16[256,2048]{1,0:T(8,128)(2,1)} %collective-permute-done.7.up.refs_0_, bf16[256,2048]{1,0:T(8,128)(2,1)} %collective-permute-done.8.down.refs_1_, f32[8,128]{1,0:T(8,128)S(1)} %copy-done.14), custom_call_target="tpu_custom_call" | custom-call | flops 1000 | bytes 1000 | tf_op jit(solution)/shard_map/pallas_call | solution.py:369
  95.7 0.6 collective-permute-start.22
  96.3 1.3 %collective-permute-start.21 = (bf16[256,512]{1,0:T(8,128)(2,1)S(1)}, bf16[256,512]{1,0:T(8,128)(2,1)S(1)}, u32[]{:S(2)}, u32[]{:S(2)}) collective-permute-start(bf16[256,512]{1,0:T(8,128)(2,1)S(1)} %get-tuple-element.53.refs_2_), channel_id=1, source_target_pairs={{0,1},{1,0},{2,3},{3,2},{4,5},{5,4},{6,7},{7,6},{8,9},{9,8},{10,11... | collective-permute-start | bytes 786440 | tf_op jit(solution)/shard_map/ppermute | solution.py:290
  97.7 5.0 %shard_map.73 = (f32[256,2048]{1,0:T(8,128)S(1)}, f32[256,128]{1,0:T(8,128)S(1)}, f32[8,128]{1,0:T(8,128)S(1)}) custom-call(s32[2,10]{1,0:T(2,128)S(1)} %pad_add_fusion.places, bf16[256,2048]{1,0:T(8,128)(2,1)S(1)} %copy-done.2, bf16[256,2048]{1,0:T(8,128)(2,1)} %get-tuple-element.34.refs_1_, bf16[256,2048]{1,0:T(8,128)(2,1)} %get-tuple-element.35.refs_2_, ...), custom_call_target="tpu_custom_call" | custom-call | flops 1000 | bytes 1000 | tf_op jit(solution)/shard_map/pallas_call | solution.py:398
  102.7 0.6 shard_map.74
  103.4 0.4 collective-permute-start.20
  103.7 1.4 %collective-permute-start.19 = (bf16[256,256]{1,0:T(8,128)(2,1)S(1)}, bf16[256,256]{1,0:T(8,128)(2,1)S(1)}, u32[]{:S(2)}, u32[]{:S(2)}) collective-permute-start(bf16[256,256]{1,0:T(8,128)(2,1)S(1)} %get-tuple-element.52.refs_2_), channel_id=1, source_target_pairs={{0,2},{1,3},{2,0},{3,1},{4,6},{5,7},{6,4},{7,5},{8,10},{9,11},{10,... | collective-permute-start | bytes 393224 | tf_op jit(solution)/shard_map/ppermute | solution.py:290
  105.1 0.2 collective-permute-start.18
  105.3 2.7 %collective-permute-done.22.refs_4_ = bf16[256,512]{1,0:T(8,128)(2,1)S(1)} collective-permute-done((bf16[256,512]{1,0:T(8,128)(2,1)S(1)}, bf16[256,512]{1,0:T(8,128)(2,1)S(1)}, u32[]{:S(2)}, u32[]{:S(2)}) %collective-permute-start.22) | collective-permute-done | bytes 262176 | tf_op jit(solution)/shard_map/ppermute | solution.py:290
  108.1 2.8 %shard_map.75 = (f32[256,2048]{1,0:T(8,128)S(1)}, f32[256,128]{1,0:T(8,128)S(1)}, bf16[256,256]{1,0:T(8,128)(2,1)S(1)}, f32[8,128]{1,0:T(8,128)}) custom-call(s32[2,6]{1,0:T(2,128)S(1)} %pad_add_fusion.1.places, bf16[256,2048]{1,0:T(8,128)(2,1)} %collective-permute-done.7.up.refs_0_, bf16[256,2048]{1,0:T(8,128)(2,1)} %collective-permute-done.8.down.refs_1_, ...), custom_call_target="tpu_custom_call" | custom-call | flops 1000 | bytes 1000 | tf_op jit(solution)/shard_map/pallas_call | solution.py:398
  110.9 1.7 %collective-permute-done.20.refs_5_ = bf16[256,256]{1,0:T(8,128)(2,1)S(1)} collective-permute-done((bf16[256,256]{1,0:T(8,128)(2,1)S(1)}, bf16[256,256]{1,0:T(8,128)(2,1)S(1)}, u32[]{:S(2)}, u32[]{:S(2)}) %collective-permute-start.20) | collective-permute-done | bytes 131104 | tf_op jit(solution)/shard_map/ppermute | solution.py:290
  112.7 1.0 collective-permute-done.19.refs_4_
  113.7 2.6 %shard_map.76 = bf16[512,2048]{1,0:T(8,128)(2,1)} custom-call(bf16[128,2048]{1,0:T(8,128)(2,1)S(1)} %collective-permute-done.12.refs_0_, bf16[128,2048]{1,0:T(8,128)(2,1)S(1)} %collective-permute-done.13.refs_1_, bf16[256,256]{1,0:T(8,128)(2,1)S(1)} %get-tuple-element.52.refs_2_, bf16[256,256]{1,0:T(8,128)(2,1)S(1)} %collective-permute-done.18.refs_3_, ...), custom_call_target="tpu_custom_call" | custom-call | flops 1000 | bytes 1000 | tf_op jit(solution)/shard_map/pallas_call | solution.py:431
  (58 shorter events, 0.5 us)
Async XLA Ops:
  0.0 37.0 %collective-permute-start.1 = (bf16[256,2048]{1,0:T(8,128)(2,1)}, bf16[256,2048]{1,0:T(8,128)(2,1)}, u32[]{:S(2)}, u32[]{:S(2)}) collective-permute-start(bf16[256,2048]{1,0:T(8,128)(2,1)} %refs_0_.3), channel_id=1, source_target_pairs={{0,16},{4,0},{8,4},{12,8},{28,12},{24,28},{20,24},{16,20},{1,17},{... | collective-permute-start | bytes 3145736 | tf_op jit(solution)/shard_map/ppermute | solution.py:481
  3.0 34.0 %collective-permute-start = (bf16[256,2048]{1,0:T(8,128)(2,1)}, bf16[256,2048]{1,0:T(8,128)(2,1)}, u32[]{:S(2)}, u32[]{:S(2)}) collective-permute-start(bf16[256,2048]{1,0:T(8,128)(2,1)} %refs_0_.3), channel_id=1, source_target_pairs={{0,4},{4,8},{8,12},{12,28},{28,24},{24,20},{20,16},{16,0},{1,5},{5... | collective-permute-start | bytes 3145736 | tf_op jit(solution)/shard_map/ppermute | solution.py:481
  37.0 23.4 %collective-permute-start.2 = (bf16[256,2048]{1,0:T(8,128)(2,1)}, bf16[256,2048]{1,0:T(8,128)(2,1)}, u32[]{:S(2)}, u32[]{:S(2)}) collective-permute-start(bf16[256,2048]{1,0:T(8,128)(2,1)} %get-tuple-element.34.refs_1_), channel_id=1, source_target_pairs={{0,4},{4,8},{8,12},{12,28},{28,24},{24,20},{20,16},{16,0},{1,5},{5... | collective-permute-start | bytes 3145736 | tf_op jit(solution)/shard_map/ppermute | solution.py:481
  37.4 22.9 %collective-permute-start.3 = (bf16[256,2048]{1,0:T(8,128)(2,1)}, bf16[256,2048]{1,0:T(8,128)(2,1)}, u32[]{:S(2)}, u32[]{:S(2)}) collective-permute-start(bf16[256,2048]{1,0:T(8,128)(2,1)} %get-tuple-element.35.refs_2_), channel_id=1, source_target_pairs={{0,16},{4,0},{8,4},{12,8},{28,12},{24,28},{20,24},{16,20},{1,17},{... | collective-permute-start | bytes 3145736 | tf_op jit(solution)/shard_map/ppermute | solution.py:481
  41.6 3.6 %collective-permute-start.6 = (f32[8,512]{1,0:T(8,128)}, f32[8,512]{1,0:T(8,128)S(1)}, u32[]{:S(2)}, u32[]{:S(2)}) collective-permute-start(f32[8,512]{1,0:T(8,128)} %shard_map.66.refs_0_), channel_id=1, source_target_pairs={{0,3},{1,2},{2,1},{3,0},{4,7},{5,6},{6,5},{7,4},{8,11},{9,10},{10,... | collective-permute-start | bytes 49160 | tf_op jit(solution)/shard_map/ppermute | solution.py:290
  41.7 4.0 %collective-permute-start.5 = (f32[8,512]{1,0:T(8,128)}, f32[8,512]{1,0:T(8,128)S(1)}, u32[]{:S(2)}, u32[]{:S(2)}) collective-permute-start(f32[8,512]{1,0:T(8,128)} %shard_map.66.refs_0_), channel_id=1, source_target_pairs={{0,2},{1,3},{2,0},{3,1},{4,6},{5,7},{6,4},{7,5},{8,10},{9,11},{10,... | collective-permute-start | bytes 49160 | tf_op jit(solution)/shard_map/ppermute | solution.py:290
  43.2 2.5 %collective-permute-start.4 = (f32[8,512]{1,0:T(8,128)}, f32[8,512]{1,0:T(8,128)S(1)}, u32[]{:S(2)}, u32[]{:S(2)}) collective-permute-start(f32[8,512]{1,0:T(8,128)} %shard_map.66.refs_0_), channel_id=1, source_target_pairs={{0,1},{1,0},{2,3},{3,2},{4,5},{5,4},{6,7},{7,6},{8,9},{9,8},{10,11... | collective-permute-start | bytes 49160 | tf_op jit(solution)/shard_map/ppermute | solution.py:290
  45.2 0.6 copy-start.15
  45.7 0.6 copy-start.16
  45.7 0.6 copy-start.17
  60.3 22.2 %collective-permute-start.7 = (bf16[256,2048]{1,0:T(8,128)(2,1)}, bf16[256,2048]{1,0:T(8,128)(2,1)}, u32[]{:S(2)}, u32[]{:S(2)}) collective-permute-start(bf16[256,2048]{1,0:T(8,128)(2,1)} %get-tuple-element.40.refs_0_.refs_3_), channel_id=1, source_target_pairs={{0,4},{4,8},{8,12},{12,28},{28,24},{24,20},{20,16},{16,0},{1,5},{5... | collective-permute-start | bytes 3145736 | tf_op jit(solution)/shard_map/ppermute | solution.py:481
  61.4 22.5 %collective-permute-start.8 = (bf16[256,2048]{1,0:T(8,128)(2,1)}, bf16[256,2048]{1,0:T(8,128)(2,1)}, u32[]{:S(2)}, u32[]{:S(2)}) collective-permute-start(bf16[256,2048]{1,0:T(8,128)(2,1)} %get-tuple-element.41.refs_1_.refs_4_), channel_id=1, source_target_pairs={{0,16},{4,0},{8,4},{12,8},{28,12},{24,28},{20,24},{16,20},{1,17},{... | collective-permute-start | bytes 3145736 | tf_op jit(solution)/shard_map/ppermute | solution.py:481
  62.4 2.1 %collective-permute-start.14 = (bf16[256,768]{1,0:T(8,128)(2,1)}, bf16[256,768]{1,0:T(8,128)(2,1)}, u32[]{:S(2)}, u32[]{:S(2)}) collective-permute-start(bf16[256,768]{1,0:T(8,128)(2,1)} %get-tuple-element.47), channel_id=1, source_target_pairs={{0,1},{1,0},{2,3},{3,2},{4,5},{5,4},{6,7},{7,6},{8,9},{9,8},{10,11... | collective-permute-start | bytes 1179656 | tf_op jit(solution)/shard_map/ppermute | solution.py:290
  62.4 8.6 %collective-permute-start.11 = (bf16[4,256,128]{2,1,0:T(8,128)(2,1)}, bf16[4,256,128]{2,1,0:T(8,128)(2,1)S(1)}, u32[]{:S(2)}, u32[]{:S(2)}) collective-permute-start(bf16[4,256,128]{2,1,0:T(8,128)(2,1)} %get-tuple-element.44.refs_1_.refs_9_.refs_6_), channel_id=1, source_target_pairs={{0,3},{1,2},{2,1},{3,0},{4,7},{5,6},{6,5},{7,4},{8,11},{9,10},{10,... | collective-permute-start | bytes 786440 | tf_op jit(solution)/shard_map/ppermute | solution.py:290
  64.0 12.8 %collective-permute-start.10 = (bf16[4,256,128]{2,1,0:T(8,128)(2,1)}, bf16[4,256,128]{2,1,0:T(8,128)(2,1)S(1)}, u32[]{:S(2)}, u32[]{:S(2)}) collective-permute-start(bf16[4,256,128]{2,1,0:T(8,128)(2,1)} %get-tuple-element.44.refs_1_.refs_9_.refs_6_), channel_id=1, source_target_pairs={{0,2},{1,3},{2,0},{3,1},{4,6},{5,7},{6,4},{7,5},{8,10},{9,11},{10,... | collective-permute-start | bytes 786440 | tf_op jit(solution)/shard_map/ppermute | solution.py:290
  64.5 13.8 %collective-permute-start.9 = (bf16[4,256,128]{2,1,0:T(8,128)(2,1)}, bf16[4,256,128]{2,1,0:T(8,128)(2,1)S(1)}, u32[]{:S(2)}, u32[]{:S(2)}) collective-permute-start(bf16[4,256,128]{2,1,0:T(8,128)(2,1)} %get-tuple-element.44.refs_1_.refs_9_.refs_6_), channel_id=1, source_target_pairs={{0,1},{1,0},{2,3},{3,2},{4,5},{5,4},{6,7},{7,6},{8,9},{9,8},{10,11... | collective-permute-start | bytes 786440 | tf_op jit(solution)/shard_map/ppermute | solution.py:290
  70.9 13.0 %copy-start.4 = (bf16[4,256,128]{2,1,0:T(8,128)(2,1)}, bf16[4,256,128]{2,1,0:T(8,128)(2,1)S(1)}, u32[]{:S(2)}) copy-start(bf16[4,256,128]{2,1,0:T(8,128)(2,1)S(1)} %collective-permute-done.11.refs_4_.refs_12_.refs_9_) | copy-start | bytes 786436
  70.9 17.2 %collective-permute-start.16 = (bf16[256,512]{1,0:T(8,128)(2,1)}, bf16[256,512]{1,0:T(8,128)(2,1)}, u32[]{:S(2)}, u32[]{:S(2)}) collective-permute-start(bf16[256,512]{1,0:T(8,128)(2,1)} %get-tuple-element.48), channel_id=1, source_target_pairs={{0,1},{1,0},{2,3},{3,2},{4,5},{5,4},{6,7},{7,6},{8,9},{9,8},{10,11... | collective-permute-start | bytes 786440 | tf_op jit(solution)/shard_map/ppermute | solution.py:290
  76.8 7.1 %copy-start.6 = (bf16[4,256,128]{2,1,0:T(8,128)(2,1)}, bf16[4,256,128]{2,1,0:T(8,128)(2,1)S(1)}, u32[]{:S(2)}) copy-start(bf16[4,256,128]{2,1,0:T(8,128)(2,1)S(1)} %collective-permute-done.10.refs_3_.refs_11_.refs_8_) | copy-start | bytes 786436
  76.8 18.9 %collective-permute-start.15 = (bf16[256,768]{1,0:T(8,128)(2,1)}, bf16[256,768]{1,0:T(8,128)(2,1)}, u32[]{:S(2)}, u32[]{:S(2)}) collective-permute-start(bf16[256,768]{1,0:T(8,128)(2,1)} %add_convert_fusion.refs_5_), channel_id=1, source_target_pairs={{0,2},{1,3},{2,0},{3,1},{4,6},{5,7},{6,4},{7,5},{8,10},{9,11},{10,... | collective-permute-start | bytes 1179656 | tf_op jit(solution)/shard_map/ppermute | solution.py:290
  78.3 5.6 %copy-start.8 = (bf16[4,256,128]{2,1,0:T(8,128)(2,1)}, bf16[4,256,128]{2,1,0:T(8,128)(2,1)S(1)}, u32[]{:S(2)}) copy-start(bf16[4,256,128]{2,1,0:T(8,128)(2,1)S(1)} %collective-permute-done.9.refs_2_.refs_10_.refs_7_) | copy-start | bytes 786436
  86.1 11.6 %copy-start.3 = (bf16[4,256,128]{2,1,0:T(8,128)(2,1)S(1)}, bf16[4,256,128]{2,1,0:T(8,128)(2,1)}, u32[]{:S(2)}) copy-start(bf16[4,256,128]{2,1,0:T(8,128)(2,1)} %get-tuple-element.44.refs_1_.refs_9_.refs_6_) | copy-start | bytes 786436
  86.1 11.6 %copy-start.5 = (bf16[4,256,128]{2,1,0:T(8,128)(2,1)S(1)}, bf16[4,256,128]{2,1,0:T(8,128)(2,1)}, u32[]{:S(2)}) copy-start(bf16[4,256,128]{2,1,0:T(8,128)(2,1)} %copy-done.4) | copy-start | bytes 786436
  86.1 11.6 %copy-start.7 = (bf16[4,256,128]{2,1,0:T(8,128)(2,1)S(1)}, bf16[4,256,128]{2,1,0:T(8,128)(2,1)}, u32[]{:S(2)}) copy-start(bf16[4,256,128]{2,1,0:T(8,128)(2,1)} %copy-done.6) | copy-start | bytes 786436
  86.1 16.6 %collective-permute-start.12 = (bf16[128,2048]{1,0:T(8,128)(2,1)}, bf16[128,2048]{1,0:T(8,128)(2,1)S(1)}, u32[]{:S(2)}, u32[]{:S(2)}) collective-permute-start(bf16[128,2048]{1,0:T(8,128)(2,1)} %get-tuple-element.45), channel_id=1, source_target_pairs={{0,4},{4,8},{8,12},{12,28},{28,24},{24,20},{20,16},{16,0},{1,5},{5... | collective-permute-start | bytes 1572872 | tf_op jit(solution)/shard_map/ppermute | solution.py:481
  87.7 15.0 %collective-permute-start.13 = (bf16[128,2048]{1,0:T(8,128)(2,1)}, bf16[128,2048]{1,0:T(8,128)(2,1)S(1)}, u32[]{:S(2)}, u32[]{:S(2)}) collective-permute-start(bf16[128,2048]{1,0:T(8,128)(2,1)} %get-tuple-element.46), channel_id=1, source_target_pairs={{0,16},{4,0},{8,4},{12,8},{28,12},{24,28},{20,24},{16,20},{1,17},{... | collective-permute-start | bytes 1572872 | tf_op jit(solution)/shard_map/ppermute | solution.py:481
  89.3 7.0 %collective-permute-start.17 = (bf16[256,512]{1,0:T(8,128)(2,1)S(1)}, bf16[256,512]{1,0:T(8,128)(2,1)S(1)}, u32[]{:S(2)}, u32[]{:S(2)}) collective-permute-start(bf16[256,512]{1,0:T(8,128)(2,1)S(1)} %add_convert_fusion.1.refs_7_), channel_id=1, source_target_pairs={{0,2},{1,3},{2,0},{3,1},{4,6},{5,7},{6,4},{7,5},{8,10},{9,11},{10,... | collective-permute-start | bytes 786440 | tf_op jit(solution)/shard_map/ppermute | solution.py:290
  90.8 1.2 %copy-start = (bf16[256,2048]{1,0:T(8,128)(2,1)S(1)}, bf16[256,2048]{1,0:T(8,128)(2,1)}, u32[]{:S(2)}) copy-start(bf16[256,2048]{1,0:T(8,128)(2,1)} %get-tuple-element.38.normed) | copy-start | bytes 3145732
  92.0 0.7 copy-start.14
  92.7 4.9 %copy-start.2 = (bf16[256,2048]{1,0:T(8,128)(2,1)S(1)}, bf16[256,2048]{1,0:T(8,128)(2,1)}, u32[]{:S(2)}) copy-start(bf16[256,2048]{1,0:T(8,128)(2,1)} %refs_0_.3) | copy-start | bytes 3145732
  92.7 4.9 %copy-start.9 = (bf16[4,256,128]{2,1,0:T(8,128)(2,1)S(1)}, bf16[4,256,128]{2,1,0:T(8,128)(2,1)}, u32[]{:S(2)}) copy-start(bf16[4,256,128]{2,1,0:T(8,128)(2,1)} %copy-done.8) | copy-start | bytes 786436
  95.6 9.5 %collective-permute-start.23 = (bf16[256,512]{1,0:T(8,128)(2,1)S(1)}, bf16[256,512]{1,0:T(8,128)(2,1)S(1)}, u32[]{:S(2)}, u32[]{:S(2)}) collective-permute-start(bf16[256,512]{1,0:T(8,128)(2,1)S(1)} %get-tuple-element.53.refs_2_), channel_id=1, source_target_pairs={{0,3},{1,2},{2,1},{3,0},{4,7},{5,6},{6,5},{7,4},{8,11},{9,10},{10,... | collective-permute-start | bytes 786440 | tf_op jit(solution)/shard_map/ppermute | solution.py:290
  95.7 12.4 %collective-permute-start.22 = (bf16[256,512]{1,0:T(8,128)(2,1)S(1)}, bf16[256,512]{1,0:T(8,128)(2,1)S(1)}, u32[]{:S(2)}, u32[]{:S(2)}) collective-permute-start(bf16[256,512]{1,0:T(8,128)(2,1)S(1)} %get-tuple-element.53.refs_2_), channel_id=1, source_target_pairs={{0,2},{1,3},{2,0},{3,1},{4,6},{5,7},{6,4},{7,5},{8,10},{9,11},{10,... | collective-permute-start | bytes 786440 | tf_op jit(solution)/shard_map/ppermute | solution.py:290
  96.3 11.8 %collective-permute-start.21 = (bf16[256,512]{1,0:T(8,128)(2,1)S(1)}, bf16[256,512]{1,0:T(8,128)(2,1)S(1)}, u32[]{:S(2)}, u32[]{:S(2)}) collective-permute-start(bf16[256,512]{1,0:T(8,128)(2,1)S(1)} %get-tuple-element.53.refs_2_), channel_id=1, source_target_pairs={{0,1},{1,0},{2,3},{3,2},{4,5},{5,4},{6,7},{7,6},{8,9},{9,8},{10,11... | collective-permute-start | bytes 786440 | tf_op jit(solution)/shard_map/ppermute | solution.py:290
  97.6 5.1 %copy-start.1 = (bf16[256,2048]{1,0:T(8,128)(2,1)S(1)}, bf16[256,2048]{1,0:T(8,128)(2,1)}, u32[]{:S(2)}) copy-start(bf16[256,2048]{1,0:T(8,128)(2,1)} %get-tuple-element.38.normed) | copy-start | bytes 3145732
  103.4 9.3 %collective-permute-start.20 = (bf16[256,256]{1,0:T(8,128)(2,1)S(1)}, bf16[256,256]{1,0:T(8,128)(2,1)S(1)}, u32[]{:S(2)}, u32[]{:S(2)}) collective-permute-start(bf16[256,256]{1,0:T(8,128)(2,1)S(1)} %get-tuple-element.52.refs_2_), channel_id=1, source_target_pairs={{0,3},{1,2},{2,1},{3,0},{4,7},{5,6},{6,5},{7,4},{8,11},{9,10},{10,... | collective-permute-start | bytes 393224 | tf_op jit(solution)/shard_map/ppermute | solution.py:290
  103.7 9.9 %collective-permute-start.19 = (bf16[256,256]{1,0:T(8,128)(2,1)S(1)}, bf16[256,256]{1,0:T(8,128)(2,1)S(1)}, u32[]{:S(2)}, u32[]{:S(2)}) collective-permute-start(bf16[256,256]{1,0:T(8,128)(2,1)S(1)} %get-tuple-element.52.refs_2_), channel_id=1, source_target_pairs={{0,2},{1,3},{2,0},{3,1},{4,6},{5,7},{6,4},{7,5},{8,10},{9,11},{10,... | collective-permute-start | bytes 393224 | tf_op jit(solution)/shard_map/ppermute | solution.py:290
  105.1 8.6 %collective-permute-start.18 = (bf16[256,256]{1,0:T(8,128)(2,1)S(1)}, bf16[256,256]{1,0:T(8,128)(2,1)S(1)}, u32[]{:S(2)}, u32[]{:S(2)}) collective-permute-start(bf16[256,256]{1,0:T(8,128)(2,1)S(1)} %get-tuple-element.52.refs_2_), channel_id=1, source_target_pairs={{0,1},{1,0},{2,3},{3,2},{4,5},{5,4},{6,7},{7,6},{8,9},{9,8},{10,11... | collective-permute-start | bytes 393224 | tf_op jit(solution)/shard_map/ppermute | solution.py:290
  108.1 5.6 %copy-start.10 = (bf16[256,2048]{1,0:T(8,128)(2,1)S(1)}, bf16[256,2048]{1,0:T(8,128)(2,1)}, u32[]{:S(2)}) copy-start(bf16[256,2048]{1,0:T(8,128)(2,1)} %get-tuple-element.60.refs_9_) | copy-start | bytes 3145732
  108.1 5.6 %copy-start.11 = (bf16[512,256]{1,0:T(8,128)(2,1)S(1)}, bf16[512,256]{1,0:T(8,128)(2,1)}, u32[]{:S(2)}) copy-start(bf16[512,256]{1,0:T(8,128)(2,1)} %get-tuple-element.62.refs_12_) | copy-start | bytes 786436
  108.1 5.6 %copy-start.12 = (f32[256,128]{1,0:T(8,128)S(1)}, f32[256,128]{1,0:T(8,128)}, u32[]{:S(2)}) copy-start(f32[256,128]{1,0:T(8,128)} %get-tuple-element.61.refs_11_) | copy-start | bytes 393220
  108.1 5.6 %copy-start.13 = (f32[2048]{0:T(1024)S(1)}, f32[2048]{0:T(1024)}, u32[]{:S(2)}) copy-start(f32[2048]{0:T(1024)} %param.9) | copy-start | bytes 24580

commit v5 on v4

--- a/solution.py
+++ b/solution.py
@@ -41,6 +41,10 @@
 
 def in_hbm(count):
     return [pl.BlockSpec(memory_space=pltpu.HBM)] * count
+
+
+def anywhere(count):
+    return [pl.BlockSpec(memory_space=pl.ANY)] * count
 
 
 TOKEN = jax.ShapeDtypeStruct((8, LANES), jnp.float32)
@@ -56,40 +60,6 @@
         input_output_aliases={i: i for i in range(count)},
     )(*values, *after)
     return values, token
-
-
-def halves_body(up, down, *refs):
-    up_half, down_half, _, buffer, copied = refs[-5:]
-    rows = up_half.shape[0]
-    ends = [(up.at[pl.ds(0, rows)], up_half), (down.at[pl.ds(rows, rows)], down_half)]
-    copies = [
-        [
-            pltpu.make_async_copy(source, buffer.at[i], copied.at[2 * i]),
-            pltpu.make_async_copy(buffer.at[i], result, copied.at[2 * i + 1]),
-        ]
-        for i, (source, result) in enumerate(ends)
-    ]
-    for first, _ in copies:
-        first.start()
-    for first, second in copies:
-        first.wait()
-        second.start()
-    for _, second in copies:
-        second.wait()
-
-
-def gate_halves(up, down, *after):
-    half = jax.ShapeDtypeStruct((up.shape[0] // 2, up.shape[1]), up.dtype)
-    return local_kernel(
-        halves_body,
-        [half, half, TOKEN],
-        in_specs=in_hbm(2 + len(after)),
-        out_specs=in_hbm(3),
-        scratch_shapes=[
-            pltpu.VMEM((2, *half.shape), half.dtype),
-            pltpu.SemaphoreType.DMA((4,)),
-        ],
-    )(up, down, *after)
 
 
 def in_vmem(count):
@@ -294,10 +264,10 @@
     return [value] + [exchange_narrow(value, d) for d in range(1, lax.axis_size("narrow"))]
 
 
-def in_two_steps(value):
-    half = value.astype(jnp.float32) + exchange_narrow(value, 1).astype(jnp.float32)
+def in_two_steps(value, first=1):
+    half = value.astype(jnp.float32) + exchange_narrow(value, first).astype(jnp.float32)
     half = half.astype(jnp.bfloat16)
-    return [half, exchange_narrow(half, 2)]
+    return [half, exchange_narrow(half, 3 - first)]
 
 
 class Device:
@@ -360,7 +330,9 @@
         )(self.arrived, self.table, self.gain, *self.squares, after)
 
     def share_targets(self):
-        self.targets = in_one_step(self.target)
+        along = exchange_narrow(self.target, 2)
+        across = exchange_narrow(self.target, 1)
+        self.targets = [self.target, across, along, exchange_narrow(along, 1)]
 
     def forward(self, group, after, vmem_bytes=VMEM_BYTES):
         count = len(group)
@@ -370,7 +342,7 @@
             functools.partial(forward_body, count),
             (jax.ShapeDtypeStruct((slots, features), jnp.bfloat16), TOKEN),
             vmem_bytes=vmem_bytes,
-            in_specs=in_hbm(2 + count),
+            in_specs=in_hbm(1) + anywhere(count) + in_hbm(1),
             out_specs=in_vmem(1) + in_hbm(1),
             scratch_shapes=[
                 pltpu.VMEM((slots, width), jnp.bfloat16),
@@ -402,7 +374,7 @@
             [jax.ShapeDtypeStruct((slots, width), jnp.float32), lanes] + targets + [TOKEN],
             vmem_bytes=vmem_bytes,
             in_specs=[pl.BlockSpec(memory_space=pltpu.SMEM)]
-            + in_hbm(count)
+            + anywhere(count)
             + in_vmem(sum(shared) + narrow + len(self.before))
             + in_hbm(1),
             out_specs=in_vmem(2 + len(targets)) + in_hbm(1),
@@ -494,25 +466,24 @@
     up, down = send(up, 1), send(down, -1)
     device.pick(token)
     sum0, done = device.forward(near, token)
-    shares0 = in_two_steps(sum0)
+    shares0 = in_two_steps(sum0, 2)
 
     (up, down, device.target), token = gate([up, down, device.target], done)
     second = [named(-2, up), named(2, down)]
     up, down = send(up, 1), send(down, -1)
     device.share_targets()
-    sum1, done = device.forward(second, token)
-    shares1 = in_two_steps(sum1)
+    sum1, done = device.forward(second, token, END_VMEM_BYTES)
+    shares1 = in_two_steps(sum1, 2)
 
     third = [named(-3, up), named(3, down)]
-    up, down, token = gate_halves(up, down, done, *device.targets)
-    up, down = send(up, 1), send(down, -1)
-    sum2, done = device.forward(third, token, END_VMEM_BYTES)
-    shares2 = in_one_step(sum2)
+    up, down = send(up[:LANES], 1), send(down[LANES:], -1)
+    sum2, done = device.forward(third, done, END_VMEM_BYTES)
+    shares2 = in_two_steps(sum2, 2)
     done = device.back(near + second, done, shares0, shares1, vmem_bytes=END_VMEM_BYTES)
 
     last = [named(4, up), named(4, down, 1)]
     sum3, done = device.forward(last, done, END_VMEM_BYTES)
-    shares3 = in_one_step(sum3)
+    shares3 = in_two_steps(sum3)
     device.back(third, done, shares2, ahead=last, vmem_bytes=END_VMEM_BYTES)
     return device.tail(last, shares3)
 

time: 117 us -> 108 us (0.923)
  Pallas kernels: 33.3 us -> 29.3 us
  waiting for transfers between devices: 23.6 us -> 21.7 us
  starting transfers between devices: 21.4 us -> 19.8 us
    ppermute x16 -> x14, waiting for transfers between devices: 12.9 us -> 7.9 us  [exchange_narrow(): lax.ppermute(value, 'narrow', [(i, i ^ distance) for i in range(narrow)])]
    ppermute x8, waiting for transfers between devices: 10.7 us -> 13.8 us  [send(): return lax.ppermute(value, HOLDERS, pairs)]
    pallas_call x1 -> x0, Pallas kernels: 2.11 us -> none  [gate_halves(): local_kernel(halves_body, [half, half, TOKEN], in_specs=in_hbm(2 + len(af...]
    ppermute x16 -> x14, starting transfers between devices: 12.2 us -> 10.6 us  [exchange_narrow(): lax.ppermute(value, 'narrow', [(i, i ^ distance) for i in range(narrow)])]
    pallas_call x4, Pallas kernels: 11.5 us -> 10.1 us  [forward(): local_kernel(functools.partial(forward_body, count), (jax.ShapeDtypeStruc...]
    convert_element_type x2 -> x4, other arithmetic: 3.09 us -> 3.03 us  [in_two_steps(): half = half.astype(jnp.bfloat16)]
    unnamed x36 -> x24, local copies, waits for them, and re-layouts: 2.55 us -> 2.54 us
  transfers between devices with their start and end apart: 24 -> 22, of which waited for: 10 -> 12; matrix products, arithmetic and copies ran while one was open for 3% -> 3% of each run, Pallas kernels for 26% -> 25%
where the time goes in v5:
time: 108 us
  blocking collectives  30.9 us (29%)
  Pallas kernels  29.3 us (27%)
  waiting for transfers between devices  21.7 us (20%)
  starting transfers between devices  19.8 us (18%)
  other arithmetic  3.07 us (3%)
  local copies, waits for them, and re-layouts  2.81 us (3%)
    all_to_all x1, blocking collectives, ask(): lax.all_to_all(self.sent.reshape(self.owners, self.slot_count, width + LA...  30.9 us
    ppermute x8, waiting for transfers between devices, send(): return lax.ppermute(value, HOLDERS, pairs)  13.8 us
    ppermute x14, starting transfers between devices, exchange_narrow(): lax.ppermute(value, 'narrow', [(i, i ^ distance) for i in range(narrow)])  10.6 us
    pallas_call x4, Pallas kernels, forward(): local_kernel(functools.partial(forward_body, count), (jax.ShapeDtypeStruc...  10.1 us
    ppermute x8, starting transfers between devices, send(): return lax.ppermute(value, HOLDERS, pairs)  9.2 us
    ppermute x14, waiting for transfers between devices, exchange_narrow(): lax.ppermute(value, 'narrow', [(i, i ^ distance) for i in range(narrow)])  7.9 us
    pallas_call x2, Pallas kernels, back(): local_kernel(functools.partial(back_body, count, shared, sizes, narrow, l...  7.42 us
    pallas_call x1, Pallas kernels, pick(): local_kernel(functools.partial(pick_body, self.width_all), (rows, rows, j...  4.7 us
  transfers between devices with their start and end apart: 22, of which 12 were waited for; matrix products, arithmetic and copies ran while one was open for 3% of the time, Pallas kernels for 25%

profile of v5, /device:TPU:0, one launch (start us, length us, event | category | flops | bytes accessed | tf_op | source)
XLA Modules:
  0.0 107.9 jit_solution(6472699146084887818)
XLA Ops:
  0.0 3.0 %collective-permute-start = (bf16[256,2048]{1,0:T(8,128)(2,1)}, bf16[256,2048]{1,0:T(8,128)(2,1)}, u32[]{:S(2)}, u32[]{:S(2)}) collective-permute-start(bf16[256,2048]{1,0:T(8,128)(2,1)} %refs_0_.3), channel_id=1, source_target_pairs={{0,4},{4,8},{8,12},{12,28},{28,24},{24,20},{20,16},{16,0},{1,5},{5... | collective-permute-start | bytes 3145736 | tf_op jit(solution)/shard_map/ppermute | solution.py:453
  3.0 2.0 %shard_map.64._ = bf16[256,640]{1,0:T(8,128)(2,1)} custom-call(s32[1,128]{1,0:T(1,128)} %bitcast.26, s32[1,128]{1,0:T(1,128)} %bitcast.27, bf16[128,512]{1,0:T(8,128)(2,1)} %target.1), custom_call_target="tpu_custom_call" | custom-call | flops 1000 | bytes 1000 | tf_op jit(solution)/shard_map/pallas_call | solution.py:288
  5.0 30.9 %all_to_all.5 = bf16[8,32,640]{2,1,0:T(8,128)(2,1)} all-to-all(bf16[8,32,640]{2,1,0:T(8,128)(2,1)} %bitcast.25), channel_id=1, replica_groups=mesh['section'=2,'wide'=4,'narrow'=4] {'section','wide'}, dimensions={0} | all-to-all | bytes 655360 | tf_op jit(solution)/shard_map/all_to_all | solution.py:292
  35.9 0.4 collective-permute-start.2
  36.4 1.6 %collective-permute-start.3 = (bf16[256,2048]{1,0:T(8,128)(2,1)}, bf16[256,2048]{1,0:T(8,128)(2,1)}, u32[]{:S(2)}, u32[]{:S(2)}) collective-permute-start(bf16[256,2048]{1,0:T(8,128)(2,1)} %get-tuple-element.32.refs_2_), channel_id=1, source_target_pairs={{0,16},{4,0},{8,4},{12,8},{28,12},{24,28},{20,24},{16,20},{1,17},{... | collective-permute-start | bytes 3145736 | tf_op jit(solution)/shard_map/ppermute | solution.py:453
  38.0 2.5 %shard_map.66.refs_0_ = f32[8,512]{1,0:T(8,128)} custom-call(bf16[512,2048]{1,0:T(8,128)(2,1)} %table.3, bf16[256,640]{1,0:T(8,128)(2,1)} %shard_map.64._), custom_call_target="tpu_custom_call" | custom-call | flops 1000 | bytes 1000 | tf_op jit(solution)/shard_map/pallas_call | solution.py:302
  40.6 1.6 %collective-permute-start.5 = (f32[8,512]{1,0:T(8,128)}, f32[8,512]{1,0:T(8,128)S(1)}, u32[]{:S(2)}, u32[]{:S(2)}) collective-permute-start(f32[8,512]{1,0:T(8,128)} %shard_map.66.refs_0_), channel_id=1, source_target_pairs={{0,2},{1,3},{2,0},{3,1},{4,6},{5,7},{6,4},{7,5},{8,10},{9,11},{10,... | collective-permute-start | bytes 49160 | tf_op jit(solution)/shard_map/ppermute | solution.py:260
  42.2 0.3 collective-permute-start.6
  42.5 2.1 %collective-permute-done.5.refs_2_ = f32[8,512]{1,0:T(8,128)S(1)} collective-permute-done((f32[8,512]{1,0:T(8,128)}, f32[8,512]{1,0:T(8,128)S(1)}, u32[]{:S(2)}, u32[]{:S(2)}) %collective-permute-start.5) | collective-permute-done | bytes 16416 | tf_op jit(solution)/shard_map/ppermute | solution.py:260
  44.6 0.9 collective-permute-done.6.refs_3_
  45.6 0.6 copy-done.11
  46.1 4.7 %shard_map.67 = (bf16[256,2048]{1,0:T(8,128)(2,1)}, bf16[256,2048]{1,0:T(8,128)(2,1)}, f32[256,128]{1,0:T(8,128)}, bf16[4,256,128]{2,1,0:T(8,128)(2,1)}, bf16[512,256]{1,0:T(8,128)(2,1)}) custom-call(bf16[256,640]{1,0:T(8,128)(2,1)} %bitcast.24, bf16[512,2048]{1,0:T(8,128)(2,1)} %table.3, f32[1,2048]{1,0:T(1,128)} %bitcast.21, f32[8,512]{1,0:T(8,128)} %shard_map.66.refs_0_, ...), custom_call_target="tpu_custom_call" | custom-call | flops 1000 | bytes 1000 | tf_op jit(solution)/shard_map/pallas_call | solution.py:316
  50.9 4.3 %shard_map.68 = (bf16[256,768]{1,0:T(8,128)(2,1)}, f32[8,128]{1,0:T(8,128)}) custom-call(bf16[256,2048]{1,0:T(8,128)(2,1)} %get-tuple-element.35.normed, bf16[256,2048]{1,0:T(8,128)(2,1)} %refs_0_.3, bf16[256,2048]{1,0:T(8,128)(2,1)} %get-tuple-element.31.refs_1_, bf16[256,2048]{1,0:T(8,128)(2,1)} %get-tuple-element.32.refs_2_, ...), custom_call_target="tpu_custom_call" | custom-call | flops 1000 | bytes 1000 | tf_op jit(solution)/shard_map/pallas_call | solution.py:341
  55.1 3.9 %collective-permute-done.2.refs_0_ = bf16[256,2048]{1,0:T(8,128)(2,1)} collective-permute-done((bf16[256,2048]{1,0:T(8,128)(2,1)}, bf16[256,2048]{1,0:T(8,128)(2,1)}, u32[]{:S(2)}, u32[]{:S(2)}) %collective-permute-start.2) | collective-permute-done | bytes 1048608 | tf_op jit(solution)/shard_map/ppermute | solution.py:453
  59.0 0.5 collective-permute-done.3.refs_1_
  59.6 1.6 %collective-permute-start.9 = (bf16[256,2048]{1,0:T(8,128)(2,1)}, bf16[256,2048]{1,0:T(8,128)(2,1)S(1)}, u32[]{:S(2)}, u32[]{:S(2)}) collective-permute-start(bf16[256,2048]{1,0:T(8,128)(2,1)} %get-tuple-element.38.refs_1_.refs_4_), channel_id=1, source_target_pairs={{0,16},{4,0},{8,4},{12,8},{28,12},{24,28},{20,24},{16,20},{1,17},{... | collective-permute-start | bytes 3145736 | tf_op jit(solution)/shard_map/ppermute | solution.py:453
  61.2 0.4 collective-permute-start.7
  61.6 1.5 %collective-permute-start.11 = (bf16[256,768]{1,0:T(8,128)(2,1)}, bf16[256,768]{1,0:T(8,128)(2,1)S(1)}, u32[]{:S(2)}, u32[]{:S(2)}) collective-permute-start(bf16[256,768]{1,0:T(8,128)(2,1)} %get-tuple-element.39), channel_id=1, source_target_pairs={{0,2},{1,3},{2,0},{3,1},{4,6},{5,7},{6,4},{7,5},{8,10},{9,11},{10,... | collective-permute-start | bytes 1179656 | tf_op jit(solution)/shard_map/ppermute | solution.py:260
  63.1 1.2 %copy-done = bf16[256,2048]{1,0:T(8,128)(2,1)S(1)} copy-done((bf16[256,2048]{1,0:T(8,128)(2,1)S(1)}, bf16[256,2048]{1,0:T(8,128)(2,1)}, u32[]{:S(2)}) %copy-start) | copy-done | bytes 1048600
  64.3 0.7 copy-done.8
  65.0 3.5 %shard_map.70 = (bf16[256,512]{1,0:T(8,128)(2,1)}, f32[8,128]{1,0:T(8,128)S(1)}) custom-call(bf16[256,2048]{1,0:T(8,128)(2,1)S(1)} %copy-done, bf16[256,2048]{1,0:T(8,128)(2,1)} %get-tuple-element.37.refs_0_.refs_3_, bf16[256,2048]{1,0:T(8,128)(2,1)} %get-tuple-element.38.refs_1_.refs_4_, f32[8,128]{1,0:T(8,128)S(1)} %copy-done.8), custom_call_target="tpu_custom_call" | custom-call | flops 1000 | bytes 1000 | tf_op jit(solution)/shard_map/pallas_call | solution.py:341
  68.5 0.6 collective-permute-start.13
  69.1 2.4 %collective-permute-done.11 = bf16[256,768]{1,0:T(8,128)(2,1)S(1)} collective-permute-done((bf16[256,768]{1,0:T(8,128)(2,1)}, bf16[256,768]{1,0:T(8,128)(2,1)S(1)}, u32[]{:S(2)}, u32[]{:S(2)}) %collective-permute-start.11) | collective-permute-done | bytes 393248 | tf_op jit(solution)/shard_map/ppermute | solution.py:260
  71.5 1.8 %add_convert_fusion.refs_5_ = bf16[256,768]{1,0:T(8,128)(2,1)} fusion(bf16[256,768]{1,0:T(8,128)(2,1)S(1)} %collective-permute-done.11, bf16[256,768]{1,0:T(8,128)(2,1)} %get-tuple-element.39), kind=kLoop, calls=%fused_computation | loop fusion | flops 786432 | bytes 1179648 | tf_op jit(solution)/shard_map/convert_element_type | solution.py:269
  73.3 2.4 %collective-permute-start.16 = (bf16[4,256,128]{2,1,0:T(8,128)(2,1)S(1)}, bf16[4,256,128]{2,1,0:T(8,128)(2,1)}, u32[]{:S(2)}, u32[]{:S(2)}) collective-permute-start(bf16[4,256,128]{2,1,0:T(8,128)(2,1)S(1)} %copy-done.3), channel_id=1, source_target_pairs={{0,2},{1,3},{2,0},{3,1},{4,6},{5,7},{6,4},{7,5},{8,10},{9,11},{10,... | collective-permute-start | bytes 786440 | tf_op jit(solution)/shard_map/ppermute | solution.py:260
  75.7 6.2 %collective-permute-done.9.refs_1_ = bf16[256,2048]{1,0:T(8,128)(2,1)S(1)} collective-permute-done((bf16[256,2048]{1,0:T(8,128)(2,1)}, bf16[256,2048]{1,0:T(8,128)(2,1)S(1)}, u32[]{:S(2)}, u32[]{:S(2)}) %collective-permute-start.9) | collective-permute-done | bytes 1048608 | tf_op jit(solution)/shard_map/ppermute | solution.py:453
  81.9 0.1 stack.82
  82.0 0.1 stack.74
  82.2 0.2 collective-permute-done.7.refs_0_
  82.4 1.5 %collective-permute-start.10 = (bf16[128,2048]{1,0:T(8,128)(2,1)S(1)}, bf16[128,2048]{1,0:T(8,128)(2,1)S(1)}, u32[]{:S(2)}, u32[]{:S(2)}) collective-permute-start(bf16[128,2048]{1,0:T(8,128)(2,1)S(1)} %slice.9), channel_id=1, source_target_pairs={{0,16},{4,0},{8,4},{12,8},{28,12},{24,28},{20,24},{16,20},{1,17},{... | collective-permute-start | bytes 1572872 | tf_op jit(solution)/shard_map/ppermute | solution.py:453
  83.9 0.6 collective-permute-start.8
  84.5 1.1 %add_convert_fusion.2.refs_7_ = bf16[256,512]{1,0:T(8,128)(2,1)S(1)} fusion(bf16[256,512]{1,0:T(8,128)(2,1)} %collective-permute-done.13, bf16[256,512]{1,0:T(8,128)(2,1)} %get-tuple-element.41), kind=kLoop, calls=%fused_computation.2 | loop fusion | flops 524288 | bytes 786432 | tf_op jit(solution)/shard_map/convert_element_type | solution.py:269
  85.6 1.7 %shard_map.71 = (bf16[256,512]{1,0:T(8,128)(2,1)S(1)}, f32[8,128]{1,0:T(8,128)S(1)}) custom-call(bf16[256,2048]{1,0:T(8,128)(2,1)S(1)} %copy-done.1, bf16[256,2048]{1,0:T(8,128)(2,1)S(1)} %collective-permute-done.7.refs_0_, bf16[256,2048]{1,0:T(8,128)(2,1)S(1)} %collective-permute-done.9.refs_1_, f32[8,128]{1,0:T(8,128)S(1)} %get-tuple-element.43.refs_2_), custom_call_target="tpu_custom_call" | custom-call | flops 1000 | bytes 1000 | tf_op jit(solution)/shard_map/pallas_call | solution.py:341
  87.3 0.1 collective-permute-start.14
  87.4 0.5 collective-permute-start.17
  87.9 1.5 %collective-permute-start.20 = (bf16[256,512]{1,0:T(8,128)(2,1)S(1)}, bf16[256,512]{1,0:T(8,128)(2,1)S(1)}, u32[]{:S(2)}, u32[]{:S(2)}) collective-permute-start(bf16[256,512]{1,0:T(8,128)(2,1)S(1)} %get-tuple-element.47), channel_id=1, source_target_pairs={{0,2},{1,3},{2,0},{3,1},{4,6},{5,7},{6,4},{7,5},{8,10},{9,11},{10,... | collective-permute-start | bytes 786440 | tf_op jit(solution)/shard_map/ppermute | solution.py:260
  89.5 0.1 collective-permute-done.17.refs_12_.refs_7_
  89.5 5.1 %shard_map.72 = (f32[256,2048]{1,0:T(8,128)S(1)}, f32[256,128]{1,0:T(8,128)S(1)}, f32[8,128]{1,0:T(8,128)S(1)}) custom-call(s32[2,10]{1,0:T(2,128)S(1)} %pad_add_fusion.places, bf16[256,2048]{1,0:T(8,128)(2,1)S(1)} %copy-done.2, bf16[256,2048]{1,0:T(8,128)(2,1)} %get-tuple-element.31.refs_1_, bf16[256,2048]{1,0:T(8,128)(2,1)} %get-tuple-element.32.refs_2_, ...), custom_call_target="tpu_custom_call" | custom-call | flops 1000 | bytes 1000 | tf_op jit(solution)/shard_map/pallas_call | solution.py:370
  94.6 1.9 %collective-permute-done.10.refs_1_ = bf16[128,2048]{1,0:T(8,128)(2,1)S(1)} collective-permute-done((bf16[128,2048]{1,0:T(8,128)(2,1)S(1)}, bf16[128,2048]{1,0:T(8,128)(2,1)S(1)}, u32[]{:S(2)}, u32[]{:S(2)}) %collective-permute-start.10) | collective-permute-done | bytes 524320 | tf_op jit(solution)/shard_map/ppermute | solution.py:453
  96.6 1.0 collective-permute-done.8.refs_0_
  97.6 0.6 shard_map.73
  98.3 0.1 collective-permute-start.18
  98.4 0.6 collective-permute-start.21
  99.0 0.7 collective-permute-done.18
  99.7 1.6 %collective-permute-start.19 = (bf16[256,256]{1,0:T(8,128)(2,1)S(1)}, bf16[256,256]{1,0:T(8,128)(2,1)S(1)}, u32[]{:S(2)}, u32[]{:S(2)}) collective-permute-start(bf16[256,256]{1,0:T(8,128)(2,1)S(1)} %add_convert_fusion.3.refs_2_), channel_id=1, source_target_pairs={{0,2},{1,3},{2,0},{3,1},{4,6},{5,7},{6,4},{7,5},{8,10},{9,11},{10,... | collective-permute-start | bytes 393224 | tf_op jit(solution)/shard_map/ppermute | solution.py:260
  101.4 2.3 %shard_map.74 = (f32[256,2048]{1,0:T(8,128)S(1)}, f32[256,128]{1,0:T(8,128)S(1)}, bf16[256,256]{1,0:T(8,128)(2,1)S(1)}, f32[8,128]{1,0:T(8,128)}) custom-call(s32[2,6]{1,0:T(2,128)S(1)} %pad_add_fusion.1.places, bf16[256,2048]{1,0:T(8,128)(2,1)S(1)} %collective-permute-done.7.refs_0_, bf16[256,2048]{1,0:T(8,128)(2,1)S(1)} %collective-permute-done.9.refs_1_, ...), custom_call_target="tpu_custom_call" | custom-call | flops 1000 | bytes 1000 | tf_op jit(solution)/shard_map/pallas_call | solution.py:370
  103.7 1.6 %collective-permute-done.19.refs_3_ = bf16[256,256]{1,0:T(8,128)(2,1)S(1)} collective-permute-done((bf16[256,256]{1,0:T(8,128)(2,1)S(1)}, bf16[256,256]{1,0:T(8,128)(2,1)S(1)}, u32[]{:S(2)}, u32[]{:S(2)}) %collective-permute-start.19) | collective-permute-done | bytes 131104 | tf_op jit(solution)/shard_map/ppermute | solution.py:260
  105.4 2.6 %shard_map.75 = bf16[512,2048]{1,0:T(8,128)(2,1)} custom-call(bf16[128,2048]{1,0:T(8,128)(2,1)S(1)} %collective-permute-done.8.refs_0_, bf16[128,2048]{1,0:T(8,128)(2,1)S(1)} %collective-permute-done.10.refs_1_, bf16[256,256]{1,0:T(8,128)(2,1)S(1)} %add_convert_fusion.3.refs_2_, bf16[256,256]{1,0:T(8,128)(2,1)S(1)} %collective-permute-done.19.refs_3_, ...), custom_call_target="tpu_custom_call" | custom-call | flops 1000 | bytes 1000 | tf_op jit(solution)/shard_map/pallas_call | solution.py:403
  (45 shorter events, 0.4 us)
Async XLA Ops:
  0.0 35.9 %collective-permute-start = (bf16[256,2048]{1,0:T(8,128)(2,1)}, bf16[256,2048]{1,0:T(8,128)(2,1)}, u32[]{:S(2)}, u32[]{:S(2)}) collective-permute-start(bf16[256,2048]{1,0:T(8,128)(2,1)} %refs_0_.3), channel_id=1, source_target_pairs={{0,4},{4,8},{8,12},{12,28},{28,24},{24,20},{20,16},{16,0},{1,5},{5... | collective-permute-start | bytes 3145736 | tf_op jit(solution)/shard_map/ppermute | solution.py:453
  3.0 32.9 %collective-permute-start.1 = (bf16[256,2048]{1,0:T(8,128)(2,1)}, bf16[256,2048]{1,0:T(8,128)(2,1)}, u32[]{:S(2)}, u32[]{:S(2)}) collective-permute-start(bf16[256,2048]{1,0:T(8,128)(2,1)} %refs_0_.3), channel_id=1, source_target_pairs={{0,16},{4,0},{8,4},{12,8},{28,12},{24,28},{20,24},{16,20},{1,17},{... | collective-permute-start | bytes 3145736 | tf_op jit(solution)/shard_map/ppermute | solution.py:453
  35.9 23.1 %collective-permute-start.2 = (bf16[256,2048]{1,0:T(8,128)(2,1)}, bf16[256,2048]{1,0:T(8,128)(2,1)}, u32[]{:S(2)}, u32[]{:S(2)}) collective-permute-start(bf16[256,2048]{1,0:T(8,128)(2,1)} %get-tuple-element.31.refs_1_), channel_id=1, source_target_pairs={{0,4},{4,8},{8,12},{12,28},{28,24},{24,20},{20,16},{16,0},{1,5},{5... | collective-permute-start | bytes 3145736 | tf_op jit(solution)/shard_map/ppermute | solution.py:453
  36.4 23.2 %collective-permute-start.3 = (bf16[256,2048]{1,0:T(8,128)(2,1)}, bf16[256,2048]{1,0:T(8,128)(2,1)}, u32[]{:S(2)}, u32[]{:S(2)}) collective-permute-start(bf16[256,2048]{1,0:T(8,128)(2,1)} %get-tuple-element.32.refs_2_), channel_id=1, source_target_pairs={{0,16},{4,0},{8,4},{12,8},{28,12},{24,28},{20,24},{16,20},{1,17},{... | collective-permute-start | bytes 3145736 | tf_op jit(solution)/shard_map/ppermute | solution.py:453
  40.5 1.9 %collective-permute-start.4 = (f32[8,512]{1,0:T(8,128)}, f32[8,512]{1,0:T(8,128)S(1)}, u32[]{:S(2)}, u32[]{:S(2)}) collective-permute-start(f32[8,512]{1,0:T(8,128)} %shard_map.66.refs_0_), channel_id=1, source_target_pairs={{0,1},{1,0},{2,3},{3,2},{4,5},{5,4},{6,7},{7,6},{8,9},{9,8},{10,11... | collective-permute-start | bytes 49160 | tf_op jit(solution)/shard_map/ppermute | solution.py:260
  40.6 4.0 %collective-permute-start.5 = (f32[8,512]{1,0:T(8,128)}, f32[8,512]{1,0:T(8,128)S(1)}, u32[]{:S(2)}, u32[]{:S(2)}) collective-permute-start(f32[8,512]{1,0:T(8,128)} %shard_map.66.refs_0_), channel_id=1, source_target_pairs={{0,2},{1,3},{2,0},{3,1},{4,6},{5,7},{6,4},{7,5},{8,10},{9,11},{10,... | collective-permute-start | bytes 49160 | tf_op jit(solution)/shard_map/ppermute | solution.py:260
  42.2 3.4 %collective-permute-start.6 = (f32[8,512]{1,0:T(8,128)}, f32[8,512]{1,0:T(8,128)S(1)}, u32[]{:S(2)}, u32[]{:S(2)}) collective-permute-start(f32[8,512]{1,0:T(8,128)} %shard_map.66.refs_0_), channel_id=1, source_target_pairs={{0,3},{1,2},{2,1},{3,0},{4,7},{5,6},{6,5},{7,4},{8,11},{9,10},{10,... | collective-permute-start | bytes 49160 | tf_op jit(solution)/shard_map/ppermute | solution.py:260
  42.5 3.1 %copy-start.9 = (f32[8,512]{1,0:T(8,128)}, f32[8,512]{1,0:T(8,128)S(1)}, u32[]{:S(2)}) copy-start(f32[8,512]{1,0:T(8,128)S(1)} %collective-permute-done.4.refs_1_) | copy-start | bytes 49156
  44.6 0.9 copy-start.10
  45.6 0.6 copy-start.11
  59.6 22.4 %collective-permute-start.9 = (bf16[256,2048]{1,0:T(8,128)(2,1)}, bf16[256,2048]{1,0:T(8,128)(2,1)S(1)}, u32[]{:S(2)}, u32[]{:S(2)}) collective-permute-start(bf16[256,2048]{1,0:T(8,128)(2,1)} %get-tuple-element.38.refs_1_.refs_4_), channel_id=1, source_target_pairs={{0,16},{4,0},{8,4},{12,8},{28,12},{24,28},{20,24},{16,20},{1,17},{... | collective-permute-start | bytes 3145736 | tf_op jit(solution)/shard_map/ppermute | solution.py:453
  61.2 21.2 %collective-permute-start.7 = (bf16[256,2048]{1,0:T(8,128)(2,1)}, bf16[256,2048]{1,0:T(8,128)(2,1)S(1)}, u32[]{:S(2)}, u32[]{:S(2)}) collective-permute-start(bf16[256,2048]{1,0:T(8,128)(2,1)} %get-tuple-element.37.refs_0_.refs_3_), channel_id=1, source_target_pairs={{0,4},{4,8},{8,12},{12,28},{28,24},{24,20},{20,16},{16,0},{1,5},{5... | collective-permute-start | bytes 3145736 | tf_op jit(solution)/shard_map/ppermute | solution.py:453
  61.6 9.9 %collective-permute-start.11 = (bf16[256,768]{1,0:T(8,128)(2,1)}, bf16[256,768]{1,0:T(8,128)(2,1)S(1)}, u32[]{:S(2)}, u32[]{:S(2)}) collective-permute-start(bf16[256,768]{1,0:T(8,128)(2,1)} %get-tuple-element.39), channel_id=1, source_target_pairs={{0,2},{1,3},{2,0},{3,1},{4,6},{5,7},{6,4},{7,5},{8,10},{9,11},{10,... | collective-permute-start | bytes 1179656 | tf_op jit(solution)/shard_map/ppermute | solution.py:260
  63.1 1.2 %copy-start = (bf16[256,2048]{1,0:T(8,128)(2,1)S(1)}, bf16[256,2048]{1,0:T(8,128)(2,1)}, u32[]{:S(2)}) copy-start(bf16[256,2048]{1,0:T(8,128)(2,1)} %get-tuple-element.35.normed) | copy-start | bytes 3145732
  64.3 0.7 copy-start.8
  65.0 8.4 %copy-start.3 = (bf16[4,256,128]{2,1,0:T(8,128)(2,1)S(1)}, bf16[4,256,128]{2,1,0:T(8,128)(2,1)}, u32[]{:S(2)}) copy-start(bf16[4,256,128]{2,1,0:T(8,128)(2,1)} %get-tuple-element.42.refs_9_.refs_4_) | copy-start | bytes 786436
  68.5 17.2 %copy-start.1 = (bf16[256,2048]{1,0:T(8,128)(2,1)S(1)}, bf16[256,2048]{1,0:T(8,128)(2,1)}, u32[]{:S(2)}) copy-start(bf16[256,2048]{1,0:T(8,128)(2,1)} %get-tuple-element.35.normed) | copy-start | bytes 3145732
  68.5 15.4 %collective-permute-start.13 = (bf16[256,512]{1,0:T(8,128)(2,1)}, bf16[256,512]{1,0:T(8,128)(2,1)}, u32[]{:S(2)}, u32[]{:S(2)}) collective-permute-start(bf16[256,512]{1,0:T(8,128)(2,1)} %get-tuple-element.41), channel_id=1, source_target_pairs={{0,2},{1,3},{2,0},{3,1},{4,6},{5,7},{6,4},{7,5},{8,10},{9,11},{10,... | collective-permute-start | bytes 786440 | tf_op jit(solution)/shard_map/ppermute | solution.py:260
  73.3 14.0 %collective-permute-start.12 = (bf16[256,768]{1,0:T(8,128)(2,1)}, bf16[256,768]{1,0:T(8,128)(2,1)}, u32[]{:S(2)}, u32[]{:S(2)}) collective-permute-start(bf16[256,768]{1,0:T(8,128)(2,1)} %add_convert_fusion.refs_5_), channel_id=1, source_target_pairs={{0,1},{1,0},{2,3},{3,2},{4,5},{5,4},{6,7},{7,6},{8,9},{9,8},{10,11... | collective-permute-start | bytes 1179656 | tf_op jit(solution)/shard_map/ppermute | solution.py:260
  73.3 14.1 %collective-permute-start.16 = (bf16[4,256,128]{2,1,0:T(8,128)(2,1)S(1)}, bf16[4,256,128]{2,1,0:T(8,128)(2,1)}, u32[]{:S(2)}, u32[]{:S(2)}) collective-permute-start(bf16[4,256,128]{2,1,0:T(8,128)(2,1)S(1)} %copy-done.3), channel_id=1, source_target_pairs={{0,2},{1,3},{2,0},{3,1},{4,6},{5,7},{6,4},{7,5},{8,10},{9,11},{10,... | collective-permute-start | bytes 786440 | tf_op jit(solution)/shard_map/ppermute | solution.py:260
  81.9 6.0 %collective-permute-start.15 = (bf16[4,256,128]{2,1,0:T(8,128)(2,1)S(1)}, bf16[4,256,128]{2,1,0:T(8,128)(2,1)}, u32[]{:S(2)}, u32[]{:S(2)}) collective-permute-start(bf16[4,256,128]{2,1,0:T(8,128)(2,1)S(1)} %copy-done.3), channel_id=1, source_target_pairs={{0,1},{1,0},{2,3},{3,2},{4,5},{5,4},{6,7},{7,6},{8,9},{9,8},{10,11... | collective-permute-start | bytes 786440 | tf_op jit(solution)/shard_map/ppermute | solution.py:260
  82.4 14.2 %collective-permute-start.10 = (bf16[128,2048]{1,0:T(8,128)(2,1)S(1)}, bf16[128,2048]{1,0:T(8,128)(2,1)S(1)}, u32[]{:S(2)}, u32[]{:S(2)}) collective-permute-start(bf16[128,2048]{1,0:T(8,128)(2,1)S(1)} %slice.9), channel_id=1, source_target_pairs={{0,16},{4,0},{8,4},{12,8},{28,12},{24,28},{20,24},{16,20},{1,17},{... | collective-permute-start | bytes 1572872 | tf_op jit(solution)/shard_map/ppermute | solution.py:453
  83.9 5.6 %copy-start.2 = (bf16[256,2048]{1,0:T(8,128)(2,1)S(1)}, bf16[256,2048]{1,0:T(8,128)(2,1)}, u32[]{:S(2)}) copy-start(bf16[256,2048]{1,0:T(8,128)(2,1)} %refs_0_.3) | copy-start | bytes 3145732
  83.9 13.7 %collective-permute-start.8 = (bf16[128,2048]{1,0:T(8,128)(2,1)S(1)}, bf16[128,2048]{1,0:T(8,128)(2,1)S(1)}, u32[]{:S(2)}, u32[]{:S(2)}) collective-permute-start(bf16[128,2048]{1,0:T(8,128)(2,1)S(1)} %slice.8), channel_id=1, source_target_pairs={{0,4},{4,8},{8,12},{12,28},{28,24},{24,20},{20,16},{16,0},{1,5},{5... | collective-permute-start | bytes 1572872 | tf_op jit(solution)/shard_map/ppermute | solution.py:453
  87.3 2.1 %collective-permute-start.14 = (bf16[256,512]{1,0:T(8,128)(2,1)S(1)}, bf16[256,512]{1,0:T(8,128)(2,1)S(1)}, u32[]{:S(2)}, u32[]{:S(2)}) collective-permute-start(bf16[256,512]{1,0:T(8,128)(2,1)S(1)} %add_convert_fusion.2.refs_7_), channel_id=1, source_target_pairs={{0,1},{1,0},{2,3},{3,2},{4,5},{5,4},{6,7},{7,6},{8,9},{9,8},{10,11... | collective-permute-start | bytes 786440 | tf_op jit(solution)/shard_map/ppermute | solution.py:260
  87.4 2.1 %collective-permute-start.17 = (bf16[4,256,128]{2,1,0:T(8,128)(2,1)}, bf16[4,256,128]{2,1,0:T(8,128)(2,1)S(1)}, u32[]{:S(2)}, u32[]{:S(2)}) collective-permute-start(bf16[4,256,128]{2,1,0:T(8,128)(2,1)} %collective-permute-done.16.refs_11_.refs_6_), channel_id=1, source_target_pairs={{0,1},{1,0},{2,3},{3,2},{4,5},{5,4},{6,7},{7,6},{8,9},{9,8},{10,11... | collective-permute-start | bytes 786440 | tf_op jit(solution)/shard_map/ppermute | solution.py:260
  87.9 10.4 %collective-permute-start.20 = (bf16[256,512]{1,0:T(8,128)(2,1)S(1)}, bf16[256,512]{1,0:T(8,128)(2,1)S(1)}, u32[]{:S(2)}, u32[]{:S(2)}) collective-permute-start(bf16[256,512]{1,0:T(8,128)(2,1)S(1)} %get-tuple-element.47), channel_id=1, source_target_pairs={{0,2},{1,3},{2,0},{3,1},{4,6},{5,7},{6,4},{7,5},{8,10},{9,11},{10,... | collective-permute-start | bytes 786440 | tf_op jit(solution)/shard_map/ppermute | solution.py:260
  98.3 1.4 %collective-permute-start.18 = (bf16[256,256]{1,0:T(8,128)(2,1)S(1)}, bf16[256,256]{1,0:T(8,128)(2,1)S(1)}, u32[]{:S(2)}, u32[]{:S(2)}) collective-permute-start(bf16[256,256]{1,0:T(8,128)(2,1)S(1)} %get-tuple-element.46), channel_id=1, source_target_pairs={{0,1},{1,0},{2,3},{3,2},{4,5},{5,4},{6,7},{7,6},{8,9},{9,8},{10,11... | collective-permute-start | bytes 393224 | tf_op jit(solution)/shard_map/ppermute | solution.py:260
  98.4 2.9 %collective-permute-start.21 = (bf16[256,512]{1,0:T(8,128)(2,1)S(1)}, bf16[256,512]{1,0:T(8,128)(2,1)S(1)}, u32[]{:S(2)}, u32[]{:S(2)}) collective-permute-start(bf16[256,512]{1,0:T(8,128)(2,1)S(1)} %add_convert_fusion.1.refs_2_), channel_id=1, source_target_pairs={{0,1},{1,0},{2,3},{3,2},{4,5},{5,4},{6,7},{7,6},{8,9},{9,8},{10,11... | collective-permute-start | bytes 786440 | tf_op jit(solution)/shard_map/ppermute | solution.py:260
  99.7 5.6 %collective-permute-start.19 = (bf16[256,256]{1,0:T(8,128)(2,1)S(1)}, bf16[256,256]{1,0:T(8,128)(2,1)S(1)}, u32[]{:S(2)}, u32[]{:S(2)}) collective-permute-start(bf16[256,256]{1,0:T(8,128)(2,1)S(1)} %add_convert_fusion.3.refs_2_), channel_id=1, source_target_pairs={{0,2},{1,3},{2,0},{3,1},{4,6},{5,7},{6,4},{7,5},{8,10},{9,11},{10,... | collective-permute-start | bytes 393224 | tf_op jit(solution)/shard_map/ppermute | solution.py:260
  101.3 4.0 %copy-start.4 = (bf16[256,2048]{1,0:T(8,128)(2,1)S(1)}, bf16[256,2048]{1,0:T(8,128)(2,1)}, u32[]{:S(2)}) copy-start(bf16[256,2048]{1,0:T(8,128)(2,1)} %get-tuple-element.54.refs_7_) | copy-start | bytes 3145732
  101.3 4.0 %copy-start.5 = (bf16[512,256]{1,0:T(8,128)(2,1)S(1)}, bf16[512,256]{1,0:T(8,128)(2,1)}, u32[]{:S(2)}) copy-start(bf16[512,256]{1,0:T(8,128)(2,1)} %get-tuple-element.56.refs_10_) | copy-start | bytes 786436
  101.3 4.0 %copy-start.6 = (f32[256,128]{1,0:T(8,128)S(1)}, f32[256,128]{1,0:T(8,128)}, u32[]{:S(2)}) copy-start(f32[256,128]{1,0:T(8,128)} %get-tuple-element.55.refs_9_) | copy-start | bytes 393220
  101.3 4.0 %copy-start.7 = (f32[2048]{0:T(1024)S(1)}, f32[2048]{0:T(1024)}, u32[]{:S(2)}) copy-start(f32[2048]{0:T(1024)} %param.9) | copy-start | bytes 24580

commit v6 on v5

--- a/solution.py
+++ b/solution.py
@@ -12,6 +12,7 @@
 HOLDERS = ("section", "wide")
 LANES = 128
 COLUMNS = 512
+TAIL_COLUMNS = 1024
 SMALL_COST = pl.CostEstimate(flops=1000, bytes_accessed=1000, transcendentals=0)
 
 
@@ -26,7 +27,7 @@
 
 
 VMEM_BYTES = 63 * 1024 * 1024
-END_VMEM_BYTES = 24 * 1024 * 1024
+END_VMEM_BYTES = 18 * 1024 * 1024
 
 
 def local_kernel(body, out_shape, vmem_bytes=VMEM_BYTES, **kwargs):
@@ -55,8 +56,8 @@
     *values, token = local_kernel(
         lambda *refs: None,
         [jax.ShapeDtypeStruct(v.shape, v.dtype) for v in values] + [TOKEN],
-        in_specs=in_hbm(count + len(after)),
-        out_specs=in_hbm(count + 1),
+        in_specs=anywhere(count + len(after)),
+        out_specs=anywhere(count) + in_hbm(1),
         input_output_aliases={i: i for i in range(count)},
     )(*values, *after)
     return values, token
@@ -240,9 +241,10 @@
     row_scale = scale[:, :1]
     factor = row_scale * row_scale * (jnp.sum(inner, axis=1, keepdims=True) / width)
     copies = []
+    size = buffer.shape[2]
     for i in range(copied.shape[0]):
-        block = slice(i * COLUMNS, (i + 1) * COLUMNS)
-        back, first = back_in[:, block], 0
+        block = slice(i * size, (i + 1) * size)
+        back = back_in[:, block]
         weights = jnp.concatenate([piece[:, block] for piece in pieces], axis=0)
         back += dot(residual[...], weights)
         row_grad[...] = (
@@ -408,9 +410,9 @@
             out_specs=in_hbm(1)[0],
             scratch_shapes=[
                 pltpu.VMEM((slots, features), jnp.bfloat16),
-                pltpu.VMEM((width // COLUMNS, vocab_rows, COLUMNS), jnp.bfloat16),
-                pltpu.VMEM((slots, COLUMNS), jnp.bfloat16),
-                pltpu.SemaphoreType.DMA((width // COLUMNS,)),
+                pltpu.VMEM((width // TAIL_COLUMNS, vocab_rows, TAIL_COLUMNS), jnp.bfloat16),
+                pltpu.VMEM((slots, TAIL_COLUMNS), jnp.bfloat16),
+                pltpu.SemaphoreType.DMA((width // TAIL_COLUMNS,)),
             ],
         )(
             *[piece for _, piece in group],

time: 108 us -> 108 us (level)
  no operation moved by 1% of the time
where the time goes in v6:
time: 108 us
  blocking collectives  30.9 us (29%)
  Pallas kernels  29.1 us (27%)
  waiting for transfers between devices  21.7 us (20%)
  starting transfers between devices  19.8 us (18%)
  other arithmetic  3.07 us (3%)
  local copies, waits for them, and re-layouts  2.81 us (3%)
    all_to_all x1, blocking collectives, ask(): lax.all_to_all(self.sent.reshape(self.owners, self.slot_count, width + LA...  30.9 us
    ppermute x8, waiting for transfers between devices, send(): return lax.ppermute(value, HOLDERS, pairs)  13.8 us
    ppermute x14, starting transfers between devices, exchange_narrow(): lax.ppermute(value, 'narrow', [(i, i ^ distance) for i in range(narrow)])  10.6 us
    pallas_call x4, Pallas kernels, forward(): local_kernel(functools.partial(forward_body, count), (jax.ShapeDtypeStruc...  10.1 us
    ppermute x8, starting transfers between devices, send(): return lax.ppermute(value, HOLDERS, pairs)  9.2 us
    ppermute x14, waiting for transfers between devices, exchange_narrow(): lax.ppermute(value, 'narrow', [(i, i ^ distance) for i in range(narrow)])  7.9 us
    pallas_call x2, Pallas kernels, back(): local_kernel(functools.partial(back_body, count, shared, sizes, narrow, l...  7.42 us
    pallas_call x1, Pallas kernels, pick(): local_kernel(functools.partial(pick_body, self.width_all), (rows, rows, j...  4.7 us
  transfers between devices with their start and end apart: 22, of which 12 were waited for; matrix products, arithmetic and copies ran while one was open for 3% of the time, Pallas kernels for 25%

profile of v6, /device:TPU:0, one launch (start us, length us, event | category | flops | bytes accessed | tf_op | source)
XLA Modules:
  0.0 107.7 jit_solution(14071494915452234988)
XLA Ops:
  0.0 3.0 %collective-permute-start = (bf16[256,2048]{1,0:T(8,128)(2,1)}, bf16[256,2048]{1,0:T(8,128)(2,1)}, u32[]{:S(2)}, u32[]{:S(2)}) collective-permute-start(bf16[256,2048]{1,0:T(8,128)(2,1)} %refs_0_.3), channel_id=1, source_target_pairs={{0,4},{4,8},{8,12},{12,28},{28,24},{24,20},{20,16},{16,0},{1,5},{5... | collective-permute-start | bytes 3145736 | tf_op jit(solution)/shard_map/ppermute | solution.py:455
  3.0 2.0 %shard_map.64._ = bf16[256,640]{1,0:T(8,128)(2,1)} custom-call(s32[1,128]{1,0:T(1,128)} %bitcast.26, s32[1,128]{1,0:T(1,128)} %bitcast.27, bf16[128,512]{1,0:T(8,128)(2,1)} %target.1), custom_call_target="tpu_custom_call" | custom-call | flops 1000 | bytes 1000 | tf_op jit(solution)/shard_map/pallas_call | solution.py:290
  5.0 30.9 %all_to_all.5 = bf16[8,32,640]{2,1,0:T(8,128)(2,1)} all-to-all(bf16[8,32,640]{2,1,0:T(8,128)(2,1)} %bitcast.25), channel_id=1, replica_groups=mesh['section'=2,'wide'=4,'narrow'=4] {'section','wide'}, dimensions={0} | all-to-all | bytes 655360 | tf_op jit(solution)/shard_map/all_to_all | solution.py:294
  35.9 0.4 collective-permute-start.2
  36.4 1.6 %collective-permute-start.3 = (bf16[256,2048]{1,0:T(8,128)(2,1)}, bf16[256,2048]{1,0:T(8,128)(2,1)}, u32[]{:S(2)}, u32[]{:S(2)}) collective-permute-start(bf16[256,2048]{1,0:T(8,128)(2,1)} %get-tuple-element.32.refs_2_), channel_id=1, source_target_pairs={{0,16},{4,0},{8,4},{12,8},{28,12},{24,28},{20,24},{16,20},{1,17},{... | collective-permute-start | bytes 3145736 | tf_op jit(solution)/shard_map/ppermute | solution.py:455
  38.0 2.5 %shard_map.66.refs_0_ = f32[8,512]{1,0:T(8,128)} custom-call(bf16[512,2048]{1,0:T(8,128)(2,1)} %table.3, bf16[256,640]{1,0:T(8,128)(2,1)} %shard_map.64._), custom_call_target="tpu_custom_call" | custom-call | flops 1000 | bytes 1000 | tf_op jit(solution)/shard_map/pallas_call | solution.py:304
  40.6 1.6 %collective-permute-start.5 = (f32[8,512]{1,0:T(8,128)}, f32[8,512]{1,0:T(8,128)S(1)}, u32[]{:S(2)}, u32[]{:S(2)}) collective-permute-start(f32[8,512]{1,0:T(8,128)} %shard_map.66.refs_0_), channel_id=1, source_target_pairs={{0,2},{1,3},{2,0},{3,1},{4,6},{5,7},{6,4},{7,5},{8,10},{9,11},{10,... | collective-permute-start | bytes 49160 | tf_op jit(solution)/shard_map/ppermute | solution.py:262
  42.2 0.3 collective-permute-start.6
  42.5 2.1 %collective-permute-done.5.refs_2_ = f32[8,512]{1,0:T(8,128)S(1)} collective-permute-done((f32[8,512]{1,0:T(8,128)}, f32[8,512]{1,0:T(8,128)S(1)}, u32[]{:S(2)}, u32[]{:S(2)}) %collective-permute-start.5) | collective-permute-done | bytes 16416 | tf_op jit(solution)/shard_map/ppermute | solution.py:262
  44.6 0.9 collective-permute-done.6.refs_3_
  45.6 0.6 copy-done.11
  46.1 4.7 %shard_map.67 = (bf16[256,2048]{1,0:T(8,128)(2,1)}, bf16[256,2048]{1,0:T(8,128)(2,1)}, f32[256,128]{1,0:T(8,128)}, bf16[4,256,128]{2,1,0:T(8,128)(2,1)}, bf16[512,256]{1,0:T(8,128)(2,1)}) custom-call(bf16[256,640]{1,0:T(8,128)(2,1)} %bitcast.24, bf16[512,2048]{1,0:T(8,128)(2,1)} %table.3, f32[1,2048]{1,0:T(1,128)} %bitcast.21, f32[8,512]{1,0:T(8,128)} %shard_map.66.refs_0_, ...), custom_call_target="tpu_custom_call" | custom-call | flops 1000 | bytes 1000 | tf_op jit(solution)/shard_map/pallas_call | solution.py:318
  50.9 4.3 %shard_map.68 = (bf16[256,768]{1,0:T(8,128)(2,1)}, f32[8,128]{1,0:T(8,128)}) custom-call(bf16[256,2048]{1,0:T(8,128)(2,1)} %get-tuple-element.35.normed, bf16[256,2048]{1,0:T(8,128)(2,1)} %refs_0_.3, bf16[256,2048]{1,0:T(8,128)(2,1)} %get-tuple-element.31.refs_1_, bf16[256,2048]{1,0:T(8,128)(2,1)} %get-tuple-element.32.refs_2_, ...), custom_call_target="tpu_custom_call" | custom-call | flops 1000 | bytes 1000 | tf_op jit(solution)/shard_map/pallas_call | solution.py:343
  55.1 3.9 %collective-permute-done.2.refs_0_ = bf16[256,2048]{1,0:T(8,128)(2,1)} collective-permute-done((bf16[256,2048]{1,0:T(8,128)(2,1)}, bf16[256,2048]{1,0:T(8,128)(2,1)}, u32[]{:S(2)}, u32[]{:S(2)}) %collective-permute-start.2) | collective-permute-done | bytes 1048608 | tf_op jit(solution)/shard_map/ppermute | solution.py:455
  59.0 0.5 collective-permute-done.3.refs_1_
  59.6 1.6 %collective-permute-start.9 = (bf16[256,2048]{1,0:T(8,128)(2,1)}, bf16[256,2048]{1,0:T(8,128)(2,1)S(1)}, u32[]{:S(2)}, u32[]{:S(2)}) collective-permute-start(bf16[256,2048]{1,0:T(8,128)(2,1)} %get-tuple-element.38.refs_1_.refs_4_), channel_id=1, source_target_pairs={{0,16},{4,0},{8,4},{12,8},{28,12},{24,28},{20,24},{16,20},{1,17},{... | collective-permute-start | bytes 3145736 | tf_op jit(solution)/shard_map/ppermute | solution.py:455
  61.2 0.4 collective-permute-start.7
  61.6 1.5 %collective-permute-start.11 = (bf16[256,768]{1,0:T(8,128)(2,1)}, bf16[256,768]{1,0:T(8,128)(2,1)S(1)}, u32[]{:S(2)}, u32[]{:S(2)}) collective-permute-start(bf16[256,768]{1,0:T(8,128)(2,1)} %get-tuple-element.39), channel_id=1, source_target_pairs={{0,2},{1,3},{2,0},{3,1},{4,6},{5,7},{6,4},{7,5},{8,10},{9,11},{10,... | collective-permute-start | bytes 1179656 | tf_op jit(solution)/shard_map/ppermute | solution.py:262
  63.1 1.2 %copy-done = bf16[256,2048]{1,0:T(8,128)(2,1)S(1)} copy-done((bf16[256,2048]{1,0:T(8,128)(2,1)S(1)}, bf16[256,2048]{1,0:T(8,128)(2,1)}, u32[]{:S(2)}) %copy-start) | copy-done | bytes 1048600
  64.3 0.7 copy-done.8
  65.0 3.5 %shard_map.70 = (bf16[256,512]{1,0:T(8,128)(2,1)}, f32[8,128]{1,0:T(8,128)S(1)}) custom-call(bf16[256,2048]{1,0:T(8,128)(2,1)S(1)} %copy-done, bf16[256,2048]{1,0:T(8,128)(2,1)} %get-tuple-element.37.refs_0_.refs_3_, bf16[256,2048]{1,0:T(8,128)(2,1)} %get-tuple-element.38.refs_1_.refs_4_, f32[8,128]{1,0:T(8,128)S(1)} %copy-done.8), custom_call_target="tpu_custom_call" | custom-call | flops 1000 | bytes 1000 | tf_op jit(solution)/shard_map/pallas_call | solution.py:343
  68.5 0.6 collective-permute-start.13
  69.1 2.4 %collective-permute-done.11 = bf16[256,768]{1,0:T(8,128)(2,1)S(1)} collective-permute-done((bf16[256,768]{1,0:T(8,128)(2,1)}, bf16[256,768]{1,0:T(8,128)(2,1)S(1)}, u32[]{:S(2)}, u32[]{:S(2)}) %collective-permute-start.11) | collective-permute-done | bytes 393248 | tf_op jit(solution)/shard_map/ppermute | solution.py:262
  71.5 1.8 %add_convert_fusion.refs_5_ = bf16[256,768]{1,0:T(8,128)(2,1)} fusion(bf16[256,768]{1,0:T(8,128)(2,1)S(1)} %collective-permute-done.11, bf16[256,768]{1,0:T(8,128)(2,1)} %get-tuple-element.39), kind=kLoop, calls=%fused_computation | loop fusion | flops 786432 | bytes 1179648 | tf_op jit(solution)/shard_map/convert_element_type | solution.py:271
  73.3 2.4 %collective-permute-start.16 = (bf16[4,256,128]{2,1,0:T(8,128)(2,1)S(1)}, bf16[4,256,128]{2,1,0:T(8,128)(2,1)}, u32[]{:S(2)}, u32[]{:S(2)}) collective-permute-start(bf16[4,256,128]{2,1,0:T(8,128)(2,1)S(1)} %copy-done.3), channel_id=1, source_target_pairs={{0,2},{1,3},{2,0},{3,1},{4,6},{5,7},{6,4},{7,5},{8,10},{9,11},{10,... | collective-permute-start | bytes 786440 | tf_op jit(solution)/shard_map/ppermute | solution.py:262
  75.7 6.2 %collective-permute-done.9.refs_1_ = bf16[256,2048]{1,0:T(8,128)(2,1)S(1)} collective-permute-done((bf16[256,2048]{1,0:T(8,128)(2,1)}, bf16[256,2048]{1,0:T(8,128)(2,1)S(1)}, u32[]{:S(2)}, u32[]{:S(2)}) %collective-permute-start.9) | collective-permute-done | bytes 1048608 | tf_op jit(solution)/shard_map/ppermute | solution.py:455
  81.9 0.1 stack.82
  82.0 0.1 stack.74
  82.2 0.2 collective-permute-done.7.refs_0_
  82.4 1.5 %collective-permute-start.10 = (bf16[128,2048]{1,0:T(8,128)(2,1)S(1)}, bf16[128,2048]{1,0:T(8,128)(2,1)S(1)}, u32[]{:S(2)}, u32[]{:S(2)}) collective-permute-start(bf16[128,2048]{1,0:T(8,128)(2,1)S(1)} %slice.9), channel_id=1, source_target_pairs={{0,16},{4,0},{8,4},{12,8},{28,12},{24,28},{20,24},{16,20},{1,17},{... | collective-permute-start | bytes 1572872 | tf_op jit(solution)/shard_map/ppermute | solution.py:455
  83.9 0.6 collective-permute-start.8
  84.5 1.1 %add_convert_fusion.2.refs_7_ = bf16[256,512]{1,0:T(8,128)(2,1)S(1)} fusion(bf16[256,512]{1,0:T(8,128)(2,1)} %collective-permute-done.13, bf16[256,512]{1,0:T(8,128)(2,1)} %get-tuple-element.41), kind=kLoop, calls=%fused_computation.2 | loop fusion | flops 524288 | bytes 786432 | tf_op jit(solution)/shard_map/convert_element_type | solution.py:271
  85.6 1.7 %shard_map.71 = (bf16[256,512]{1,0:T(8,128)(2,1)S(1)}, f32[8,128]{1,0:T(8,128)S(1)}) custom-call(bf16[256,2048]{1,0:T(8,128)(2,1)S(1)} %copy-done.1, bf16[256,2048]{1,0:T(8,128)(2,1)S(1)} %collective-permute-done.7.refs_0_, bf16[256,2048]{1,0:T(8,128)(2,1)S(1)} %collective-permute-done.9.refs_1_, f32[8,128]{1,0:T(8,128)S(1)} %get-tuple-element.43.refs_2_), custom_call_target="tpu_custom_call" | custom-call | flops 1000 | bytes 1000 | tf_op jit(solution)/shard_map/pallas_call | solution.py:343
  87.3 0.1 collective-permute-start.14
  87.4 0.5 collective-permute-start.17
  87.9 1.5 %collective-permute-start.20 = (bf16[256,512]{1,0:T(8,128)(2,1)S(1)}, bf16[256,512]{1,0:T(8,128)(2,1)S(1)}, u32[]{:S(2)}, u32[]{:S(2)}) collective-permute-start(bf16[256,512]{1,0:T(8,128)(2,1)S(1)} %get-tuple-element.47), channel_id=1, source_target_pairs={{0,2},{1,3},{2,0},{3,1},{4,6},{5,7},{6,4},{7,5},{8,10},{9,11},{10,... | collective-permute-start | bytes 786440 | tf_op jit(solution)/shard_map/ppermute | solution.py:262
  89.5 0.1 collective-permute-done.17.refs_12_.refs_7_
  89.5 5.1 %shard_map.72 = (f32[256,2048]{1,0:T(8,128)S(1)}, f32[256,128]{1,0:T(8,128)S(1)}, f32[8,128]{1,0:T(8,128)S(1)}) custom-call(s32[2,10]{1,0:T(2,128)S(1)} %pad_add_fusion.places, bf16[256,2048]{1,0:T(8,128)(2,1)S(1)} %copy-done.2, bf16[256,2048]{1,0:T(8,128)(2,1)} %get-tuple-element.31.refs_1_, bf16[256,2048]{1,0:T(8,128)(2,1)} %get-tuple-element.32.refs_2_, ...), custom_call_target="tpu_custom_call" | custom-call | flops 1000 | bytes 1000 | tf_op jit(solution)/shard_map/pallas_call | solution.py:372
  94.6 1.9 %collective-permute-done.10.refs_1_ = bf16[128,2048]{1,0:T(8,128)(2,1)S(1)} collective-permute-done((bf16[128,2048]{1,0:T(8,128)(2,1)S(1)}, bf16[128,2048]{1,0:T(8,128)(2,1)S(1)}, u32[]{:S(2)}, u32[]{:S(2)}) %collective-permute-start.10) | collective-permute-done | bytes 524320 | tf_op jit(solution)/shard_map/ppermute | solution.py:455
  96.6 1.0 collective-permute-done.8.refs_0_
  97.6 0.6 shard_map.73
  98.3 0.1 collective-permute-start.18
  98.4 0.6 collective-permute-start.21
  99.0 0.7 collective-permute-done.18
  99.7 1.6 %collective-permute-start.19 = (bf16[256,256]{1,0:T(8,128)(2,1)S(1)}, bf16[256,256]{1,0:T(8,128)(2,1)S(1)}, u32[]{:S(2)}, u32[]{:S(2)}) collective-permute-start(bf16[256,256]{1,0:T(8,128)(2,1)S(1)} %add_convert_fusion.3.refs_2_), channel_id=1, source_target_pairs={{0,2},{1,3},{2,0},{3,1},{4,6},{5,7},{6,4},{7,5},{8,10},{9,11},{10,... | collective-permute-start | bytes 393224 | tf_op jit(solution)/shard_map/ppermute | solution.py:262
  101.4 2.3 %shard_map.74 = (f32[256,2048]{1,0:T(8,128)S(1)}, f32[256,128]{1,0:T(8,128)S(1)}, bf16[256,256]{1,0:T(8,128)(2,1)S(1)}, f32[8,128]{1,0:T(8,128)}) custom-call(s32[2,6]{1,0:T(2,128)S(1)} %pad_add_fusion.1.places, bf16[256,2048]{1,0:T(8,128)(2,1)S(1)} %collective-permute-done.7.refs_0_, bf16[256,2048]{1,0:T(8,128)(2,1)S(1)} %collective-permute-done.9.refs_1_, ...), custom_call_target="tpu_custom_call" | custom-call | flops 1000 | bytes 1000 | tf_op jit(solution)/shard_map/pallas_call | solution.py:372
  103.7 1.6 %collective-permute-done.19.refs_3_ = bf16[256,256]{1,0:T(8,128)(2,1)S(1)} collective-permute-done((bf16[256,256]{1,0:T(8,128)(2,1)S(1)}, bf16[256,256]{1,0:T(8,128)(2,1)S(1)}, u32[]{:S(2)}, u32[]{:S(2)}) %collective-permute-start.19) | collective-permute-done | bytes 131104 | tf_op jit(solution)/shard_map/ppermute | solution.py:262
  105.4 2.4 %shard_map.75 = bf16[512,2048]{1,0:T(8,128)(2,1)} custom-call(bf16[128,2048]{1,0:T(8,128)(2,1)S(1)} %collective-permute-done.8.refs_0_, bf16[128,2048]{1,0:T(8,128)(2,1)S(1)} %collective-permute-done.10.refs_1_, bf16[256,256]{1,0:T(8,128)(2,1)S(1)} %add_convert_fusion.3.refs_2_, bf16[256,256]{1,0:T(8,128)(2,1)S(1)} %collective-permute-done.19.refs_3_, ...), custom_call_target="tpu_custom_call" | custom-call | flops 1000 | bytes 1000 | tf_op jit(solution)/shard_map/pallas_call | solution.py:405
  (45 shorter events, 0.4 us)
Async XLA Ops:
  0.0 35.9 %collective-permute-start = (bf16[256,2048]{1,0:T(8,128)(2,1)}, bf16[256,2048]{1,0:T(8,128)(2,1)}, u32[]{:S(2)}, u32[]{:S(2)}) collective-permute-start(bf16[256,2048]{1,0:T(8,128)(2,1)} %refs_0_.3), channel_id=1, source_target_pairs={{0,4},{4,8},{8,12},{12,28},{28,24},{24,20},{20,16},{16,0},{1,5},{5... | collective-permute-start | bytes 3145736 | tf_op jit(solution)/shard_map/ppermute | solution.py:455
  3.0 32.9 %collective-permute-start.1 = (bf16[256,2048]{1,0:T(8,128)(2,1)}, bf16[256,2048]{1,0:T(8,128)(2,1)}, u32[]{:S(2)}, u32[]{:S(2)}) collective-permute-start(bf16[256,2048]{1,0:T(8,128)(2,1)} %refs_0_.3), channel_id=1, source_target_pairs={{0,16},{4,0},{8,4},{12,8},{28,12},{24,28},{20,24},{16,20},{1,17},{... | collective-permute-start | bytes 3145736 | tf_op jit(solution)/shard_map/ppermute | solution.py:455
  35.9 23.1 %collective-permute-start.2 = (bf16[256,2048]{1,0:T(8,128)(2,1)}, bf16[256,2048]{1,0:T(8,128)(2,1)}, u32[]{:S(2)}, u32[]{:S(2)}) collective-permute-start(bf16[256,2048]{1,0:T(8,128)(2,1)} %get-tuple-element.31.refs_1_), channel_id=1, source_target_pairs={{0,4},{4,8},{8,12},{12,28},{28,24},{24,20},{20,16},{16,0},{1,5},{5... | collective-permute-start | bytes 3145736 | tf_op jit(solution)/shard_map/ppermute | solution.py:455
  36.4 23.2 %collective-permute-start.3 = (bf16[256,2048]{1,0:T(8,128)(2,1)}, bf16[256,2048]{1,0:T(8,128)(2,1)}, u32[]{:S(2)}, u32[]{:S(2)}) collective-permute-start(bf16[256,2048]{1,0:T(8,128)(2,1)} %get-tuple-element.32.refs_2_), channel_id=1, source_target_pairs={{0,16},{4,0},{8,4},{12,8},{28,12},{24,28},{20,24},{16,20},{1,17},{... | collective-permute-start | bytes 3145736 | tf_op jit(solution)/shard_map/ppermute | solution.py:455
  40.5 1.9 %collective-permute-start.4 = (f32[8,512]{1,0:T(8,128)}, f32[8,512]{1,0:T(8,128)S(1)}, u32[]{:S(2)}, u32[]{:S(2)}) collective-permute-start(f32[8,512]{1,0:T(8,128)} %shard_map.66.refs_0_), channel_id=1, source_target_pairs={{0,1},{1,0},{2,3},{3,2},{4,5},{5,4},{6,7},{7,6},{8,9},{9,8},{10,11... | collective-permute-start | bytes 49160 | tf_op jit(solution)/shard_map/ppermute | solution.py:262
  40.6 4.0 %collective-permute-start.5 = (f32[8,512]{1,0:T(8,128)}, f32[8,512]{1,0:T(8,128)S(1)}, u32[]{:S(2)}, u32[]{:S(2)}) collective-permute-start(f32[8,512]{1,0:T(8,128)} %shard_map.66.refs_0_), channel_id=1, source_target_pairs={{0,2},{1,3},{2,0},{3,1},{4,6},{5,7},{6,4},{7,5},{8,10},{9,11},{10,... | collective-permute-start | bytes 49160 | tf_op jit(solution)/shard_map/ppermute | solution.py:262
  42.2 3.4 %collective-permute-start.6 = (f32[8,512]{1,0:T(8,128)}, f32[8,512]{1,0:T(8,128)S(1)}, u32[]{:S(2)}, u32[]{:S(2)}) collective-permute-start(f32[8,512]{1,0:T(8,128)} %shard_map.66.refs_0_), channel_id=1, source_target_pairs={{0,3},{1,2},{2,1},{3,0},{4,7},{5,6},{6,5},{7,4},{8,11},{9,10},{10,... | collective-permute-start | bytes 49160 | tf_op jit(solution)/shard_map/ppermute | solution.py:262
  42.5 3.1 %copy-start.9 = (f32[8,512]{1,0:T(8,128)}, f32[8,512]{1,0:T(8,128)S(1)}, u32[]{:S(2)}) copy-start(f32[8,512]{1,0:T(8,128)S(1)} %collective-permute-done.4.refs_1_) | copy-start | bytes 49156
  44.6 0.9 copy-start.10
  45.6 0.6 copy-start.11
  59.6 22.4 %collective-permute-start.9 = (bf16[256,2048]{1,0:T(8,128)(2,1)}, bf16[256,2048]{1,0:T(8,128)(2,1)S(1)}, u32[]{:S(2)}, u32[]{:S(2)}) collective-permute-start(bf16[256,2048]{1,0:T(8,128)(2,1)} %get-tuple-element.38.refs_1_.refs_4_), channel_id=1, source_target_pairs={{0,16},{4,0},{8,4},{12,8},{28,12},{24,28},{20,24},{16,20},{1,17},{... | collective-permute-start | bytes 3145736 | tf_op jit(solution)/shard_map/ppermute | solution.py:455
  61.2 21.2 %collective-permute-start.7 = (bf16[256,2048]{1,0:T(8,128)(2,1)}, bf16[256,2048]{1,0:T(8,128)(2,1)S(1)}, u32[]{:S(2)}, u32[]{:S(2)}) collective-permute-start(bf16[256,2048]{1,0:T(8,128)(2,1)} %get-tuple-element.37.refs_0_.refs_3_), channel_id=1, source_target_pairs={{0,4},{4,8},{8,12},{12,28},{28,24},{24,20},{20,16},{16,0},{1,5},{5... | collective-permute-start | bytes 3145736 | tf_op jit(solution)/shard_map/ppermute | solution.py:455
  61.6 9.9 %collective-permute-start.11 = (bf16[256,768]{1,0:T(8,128)(2,1)}, bf16[256,768]{1,0:T(8,128)(2,1)S(1)}, u32[]{:S(2)}, u32[]{:S(2)}) collective-permute-start(bf16[256,768]{1,0:T(8,128)(2,1)} %get-tuple-element.39), channel_id=1, source_target_pairs={{0,2},{1,3},{2,0},{3,1},{4,6},{5,7},{6,4},{7,5},{8,10},{9,11},{10,... | collective-permute-start | bytes 1179656 | tf_op jit(solution)/shard_map/ppermute | solution.py:262
  63.1 1.2 %copy-start = (bf16[256,2048]{1,0:T(8,128)(2,1)S(1)}, bf16[256,2048]{1,0:T(8,128)(2,1)}, u32[]{:S(2)}) copy-start(bf16[256,2048]{1,0:T(8,128)(2,1)} %get-tuple-element.35.normed) | copy-start | bytes 3145732
  64.3 0.7 copy-start.8
  65.0 8.4 %copy-start.3 = (bf16[4,256,128]{2,1,0:T(8,128)(2,1)S(1)}, bf16[4,256,128]{2,1,0:T(8,128)(2,1)}, u32[]{:S(2)}) copy-start(bf16[4,256,128]{2,1,0:T(8,128)(2,1)} %get-tuple-element.42.refs_9_.refs_4_) | copy-start | bytes 786436
  68.5 17.2 %copy-start.1 = (bf16[256,2048]{1,0:T(8,128)(2,1)S(1)}, bf16[256,2048]{1,0:T(8,128)(2,1)}, u32[]{:S(2)}) copy-start(bf16[256,2048]{1,0:T(8,128)(2,1)} %get-tuple-element.35.normed) | copy-start | bytes 3145732
  68.5 15.4 %collective-permute-start.13 = (bf16[256,512]{1,0:T(8,128)(2,1)}, bf16[256,512]{1,0:T(8,128)(2,1)}, u32[]{:S(2)}, u32[]{:S(2)}) collective-permute-start(bf16[256,512]{1,0:T(8,128)(2,1)} %get-tuple-element.41), channel_id=1, source_target_pairs={{0,2},{1,3},{2,0},{3,1},{4,6},{5,7},{6,4},{7,5},{8,10},{9,11},{10,... | collective-permute-start | bytes 786440 | tf_op jit(solution)/shard_map/ppermute | solution.py:262
  73.3 14.0 %collective-permute-start.12 = (bf16[256,768]{1,0:T(8,128)(2,1)}, bf16[256,768]{1,0:T(8,128)(2,1)}, u32[]{:S(2)}, u32[]{:S(2)}) collective-permute-start(bf16[256,768]{1,0:T(8,128)(2,1)} %add_convert_fusion.refs_5_), channel_id=1, source_target_pairs={{0,1},{1,0},{2,3},{3,2},{4,5},{5,4},{6,7},{7,6},{8,9},{9,8},{10,11... | collective-permute-start | bytes 1179656 | tf_op jit(solution)/shard_map/ppermute | solution.py:262
  73.3 14.1 %collective-permute-start.16 = (bf16[4,256,128]{2,1,0:T(8,128)(2,1)S(1)}, bf16[4,256,128]{2,1,0:T(8,128)(2,1)}, u32[]{:S(2)}, u32[]{:S(2)}) collective-permute-start(bf16[4,256,128]{2,1,0:T(8,128)(2,1)S(1)} %copy-done.3), channel_id=1, source_target_pairs={{0,2},{1,3},{2,0},{3,1},{4,6},{5,7},{6,4},{7,5},{8,10},{9,11},{10,... | collective-permute-start | bytes 786440 | tf_op jit(solution)/shard_map/ppermute | solution.py:262
  81.9 6.0 %collective-permute-start.15 = (bf16[4,256,128]{2,1,0:T(8,128)(2,1)S(1)}, bf16[4,256,128]{2,1,0:T(8,128)(2,1)}, u32[]{:S(2)}, u32[]{:S(2)}) collective-permute-start(bf16[4,256,128]{2,1,0:T(8,128)(2,1)S(1)} %copy-done.3), channel_id=1, source_target_pairs={{0,1},{1,0},{2,3},{3,2},{4,5},{5,4},{6,7},{7,6},{8,9},{9,8},{10,11... | collective-permute-start | bytes 786440 | tf_op jit(solution)/shard_map/ppermute | solution.py:262
  82.4 14.2 %collective-permute-start.10 = (bf16[128,2048]{1,0:T(8,128)(2,1)S(1)}, bf16[128,2048]{1,0:T(8,128)(2,1)S(1)}, u32[]{:S(2)}, u32[]{:S(2)}) collective-permute-start(bf16[128,2048]{1,0:T(8,128)(2,1)S(1)} %slice.9), channel_id=1, source_target_pairs={{0,16},{4,0},{8,4},{12,8},{28,12},{24,28},{20,24},{16,20},{1,17},{... | collective-permute-start | bytes 1572872 | tf_op jit(solution)/shard_map/ppermute | solution.py:455
  83.9 5.6 %copy-start.2 = (bf16[256,2048]{1,0:T(8,128)(2,1)S(1)}, bf16[256,2048]{1,0:T(8,128)(2,1)}, u32[]{:S(2)}) copy-start(bf16[256,2048]{1,0:T(8,128)(2,1)} %refs_0_.3) | copy-start | bytes 3145732
  83.9 13.7 %collective-permute-start.8 = (bf16[128,2048]{1,0:T(8,128)(2,1)S(1)}, bf16[128,2048]{1,0:T(8,128)(2,1)S(1)}, u32[]{:S(2)}, u32[]{:S(2)}) collective-permute-start(bf16[128,2048]{1,0:T(8,128)(2,1)S(1)} %slice.8), channel_id=1, source_target_pairs={{0,4},{4,8},{8,12},{12,28},{28,24},{24,20},{20,16},{16,0},{1,5},{5... | collective-permute-start | bytes 1572872 | tf_op jit(solution)/shard_map/ppermute | solution.py:455
  87.3 2.1 %collective-permute-start.14 = (bf16[256,512]{1,0:T(8,128)(2,1)S(1)}, bf16[256,512]{1,0:T(8,128)(2,1)S(1)}, u32[]{:S(2)}, u32[]{:S(2)}) collective-permute-start(bf16[256,512]{1,0:T(8,128)(2,1)S(1)} %add_convert_fusion.2.refs_7_), channel_id=1, source_target_pairs={{0,1},{1,0},{2,3},{3,2},{4,5},{5,4},{6,7},{7,6},{8,9},{9,8},{10,11... | collective-permute-start | bytes 786440 | tf_op jit(solution)/shard_map/ppermute | solution.py:262
  87.4 2.1 %collective-permute-start.17 = (bf16[4,256,128]{2,1,0:T(8,128)(2,1)}, bf16[4,256,128]{2,1,0:T(8,128)(2,1)S(1)}, u32[]{:S(2)}, u32[]{:S(2)}) collective-permute-start(bf16[4,256,128]{2,1,0:T(8,128)(2,1)} %collective-permute-done.16.refs_11_.refs_6_), channel_id=1, source_target_pairs={{0,1},{1,0},{2,3},{3,2},{4,5},{5,4},{6,7},{7,6},{8,9},{9,8},{10,11... | collective-permute-start | bytes 786440 | tf_op jit(solution)/shard_map/ppermute | solution.py:262
  87.9 10.4 %collective-permute-start.20 = (bf16[256,512]{1,0:T(8,128)(2,1)S(1)}, bf16[256,512]{1,0:T(8,128)(2,1)S(1)}, u32[]{:S(2)}, u32[]{:S(2)}) collective-permute-start(bf16[256,512]{1,0:T(8,128)(2,1)S(1)} %get-tuple-element.47), channel_id=1, source_target_pairs={{0,2},{1,3},{2,0},{3,1},{4,6},{5,7},{6,4},{7,5},{8,10},{9,11},{10,... | collective-permute-start | bytes 786440 | tf_op jit(solution)/shard_map/ppermute | solution.py:262
  98.3 1.4 %collective-permute-start.18 = (bf16[256,256]{1,0:T(8,128)(2,1)S(1)}, bf16[256,256]{1,0:T(8,128)(2,1)S(1)}, u32[]{:S(2)}, u32[]{:S(2)}) collective-permute-start(bf16[256,256]{1,0:T(8,128)(2,1)S(1)} %get-tuple-element.46), channel_id=1, source_target_pairs={{0,1},{1,0},{2,3},{3,2},{4,5},{5,4},{6,7},{7,6},{8,9},{9,8},{10,11... | collective-permute-start | bytes 393224 | tf_op jit(solution)/shard_map/ppermute | solution.py:262
  98.4 2.9 %collective-permute-start.21 = (bf16[256,512]{1,0:T(8,128)(2,1)S(1)}, bf16[256,512]{1,0:T(8,128)(2,1)S(1)}, u32[]{:S(2)}, u32[]{:S(2)}) collective-permute-start(bf16[256,512]{1,0:T(8,128)(2,1)S(1)} %add_convert_fusion.1.refs_2_), channel_id=1, source_target_pairs={{0,1},{1,0},{2,3},{3,2},{4,5},{5,4},{6,7},{7,6},{8,9},{9,8},{10,11... | collective-permute-start | bytes 786440 | tf_op jit(solution)/shard_map/ppermute | solution.py:262
  99.7 5.6 %collective-permute-start.19 = (bf16[256,256]{1,0:T(8,128)(2,1)S(1)}, bf16[256,256]{1,0:T(8,128)(2,1)S(1)}, u32[]{:S(2)}, u32[]{:S(2)}) collective-permute-start(bf16[256,256]{1,0:T(8,128)(2,1)S(1)} %add_convert_fusion.3.refs_2_), channel_id=1, source_target_pairs={{0,2},{1,3},{2,0},{3,1},{4,6},{5,7},{6,4},{7,5},{8,10},{9,11},{10,... | collective-permute-start | bytes 393224 | tf_op jit(solution)/shard_map/ppermute | solution.py:262
  101.3 4.0 %copy-start.4 = (bf16[256,2048]{1,0:T(8,128)(2,1)S(1)}, bf16[256,2048]{1,0:T(8,128)(2,1)}, u32[]{:S(2)}) copy-start(bf16[256,2048]{1,0:T(8,128)(2,1)} %get-tuple-element.54.refs_7_) | copy-start | bytes 3145732
  101.3 4.0 %copy-start.5 = (bf16[512,256]{1,0:T(8,128)(2,1)S(1)}, bf16[512,256]{1,0:T(8,128)(2,1)}, u32[]{:S(2)}) copy-start(bf16[512,256]{1,0:T(8,128)(2,1)} %get-tuple-element.56.refs_10_) | copy-start | bytes 786436
  101.3 4.0 %copy-start.6 = (f32[256,128]{1,0:T(8,128)S(1)}, f32[256,128]{1,0:T(8,128)}, u32[]{:S(2)}) copy-start(f32[256,128]{1,0:T(8,128)} %get-tuple-element.55.refs_9_) | copy-start | bytes 393220
  101.3 4.0 %copy-start.7 = (f32[2048]{0:T(1024)S(1)}, f32[2048]{0:T(1024)}, u32[]{:S(2)}) copy-start(f32[2048]{0:T(1024)} %param.9) | copy-start | bytes 24580
